TPU v7x, 512 devices: a whole 4x8x8 slice. The times are simulated.
512 devices in a mesh: loop: 128 (over y, x, z_hi), narrow: 4 (over z_lo, core).
Axes of the slice: x: 4, y: 8, z: 8 (z_hi: 4, z_lo: 2; z = z_hi * 2 + z_lo), core: 2. Of those that a mesh axis runs over, the one named last changes fastest.
Arguments:
- picture_vectors: bfloat16 [114688, 1152], P(('loop', 'narrow')), may hold values from -0.1796875 to 0.1796875
- caption_vectors: bfloat16 [114688, 1152], P(('loop', 'narrow')), may hold values from -0.1796875 to 0.1796875
- caption_position: int32 [128, 896], P('loop'), may hold values from 0 to 895, each once within a row
- sharpness_factor: float32 [1], replicated, may hold values from 4 to 12
- affine_offset: float32 [1], replicated, may hold values from -3 to -1
Outputs:
- image_grad: float32 [114688, 1152], P(('loop', 'narrow'))
- text_grad: float32 [114688, 1152], P(('loop', 'narrow'))
Inputs may be any that keep to these rules, and one draw needn't show every extreme that they name: Each row of caption_position is a permutation of 0 to 895.
All inputs are finite; a program needn't handle non-finite values.
Results may differ from a plain program's by a relative error of at most 0.014.
Values may be sent and summed in bfloat16 or wider, within the bound.
No kernel may reach another device: no remote copies, remote signals or barrier semaphores. Data moves between devices by JAX's collectives and lax.ppermute only.
A program may use at most 64 MiB of HBM per device.

v0:
```python
import jax
import jax.numpy as jnp
from jax import lax
from jax.sharding import PartitionSpec as P


def passed_along(x, axis, by):
    peers = lax.axis_size(axis)
    return lax.ppermute(x, axis, [(i, (i + by) % peers) for i in range(peers)])


def unit_rows(rows):
    values = rows.astype(jnp.float32)
    inv = lax.rsqrt(jnp.sum(values * values, axis=-1, keepdims=True) + 1e-06)
    return (values * inv, inv)


def row_terms(weights, img_b):
    return lax.dot_general(
        weights, img_b, (((0,), (0,)), ((), ())), preferred_element_type=jnp.float32
    )


def local(picture_vectors, caption_vectors, caption_position, sharpness_factor, affine_offset):
    score_multiplier = sharpness_factor[0]
    shift_b = affine_offset[0]
    rows_here = picture_vectors.shape[0]
    img_unit, img_inv = unit_rows(picture_vectors)
    txt_unit, text_inverse_norm = unit_rows(caption_vectors)
    img_b = img_unit.astype(jnp.bfloat16)
    txt_b = txt_unit.astype(jnp.bfloat16)
    own_texts = lax.all_gather(txt_b, "narrow", axis=0, tiled=True)
    vis_texts = passed_along(own_texts, "loop", 1)
    group_rows = own_texts.shape[0]
    start = lax.axis_index("narrow") * rows_here
    pairs_all = caption_position[0]
    pairs = lax.dynamic_slice_in_dim(pairs_all, start, rows_here)
    column_count = lax.broadcasted_iota(jnp.int32, (rows_here, group_rows), 1)
    positive = (column_count == pairs[:, None]).astype(jnp.float32)
    matched_logit = (
        score_multiplier * jnp.dot(img_b, own_texts.T, preferred_element_type=jnp.float32) + shift_b
    )
    visiting_logit = (
        score_multiplier * jnp.dot(img_b, vis_texts.T, preferred_element_type=jnp.float32) + shift_b
    )
    matched_gradient = (score_multiplier * (jax.nn.sigmoid(matched_logit) - positive)).astype(
        jnp.bfloat16
    )
    vis_grad = (score_multiplier * jax.nn.sigmoid(visiting_logit)).astype(jnp.bfloat16)
    img_dunit = jnp.dot(matched_gradient, own_texts, preferred_element_type=jnp.float32)
    img_dunit = img_dunit + jnp.dot(vis_grad, vis_texts, preferred_element_type=jnp.float32)
    own_terms = row_terms(matched_gradient, img_b)
    vis_terms = row_terms(vis_grad, img_b)
    returned = passed_along(vis_terms.astype(jnp.bfloat16), "loop", -1)
    own_sum, vis_sum = (
        lax.psum_scatter(
            own_terms.astype(jnp.bfloat16), "narrow", scatter_dimension=0, tiled=True
        ).astype(jnp.float32),
        lax.psum_scatter(
            returned.astype(jnp.float32).astype(jnp.bfloat16),
            "narrow",
            scatter_dimension=0,
            tiled=True,
        ).astype(jnp.float32),
    )
    txt_dunit = own_sum + vis_sum
    image_grad = (
        img_dunit - img_unit * jnp.sum(img_unit * img_dunit, axis=-1, keepdims=True)
    ) * img_inv
    text_grad = (
        txt_dunit - txt_unit * jnp.sum(txt_unit * txt_dunit, axis=-1, keepdims=True)
    ) * text_inverse_norm
    return (image_grad, text_grad)


def solution(mesh):
    return jax.shard_map(
        local,
        mesh=mesh,
        in_specs=(
            P(("loop", "narrow"), None),
            P(("loop", "narrow"), None),
            P("loop", None),
            P(),
            P(),
        ),
        out_specs=(P(("loop", "narrow"), None), P(("loop", "narrow"), None)),
        check_vma=False,
    )
```

profile of v0, /device:TPU:1, one launch (start us, length us, event | category | flops | bytes accessed | tf_op | source)
XLA Modules:
  0.0 312.9 jit_solution(9836308730830189052)
XLA Ops:
  7.2 0.0 copy-start
  7.2 0.0 copy-start.1
  7.2 0.0 all-gather.2.cloned.1.call-start
  7.2 1.3 fusion.28
  8.5 2.0 fusion.15
  10.5 0.0 all-gather.2.cloned.1.call-update
  10.5 0.0 reduce-scatter.3.cloned.1.call-start
  11.9 0.0 copy-done
  11.9 0.1 constant_dynamic-slice_fusion
  12.0 0.0 copy-done.1
  12.0 0.2 fusion.24
  12.2 38.8 %all-gather.2.cloned.1.call-done = bf16[896,1152]{1,0:T(8,128)(2,1)} async-done(((bf16[224,1152]{1,0:T(8,128)(2,1)}), bf16[896,1152]{1,0:T(8,128)(2,1)}) %all-gather.2.cloned.1.call-update) | async-done | bytes 2064400 | tf_op jit(solution)/shard_map/all_gather | solution.py:32
  51.0 4.4 %collective-permute-start = (bf16[896,1152]{1,0:T(8,128)(2,1)}, bf16[896,1152]{1,0:T(8,128)(2,1)S(1)}, u32[]{:S(2)}, u32[]{:S(2)}) collective-permute-start(bf16[896,1152]{1,0:T(8,128)(2,1)} %all-gather.2.cloned.1.call-done), channel_id=1, source_target_pairs={{0,4},{4,8},{8,12},{12,16},{16,20},{20,24},{24,28},{28,32},{32,36}... | collective-permute-start | bytes 6193160 | tf_op jit(solution)/shard_map/ppermute | solution.py:9
  55.4 2.5 fusion.19
  57.9 2.2 convolution_convert_fusion.1
  60.1 0.0 reduce-scatter.3.cloned.1.call-update
  60.1 0.0 reduce-scatter.5.cloned.1.call-start
  60.1 100.6 %collective-permute-done = bf16[896,1152]{1,0:T(8,128)(2,1)S(1)} collective-permute-done((bf16[896,1152]{1,0:T(8,128)(2,1)}, bf16[896,1152]{1,0:T(8,128)(2,1)S(1)}, u32[]{:S(2)}, u32[]{:S(2)}) %collective-permute-start) | collective-permute-done | bytes 2064416 | tf_op jit(solution)/shard_map/ppermute | solution.py:9
  160.8 0.0 copy-start.4
  160.8 1.3 copy-done.4
  162.1 0.9 fusion.20
  163.0 0.0 copy-start.3
  163.1 0.9 convolution_convert_fusion
  163.9 10.4 %collective-permute-start.1 = (bf16[896,1152]{1,0:T(8,128)(2,1)S(1)}, bf16[896,1152]{1,0:T(8,128)(2,1)}, u32[]{:S(2)}, u32[]{:S(2)}) collective-permute-start(bf16[896,1152]{1,0:T(8,128)(2,1)S(1)} %convolution_convert_fusion), channel_id=1, source_target_pairs={{0,508},{4,0},{8,4},{12,8},{16,12},{20,16},{24,20},{28,24},{32,28}... | collective-permute-start | bytes 6193160 | tf_op jit(solution)/shard_map/ppermute | solution.py:9
  174.3 100.8 %collective-permute-done.1 = bf16[896,1152]{1,0:T(8,128)(2,1)} collective-permute-done((bf16[896,1152]{1,0:T(8,128)(2,1)S(1)}, bf16[896,1152]{1,0:T(8,128)(2,1)}, u32[]{:S(2)}, u32[]{:S(2)}) %collective-permute-start.1) | collective-permute-done | bytes 2064416 | tf_op jit(solution)/shard_map/ppermute | solution.py:9
  275.1 0.0 reduce-scatter.5.cloned.1.call-update
  275.1 0.0 copy-done.3
  275.1 0.0 copy-start.5
  275.1 0.7 fusion.33
  275.9 0.8 copy-done.5
  276.7 0.9 fusion.21
  277.6 0.0 copy-start.2
  277.6 1.2 fusion.23
  278.8 0.0 reduce-scatter.3.cloned.1.call-done
  278.8 23.5 %reduce-scatter.5.cloned.1.call-done = bf16[224,1152]{1,0:T(8,128)(2,1)} async-done(((bf16[896,1152]{1,0:T(8,128)(2,1)}), bf16[224,1152]{1,0:T(8,128)(2,1)}) %reduce-scatter.5.cloned.1.call-update) | async-done | bytes 516112 | tf_op jit(solution)/shard_map/reduce_scatter | solution.py:59
  302.3 0.0 copy-done.2
  302.3 1.6 fusion.25
  303.9 2.5 fusion.27
  (2 shorter events, 0.0 us)
Async XLA Ops:
  7.2 4.7 %copy-start = (s32[1,896]{1,0:T(1,128)S(1)}, s32[1,896]{1,0:T(1,128)}, u32[]{:S(2)}) copy-start(s32[1,896]{1,0:T(1,128)} %param.7) | copy-start | bytes 10756
  7.2 4.8 %copy-start.1 = (bf16[224,1152]{1,0:T(8,128)(2,1)S(1)}, bf16[224,1152]{1,0:T(8,128)(2,1)}, u32[]{:S(2)}) copy-start(bf16[224,1152]{1,0:T(8,128)(2,1)} %param.5) | copy-start | bytes 1548292
  7.2 43.8 %all-gather.2.cloned.1.call-start = ((), (), s32[]{:S(2)}) async-start(), calls=%async_computation.2 | async-start | bytes 2580480 | tf_op jit(solution)/shard_map/all_gather | solution.py:32
  10.5 268.3 %reduce-scatter.3.cloned.1.call-start = ((), (), s32[]{:S(2)}) async-start(), calls=%async_computation.3 | async-start | bytes 2580480 | tf_op jit(solution)/shard_map/reduce_scatter | solution.py:56
  51.0 109.8 %collective-permute-start = (bf16[896,1152]{1,0:T(8,128)(2,1)}, bf16[896,1152]{1,0:T(8,128)(2,1)S(1)}, u32[]{:S(2)}, u32[]{:S(2)}) collective-permute-start(bf16[896,1152]{1,0:T(8,128)(2,1)} %all-gather.2.cloned.1.call-done), channel_id=1, source_target_pairs={{0,4},{4,8},{8,12},{12,16},{16,20},{20,24},{24,28},{28,32},{32,36}... | collective-permute-start | bytes 6193160 | tf_op jit(solution)/shard_map/ppermute | solution.py:9
  60.1 242.3 %reduce-scatter.5.cloned.1.call-start = ((), (), s32[]{:S(2)}) async-start(), calls=%async_computation.4 | async-start | bytes 2580480 | tf_op jit(solution)/shard_map/reduce_scatter | solution.py:59
  160.8 1.3 copy-start.4
  163.0 112.1 %copy-start.3 = (bf16[896,1152]{1,0:T(8,128)(2,1)S(1)}, bf16[896,1152]{1,0:T(8,128)(2,1)}, u32[]{:S(2)}) copy-start(bf16[896,1152]{1,0:T(8,128)(2,1)} %all-gather.2.cloned.1.call-done) | copy-start | bytes 6193156
  163.9 111.2 %collective-permute-start.1 = (bf16[896,1152]{1,0:T(8,128)(2,1)S(1)}, bf16[896,1152]{1,0:T(8,128)(2,1)}, u32[]{:S(2)}, u32[]{:S(2)}) collective-permute-start(bf16[896,1152]{1,0:T(8,128)(2,1)S(1)} %convolution_convert_fusion), channel_id=1, source_target_pairs={{0,508},{4,0},{8,4},{12,8},{16,12},{20,16},{24,20},{28,24},{32,28}... | collective-permute-start | bytes 6193160 | tf_op jit(solution)/shard_map/ppermute | solution.py:9
  275.1 1.6 copy-start.5
  277.6 24.7 %copy-start.2 = (bf16[224,1152]{1,0:T(8,128)(2,1)S(1)}, bf16[224,1152]{1,0:T(8,128)(2,1)}, u32[]{:S(2)}) copy-start(bf16[224,1152]{1,0:T(8,128)(2,1)} %param.6) | copy-start | bytes 1548292
Sparse Core Ops, SparseCore 0:
  10.7 40.2 all-gather.1
  60.2 85.3 reduce-scatter.2
  275.2 27.0 reduce-scatter.4
where the time goes:
time: 313 us
  waiting for transfers between devices  264 us (84%)
  between operations  15.2 us (5%)
  starting transfers between devices  14.9 us (5%)
  other arithmetic  8.68 us (3%)
  matrix products  8.13 us (3%)
    ppermute x2, waiting for transfers between devices, passed_along(): return lax.ppermute(x, axis, [(i, (i + by) % peers) for i in range(peers)])  201 us
    all_gather x1, waiting for transfers between devices, local(): own_texts = lax.all_gather(txt_b, 'narrow', axis=0, tiled=True)  38.8 us
    reduce_scatter x1, waiting for transfers between devices, local(): lax.psum_scatter(returned.astype(jnp.float32).astype(jnp.bfloat16), 'narr...  23.5 us
    ppermute x2, starting transfers between devices, passed_along(): return lax.ppermute(x, axis, [(i, (i + by) % peers) for i in range(peers)])  14.7 us
  transfers between devices with their start and end apart: 5, of which 4 were waited for; matrix products, arithmetic and copies ran while one was open for 3% of the time, Pallas kernels for 0%

commit v1 on v0

v1 whole, which is shorter than its diff:
```python
import functools

import jax
import jax.numpy as jnp
from jax import lax
from jax.experimental import pallas as pl
from jax.experimental.pallas import tpu as pltpu
from jax.sharding import PartitionSpec as P

AXES = ("loop", "narrow")
VMEM = pl.BlockSpec(memory_space=pltpu.VMEM)
SMEM = pl.BlockSpec(memory_space=pltpu.SMEM)
NT = (((1,), (1,)), ((), ()))
NN = (((1,), (0,)), ((), ()))


def inv_norm(values):
    return lax.rsqrt(jnp.sum(values * values, axis=-1, keepdims=True) + 1e-06)


def dot(a, b, dims):
    return lax.dot_general(a, b, dims, preferred_element_type=jnp.float32)


def call(body, out_shape, n_smem, n_vmem, flops=0):
    return pl.pallas_call(
        body,
        out_shape=out_shape,
        in_specs=[SMEM] * n_smem + [VMEM] * n_vmem,
        out_specs=jax.tree.map(lambda _: VMEM, out_shape),
        compiler_params=pltpu.CompilerParams(vmem_limit_bytes=32 * 1024 * 1024),
        cost_estimate=pl.CostEstimate(
            flops=flops, bytes_accessed=4 * 1024 * 1024, transcendentals=0
        ),
    )


def unit_body(odd, img, txt, p, q, pq):
    rows = img.shape[0]

    def unit(ref):
        values = ref[...].astype(jnp.float32)
        return (values * inv_norm(values)).astype(jnp.bfloat16)

    def put(first, second):
        p[...] = first
        q[...] = second
        pq[:rows] = first
        pq[rows:] = second

    img_b, txt_b = unit(img), unit(txt)

    @pl.when(odd[0] == 0)
    def _():
        put(img_b, txt_b)

    @pl.when(odd[0] == 1)
    def _():
        put(txt_b, img_b)


def weights(x, y, scale, shift):
    return scale * lax.logistic(scale * dot(x, y, NT) + shift)


def add_terms(x, ys, scale, shift):
    total = None
    for y in ys:
        term = dot(weights(x, y, scale, shift).astype(jnp.bfloat16), y, NN)
        total = term if total is None else total + term
    return total


def add_own(x, ys, u, v, scale, shift):
    total = None
    for j, y in enumerate(ys):
        positive = (u == v[j : j + 1]).astype(jnp.float32)
        g = scale * (lax.logistic(scale * dot(x, y, NT) + shift) - positive)
        term = dot(g.astype(jnp.bfloat16), y, NN)
        total = term if total is None else total + term
    return total


def early_body(scale, shift, p, x2, y0, y0c, part_p, part_x):
    ys = [y0[...], y0c[...]]
    part_x[...] = add_terms(x2[...], ys, scale[0], shift[0])
    part_p[...] = add_terms(p[...], ys, scale[0], shift[0])


def own_q_body(scale, shift, q, pq_c, p, x2, x2c, u, v, out):
    rows = q.shape[0]
    ys = [p[...], pq_c[:rows], x2[...], x2c[...]]
    out[...] = add_own(q[...], ys, u[...], v[...], scale[0], shift[0])


def late_body(scale, shift, x2, y1, y1c, part_x, out):
    ys = [y1[...], y1c[...]]
    out[...] = (part_x[...] + add_terms(x2[...], ys, scale[0], shift[0])).astype(jnp.bfloat16)


def tangent(raw, dunit):
    values = raw.astype(jnp.float32)
    inv = inv_norm(values)
    unit = values * inv
    return (dunit - unit * jnp.sum(unit * dunit, axis=-1, keepdims=True)) * inv


def rest_p_body(scale, shift, odd, img, txt, p, y1, y1c, part_p, q, pq_c, w2, w2c, u, v, out):
    rows = p.shape[0]
    x = p[...]
    total = part_p[...] + add_terms(x, [y1[...], y1c[...]], scale[0], shift[0])
    ys = [q[...], pq_c[rows:], w2[...], w2c[...]]
    total = total + add_own(x, ys, u[...], v[...], scale[0], shift[0])

    @pl.when(odd[0] == 0)
    def _():
        out[...] = tangent(img[...], total)

    @pl.when(odd[0] == 1)
    def _():
        out[...] = tangent(txt[...], total)


def last_body(odd, img, txt, own_q, back, grad_p, img_grad, txt_grad):
    total = own_q[...] + back[...].astype(jnp.float32)

    @pl.when(odd[0] == 0)
    def _():
        img_grad[...] = grad_p[...]
        txt_grad[...] = tangent(txt[...], total)

    @pl.when(odd[0] == 1)
    def _():
        img_grad[...] = tangent(img[...], total)
        txt_grad[...] = grad_p[...]


def local(picture_vectors, caption_vectors, caption_position, sharpness_factor, affine_offset):
    groups = lax.axis_size("loop")
    rows, depth = picture_vectors.shape
    img, txt, scale, shift = picture_vectors, caption_vectors, sharpness_factor, affine_offset

    def swap(to):
        pairs = []
        for g in range(groups):
            for n in range(4):
                h, m = to(g, n)
                pairs.append((g * 4 + n, (h % groups) * 4 + m))
        return lambda x: lax.ppermute(x, AXES, pairs)

    core = swap(lambda g, n: (g, n ^ 1))
    chip = swap(lambda g, n: (g, n ^ 2))
    group = swap(lambda g, n: (g + 1, n - 2) if n >= 2 else (g - 1, n + 2))

    here = lax.axis_index("narrow")
    odd = here // 2
    odd1 = odd.reshape(1).astype(jnp.int32)
    block = jax.ShapeDtypeStruct((rows, depth), jnp.bfloat16)
    wide = jax.ShapeDtypeStruct((rows, depth), jnp.float32)
    both = jax.ShapeDtypeStruct((2 * rows, depth), jnp.bfloat16)

    p, q, pq = call(unit_body, (block, block, both), 1, 2)(odd1, img, txt)
    x2 = chip(q)
    y0 = group(p)
    pq_c = core(pq)

    order = here ^ jnp.arange(4, dtype=jnp.int32)
    matches = caption_position.reshape(4, rows)[order]
    places = order[:, None] * rows + jnp.arange(rows, dtype=jnp.int32)[None, :]
    is_odd = odd == 1
    u_p = jnp.where(is_odd, places[0], matches[0])[:, None]
    u_q = jnp.where(is_odd, matches[0], places[0])[:, None]
    v_p = jnp.where(is_odd, matches, places)
    v_q = jnp.where(is_odd, places, matches)

    y1 = group(x2)
    w2 = chip(p)
    y0c = core(y0)
    x2c = core(x2)
    unit_flops = 4 * rows * rows * depth
    part_p, part_x = call(early_body, (wide, wide), 2, 4, 4 * unit_flops)(
        scale, shift, p, x2, y0, y0c
    )
    own_q = call(own_q_body, wide, 2, 7, 4 * unit_flops)(
        scale, shift, q, pq_c, p, x2, x2c, u_q, v_q
    )
    w2c = core(w2)
    y1c = core(y1)
    send = call(late_body, block, 2, 4, 2 * unit_flops)(scale, shift, x2, y1, y1c, part_x)
    back = chip(send)
    grad_p = call(rest_p_body, wide, 3, 12, 6 * unit_flops)(
        scale, shift, odd1, img, txt, p, y1, y1c, part_p, q, pq_c, w2, w2c, u_p, v_p
    )
    return call(last_body, (wide, wide), 1, 5)(odd1, img, txt, own_q, back, grad_p)


def solution(mesh):
    return jax.shard_map(
        local,
        mesh=mesh,
        in_specs=(
            P(AXES, None),
            P(AXES, None),
            P("loop", None),
            P(),
            P(),
        ),
        out_specs=(P(AXES, None), P(AXES, None)),
        check_vma=False,
    )
```

time: 313 us -> 82.1 us (0.26)
  waiting for transfers between devices: 264 us -> 7.62 us
  starting transfers between devices: 14.9 us -> 48.8 us
  Pallas kernels: 0 us -> 16.6 us
  between operations: 15.2 us -> 2.22 us
  other arithmetic: 8.68 us -> 0.11 us
  matrix products: 8.13 us -> 0 us
  local copies, waits for them, and re-layouts: 2.27 us -> 6.01 us
    ppermute x2 -> x10, waiting for transfers between devices: 201 us -> 7.62 us  [swap(): return lambda x: lax.ppermute(x, AXES, pairs)]
    all_gather x1 -> x0, waiting for transfers between devices: 38.8 us -> none  [local(): own_texts = lax.all_gather(txt_b, 'narrow', axis=0, tiled=True)]
    ppermute x2 -> x10, starting transfers between devices: 14.7 us -> 48.8 us  [swap(): return lambda x: lax.ppermute(x, AXES, pairs)]
    reduce_scatter x2 -> x0, waiting for transfers between devices: 23.5 us -> none  [the longest x1 23.5 us: local(): lax.psum_scatter(returned.astype(jnp.float32).astype(jnp.bfloat16), 'narr...]
    pallas_call x0 -> x6, Pallas kernels: none -> 16.6 us  [the longest x1 4.42 us: local(): call(rest_p_body, wide, 3, 12, 6 * unit_flops)]
    dot_general x6 -> x0, matrix products: 8.13 us -> none  [the longest x2 3.03 us: row_terms(): lax.dot_general(weights, img_b, (((0,), (0,)), ((), ())), preferred_eleme...]
    mul x2 -> x1, other arithmetic: 3.67 us -> 0.01 us  [local(): places = order[:, None] * rows + jnp.arange(rows, dtype=jnp.int32)[None, :]]
  transfers between devices with their start and end apart: 5 -> 10, of which waited for: 4 -> 2; matrix products, arithmetic and copies ran while one was open for 3% -> 1% of each run, Pallas kernels for 0% -> 15%
where the time goes in v1:
time: 82.1 us; the launch traced here: 81.4 us
  starting transfers between devices  48.8 us (59%)
  Pallas kernels  16.6 us (20%)
  waiting for transfers between devices  7.62 us (9%)
  local copies, waits for them, and re-layouts  6.01 us (7%)
  between operations  2.22 us (3%)
    ppermute x10, starting transfers between devices, swap(): return lambda x: lax.ppermute(x, AXES, pairs)  48.8 us
    ppermute x10, waiting for transfers between devices, swap(): return lambda x: lax.ppermute(x, AXES, pairs)  7.62 us
    unnamed x20, local copies, waits for them, and re-layouts  5.11 us
    pallas_call x1, Pallas kernels, local(): call(rest_p_body, wide, 3, 12, 6 * unit_flops)  4.42 us
    pallas_call x1, Pallas kernels, local(): call(own_q_body, wide, 2, 7, 4 * unit_flops)  3.26 us
    pallas_call x1, Pallas kernels, local(): call(early_body, (wide, wide), 2, 4, 4 * unit_flops)  2.9 us
    pallas_call x1, Pallas kernels, local(): call(last_body, (wide, wide), 1, 5)(odd1, img, txt, own_q, back, grad_p)  2.88 us
    pallas_call x1, Pallas kernels, local(): call(late_body, block, 2, 4, 2 * unit_flops)  1.72 us
  transfers between devices with their start and end apart: 10, of which 2 were waited for; matrix products, arithmetic and copies ran while one was open for 1% of the time, Pallas kernels for 15%

profile of v1, /device:TPU:1, one launch (start us, length us, event | category | flops | bytes accessed | tf_op | source)
XLA Modules:
  0.0 81.4 jit_solution(5675076084598634273)
XLA Ops:
  0.6 0.0 copy-start
  0.7 1.0 %copy-done = bf16[224,1152]{1,0:T(8,128)(2,1)S(1)} copy-done((bf16[224,1152]{1,0:T(8,128)(2,1)S(1)}, bf16[224,1152]{1,0:T(8,128)(2,1)}, u32[]{:S(2)}) %copy-start) | copy-done | bytes 516120
  1.7 0.0 copy-start.2
  1.7 1.0 %copy-done.2 = bf16[224,1152]{1,0:T(8,128)(2,1)S(1)} copy-done((bf16[224,1152]{1,0:T(8,128)(2,1)S(1)}, bf16[224,1152]{1,0:T(8,128)(2,1)}, u32[]{:S(2)}) %copy-start.2) | copy-done | bytes 516120
  2.7 1.5 %shard_map.68 = (bf16[224,1152]{1,0:T(8,128)(2,1)S(1)}, bf16[224,1152]{1,0:T(8,128)(2,1)S(1)}, bf16[448,1152]{1,0:T(8,128)(2,1)}) custom-call(s32[1]{0:T(128)} %bitcast.odd, bf16[224,1152]{1,0:T(8,128)(2,1)S(1)} %copy-done, bf16[224,1152]{1,0:T(8,128)(2,1)S(1)} %copy-done.2), custom_call_target="tpu_custom_call" | custom-call | bytes 4194304 | tf_op jit(solution)/shard_map/pallas_call | solution.py:162
  4.2 4.8 %collective-permute-start.1 = (bf16[224,1152]{1,0:T(8,128)(2,1)S(1)}, bf16[224,1152]{1,0:T(8,128)(2,1)S(1)}, u32[]{:S(2)}, u32[]{:S(2)}) collective-permute-start(bf16[224,1152]{1,0:T(8,128)(2,1)S(1)} %get-tuple-element.7.q), channel_id=1, source_target_pairs={{0,2},{1,3},{2,0},{3,1},{4,6},{5,7},{6,4},{7,5},{8,10},{9,11},{10,... | collective-permute-start | bytes 1548296 | tf_op jit(solution)/shard_map/ppermute | solution.py:149
  9.0 0.0 copy-start.9
  9.0 14.0 %collective-permute-start.5 = (bf16[224,1152]{1,0:T(8,128)(2,1)S(1)}, bf16[224,1152]{1,0:T(8,128)(2,1)}, u32[]{:S(2)}, u32[]{:S(2)}) collective-permute-start(bf16[224,1152]{1,0:T(8,128)(2,1)S(1)} %get-tuple-element.9.p), channel_id=1, source_target_pairs={{0,510},{1,511},{2,4},{3,5},{4,2},{5,3},{6,8},{7,9},{8,6},{9,7},{1... | collective-permute-start | bytes 1548296 | tf_op jit(solution)/shard_map/ppermute | solution.py:149
  23.0 0.0 collective-permute-done.1.x2
  23.0 0.0 copy-start.4
  23.0 12.4 %collective-permute-start.3 = (bf16[224,1152]{1,0:T(8,128)(2,1)S(1)}, bf16[224,1152]{1,0:T(8,128)(2,1)S(1)}, u32[]{:S(2)}, u32[]{:S(2)}) collective-permute-start(bf16[224,1152]{1,0:T(8,128)(2,1)S(1)} %collective-permute-done.1.x2), channel_id=1, source_target_pairs={{0,510},{1,511},{2,4},{3,5},{4,2},{5,3},{6,8},{7,9},{8,6},{9,7},{1... | collective-permute-start | bytes 1548296 | tf_op jit(solution)/shard_map/ppermute | solution.py:149
  35.4 1.9 %collective-permute-start.8 = (bf16[224,1152]{1,0:T(8,128)(2,1)S(1)}, bf16[224,1152]{1,0:T(8,128)(2,1)}, u32[]{:S(2)}, u32[]{:S(2)}) collective-permute-start(bf16[224,1152]{1,0:T(8,128)(2,1)S(1)} %get-tuple-element.9.p), channel_id=1, source_target_pairs={{0,2},{1,3},{2,0},{3,1},{4,6},{5,7},{6,4},{7,5},{8,10},{9,11},{10,... | collective-permute-start | bytes 1548296 | tf_op jit(solution)/shard_map/ppermute | solution.py:149
  37.3 0.0 collective-permute-done.5.y0
  37.3 3.6 %collective-permute-start.6 = (bf16[224,1152]{1,0:T(8,128)(2,1)}, bf16[224,1152]{1,0:T(8,128)(2,1)}, u32[]{:S(2)}, u32[]{:S(2)}) collective-permute-start(bf16[224,1152]{1,0:T(8,128)(2,1)} %collective-permute-done.5.y0), channel_id=1, source_target_pairs={{0,1},{1,0},{2,3},{3,2},{4,5},{5,4},{6,7},{7,6},{8,9},{9,8},{10,11... | collective-permute-start | bytes 1548296 | tf_op jit(solution)/shard_map/ppermute | solution.py:149
  41.0 1.9 %collective-permute-start = (bf16[448,1152]{1,0:T(8,128)(2,1)}, bf16[448,1152]{1,0:T(8,128)(2,1)S(1)}, u32[]{:S(2)}, u32[]{:S(2)}) collective-permute-start(bf16[448,1152]{1,0:T(8,128)(2,1)} %get-tuple-element.8), channel_id=1, source_target_pairs={{0,1},{1,0},{2,3},{3,2},{4,5},{5,4},{6,7},{7,6},{8,9},{9,8},{10,11... | collective-permute-start | bytes 3096584 | tf_op jit(solution)/shard_map/ppermute | solution.py:149
  42.9 3.1 %collective-permute-done.3.y1 = bf16[224,1152]{1,0:T(8,128)(2,1)S(1)} collective-permute-done((bf16[224,1152]{1,0:T(8,128)(2,1)S(1)}, bf16[224,1152]{1,0:T(8,128)(2,1)S(1)}, u32[]{:S(2)}, u32[]{:S(2)}) %collective-permute-start.3) | collective-permute-done | bytes 516128 | tf_op jit(solution)/shard_map/ppermute | solution.py:149
  46.0 0.0 copy-done.4
  46.0 4.0 %collective-permute-start.4 = (bf16[224,1152]{1,0:T(8,128)(2,1)S(1)}, bf16[224,1152]{1,0:T(8,128)(2,1)S(1)}, u32[]{:S(2)}, u32[]{:S(2)}) collective-permute-start(bf16[224,1152]{1,0:T(8,128)(2,1)S(1)} %collective-permute-done.3.y1), channel_id=1, source_target_pairs={{0,1},{1,0},{2,3},{3,2},{4,5},{5,4},{6,7},{7,6},{8,9},{9,8},{10,11... | collective-permute-start | bytes 1548296 | tf_op jit(solution)/shard_map/ppermute | solution.py:149
  51.3 0.0 copy-done.9
  51.3 0.1 reshape.69
  51.4 0.6 gather_fusion
  52.0 1.9 %collective-permute-start.2 = (bf16[224,1152]{1,0:T(8,128)(2,1)}, bf16[224,1152]{1,0:T(8,128)(2,1)}, u32[]{:S(2)}, u32[]{:S(2)}) collective-permute-start(bf16[224,1152]{1,0:T(8,128)(2,1)} %copy-done.4), channel_id=1, source_target_pairs={{0,1},{1,0},{2,3},{3,2},{4,5},{5,4},{6,7},{7,6},{8,9},{9,8},{10,11... | collective-permute-start | bytes 1548296 | tf_op jit(solution)/shard_map/ppermute | solution.py:149
  53.9 0.0 collective-permute-done.8.w2
  53.9 2.4 %collective-permute-start.9 = (bf16[224,1152]{1,0:T(8,128)(2,1)}, bf16[224,1152]{1,0:T(8,128)(2,1)}, u32[]{:S(2)}, u32[]{:S(2)}) collective-permute-start(bf16[224,1152]{1,0:T(8,128)(2,1)} %collective-permute-done.8.w2), channel_id=1, source_target_pairs={{0,1},{1,0},{2,3},{3,2},{4,5},{5,4},{6,7},{7,6},{8,9},{9,8},{10,11... | collective-permute-start | bytes 1548296 | tf_op jit(solution)/shard_map/ppermute | solution.py:149
  56.3 0.0 collective-permute-done.6.y0c
  56.4 0.0 copy-start.5
  56.4 1.0 %copy-done.5 = bf16[224,1152]{1,0:T(8,128)(2,1)S(1)} copy-done((bf16[224,1152]{1,0:T(8,128)(2,1)S(1)}, bf16[224,1152]{1,0:T(8,128)(2,1)}, u32[]{:S(2)}) %copy-start.5) | copy-done | bytes 516120
  57.4 2.9 %shard_map.70 = (f32[224,1152]{1,0:T(8,128)S(1)}, f32[224,1152]{1,0:T(8,128)S(1)}) custom-call(f32[1]{0:T(128)S(6)} %copy.9.scale, f32[1]{0:T(128)S(6)} %copy.10.shift, bf16[224,1152]{1,0:T(8,128)(2,1)S(1)} %get-tuple-element.9.p, bf16[224,1152]{1,0:T(8,128)(2,1)S(1)} %copy-done.5, bf16[224,1152]{1,0:T(8,128)(2,1)} %collective-permute-done.5.y0, ...), custom_call_target="tpu_custom_call" | custom-call | flops 924844032 | bytes 4194304 | tf_op jit(solution)/shard_map/pallas_call | solution.py:181
  60.3 0.0 copy-start.7
  60.3 1.0 %copy-done.7 = f32[224,1152]{1,0:T(8,128)} copy-done((f32[224,1152]{1,0:T(8,128)}, f32[224,1152]{1,0:T(8,128)S(1)}, u32[]{:S(2)}) %copy-start.7) | copy-done | bytes 1032216
  61.3 0.0 collective-permute-done.4.y1c
  61.3 1.7 %shard_map.71 = bf16[224,1152]{1,0:T(8,128)(2,1)} custom-call(f32[1]{0:T(128)S(6)} %copy.9.scale, f32[1]{0:T(128)S(6)} %copy.10.shift, bf16[224,1152]{1,0:T(8,128)(2,1)S(1)} %copy-done.5, bf16[224,1152]{1,0:T(8,128)(2,1)S(1)} %collective-permute-done.3.y1, bf16[224,1152]{1,0:T(8,128)(2,1)S(1)} %collective-permute-done.4.y1c, ...), custom_call_target="tpu_custom_call" | custom-call | flops 462422016 | bytes 4194304 | tf_op jit(solution)/shard_map/pallas_call | solution.py:189
  63.0 1.9 %collective-permute-start.7 = (bf16[224,1152]{1,0:T(8,128)(2,1)}, bf16[224,1152]{1,0:T(8,128)(2,1)}, u32[]{:S(2)}, u32[]{:S(2)}) collective-permute-start(bf16[224,1152]{1,0:T(8,128)(2,1)} %shard_map.71), channel_id=1, source_target_pairs={{0,2},{1,3},{2,0},{3,1},{4,6},{5,7},{6,4},{7,5},{8,10},{9,11},{10,... | collective-permute-start | bytes 1548296 | tf_op jit(solution)/shard_map/ppermute | solution.py:149
  64.9 0.1 fusion
  65.0 0.1 copy.7.u
  65.1 0.1 copy.8.u
  65.3 0.0 collective-permute-done.pq_c
  65.3 0.0 collective-permute-done.2.x2c
  65.3 0.0 copy-start.6
  65.3 1.0 %copy-done.6 = bf16[224,1152]{1,0:T(8,128)(2,1)S(1)} copy-done((bf16[224,1152]{1,0:T(8,128)(2,1)S(1)}, bf16[224,1152]{1,0:T(8,128)(2,1)}, u32[]{:S(2)}) %copy-start.6) | copy-done | bytes 516120
  66.3 0.0 copy-start.1
  66.3 0.0 copy-start.3
  66.3 0.0 copy-start.8
  66.3 3.3 %shard_map.69.own_q = f32[224,1152]{1,0:T(8,128)S(1)} custom-call(f32[1]{0:T(128)S(6)} %copy.9.scale, f32[1]{0:T(128)S(6)} %copy.10.shift, bf16[224,1152]{1,0:T(8,128)(2,1)S(1)} %get-tuple-element.7.q, bf16[448,1152]{1,0:T(8,128)(2,1)S(1)} %collective-permute-done.pq_c, bf16[224,1152]{1,0:T(8,128)(2,1)S(1)} %get-tuple-element.9.p, ...), custom_call_target="tpu_custom_call" | custom-call | flops 924844032 | bytes 4194304 | tf_op jit(solution)/shard_map/pallas_call | solution.py:184
  69.6 0.0 collective-permute-done.9.w2c
  69.6 0.0 copy-done.1
  69.6 0.0 copy-done.3
  69.6 0.0 copy-done.8
  69.6 4.4 %shard_map.72.grad_p = f32[224,1152]{1,0:T(8,128)S(1)} custom-call(f32[1]{0:T(128)S(6)} %copy.9.scale, f32[1]{0:T(128)S(6)} %copy.10.shift, s32[1]{0:T(128)} %bitcast.odd, bf16[224,1152]{1,0:T(8,128)(2,1)S(1)} %copy-done.1, bf16[224,1152]{1,0:T(8,128)(2,1)S(1)} %copy-done.3, bf16[224,1152]{1,0:T(8,128)(2,1)S(1)} %get-tuple-element.9.p, ...), custom_call_target="tpu_custom_call" | custom-call | flops 1387266048 | bytes 4194304 | tf_op jit(solution)/shard_map/pallas_call | solution.py:191
  74.0 4.5 %collective-permute-done.7.back = bf16[224,1152]{1,0:T(8,128)(2,1)} collective-permute-done((bf16[224,1152]{1,0:T(8,128)(2,1)}, bf16[224,1152]{1,0:T(8,128)(2,1)}, u32[]{:S(2)}, u32[]{:S(2)}) %collective-permute-start.7) | collective-permute-done | bytes 516128 | tf_op jit(solution)/shard_map/ppermute | solution.py:149
  78.6 2.9 %shard_map.73 = (f32[224,1152]{1,0:T(8,128)}, f32[224,1152]{1,0:T(8,128)}) custom-call(s32[1]{0:T(128)} %bitcast.odd, bf16[224,1152]{1,0:T(8,128)(2,1)S(1)} %copy-done.1, bf16[224,1152]{1,0:T(8,128)(2,1)S(1)} %copy-done.3, f32[224,1152]{1,0:T(8,128)S(1)} %shard_map.69.own_q, bf16[224,1152]{1,0:T(8,128)(2,1)} %collective-permute-done.7.back, ...), custom_call_target="tpu_custom_call" | custom-call | bytes 4194304 | tf_op jit(solution)/shard_map/pallas_call | solution.py:194
  (5 shorter events, 0.0 us)
Async XLA Ops:
  0.6 1.0 %copy-start = (bf16[224,1152]{1,0:T(8,128)(2,1)S(1)}, bf16[224,1152]{1,0:T(8,128)(2,1)}, u32[]{:S(2)}) copy-start(bf16[224,1152]{1,0:T(8,128)(2,1)} %img.5) | copy-start | bytes 1548292
  1.7 1.0 %copy-start.2 = (bf16[224,1152]{1,0:T(8,128)(2,1)S(1)}, bf16[224,1152]{1,0:T(8,128)(2,1)}, u32[]{:S(2)}) copy-start(bf16[224,1152]{1,0:T(8,128)(2,1)} %txt.5) | copy-start | bytes 1548292
  4.2 18.8 %collective-permute-start.1 = (bf16[224,1152]{1,0:T(8,128)(2,1)S(1)}, bf16[224,1152]{1,0:T(8,128)(2,1)S(1)}, u32[]{:S(2)}, u32[]{:S(2)}) collective-permute-start(bf16[224,1152]{1,0:T(8,128)(2,1)S(1)} %get-tuple-element.7.q), channel_id=1, source_target_pairs={{0,2},{1,3},{2,0},{3,1},{4,6},{5,7},{6,4},{7,5},{8,10},{9,11},{10,... | collective-permute-start | bytes 1548296 | tf_op jit(solution)/shard_map/ppermute | solution.py:149
  9.0 42.3 %copy-start.9 = (s32[1,896]{1,0:T(1,128)S(1)}, s32[1,896]{1,0:T(1,128)}, u32[]{:S(2)}) copy-start(s32[1,896]{1,0:T(1,128)} %param.7) | copy-start | bytes 10756
  9.0 28.3 %collective-permute-start.5 = (bf16[224,1152]{1,0:T(8,128)(2,1)S(1)}, bf16[224,1152]{1,0:T(8,128)(2,1)}, u32[]{:S(2)}, u32[]{:S(2)}) collective-permute-start(bf16[224,1152]{1,0:T(8,128)(2,1)S(1)} %get-tuple-element.9.p), channel_id=1, source_target_pairs={{0,510},{1,511},{2,4},{3,5},{4,2},{5,3},{6,8},{7,9},{8,6},{9,7},{1... | collective-permute-start | bytes 1548296 | tf_op jit(solution)/shard_map/ppermute | solution.py:149
  23.0 23.0 %copy-start.4 = (bf16[224,1152]{1,0:T(8,128)(2,1)}, bf16[224,1152]{1,0:T(8,128)(2,1)S(1)}, u32[]{:S(2)}) copy-start(bf16[224,1152]{1,0:T(8,128)(2,1)S(1)} %collective-permute-done.1.x2) | copy-start | bytes 1548292
  23.0 23.0 %collective-permute-start.3 = (bf16[224,1152]{1,0:T(8,128)(2,1)S(1)}, bf16[224,1152]{1,0:T(8,128)(2,1)S(1)}, u32[]{:S(2)}, u32[]{:S(2)}) collective-permute-start(bf16[224,1152]{1,0:T(8,128)(2,1)S(1)} %collective-permute-done.1.x2), channel_id=1, source_target_pairs={{0,510},{1,511},{2,4},{3,5},{4,2},{5,3},{6,8},{7,9},{8,6},{9,7},{1... | collective-permute-start | bytes 1548296 | tf_op jit(solution)/shard_map/ppermute | solution.py:149
  35.4 18.5 %collective-permute-start.8 = (bf16[224,1152]{1,0:T(8,128)(2,1)S(1)}, bf16[224,1152]{1,0:T(8,128)(2,1)}, u32[]{:S(2)}, u32[]{:S(2)}) collective-permute-start(bf16[224,1152]{1,0:T(8,128)(2,1)S(1)} %get-tuple-element.9.p), channel_id=1, source_target_pairs={{0,2},{1,3},{2,0},{3,1},{4,6},{5,7},{6,4},{7,5},{8,10},{9,11},{10,... | collective-permute-start | bytes 1548296 | tf_op jit(solution)/shard_map/ppermute | solution.py:149
  37.3 19.0 %collective-permute-start.6 = (bf16[224,1152]{1,0:T(8,128)(2,1)}, bf16[224,1152]{1,0:T(8,128)(2,1)}, u32[]{:S(2)}, u32[]{:S(2)}) collective-permute-start(bf16[224,1152]{1,0:T(8,128)(2,1)} %collective-permute-done.5.y0), channel_id=1, source_target_pairs={{0,1},{1,0},{2,3},{3,2},{4,5},{5,4},{6,7},{7,6},{8,9},{9,8},{10,11... | collective-permute-start | bytes 1548296 | tf_op jit(solution)/shard_map/ppermute | solution.py:149
  41.0 24.3 %collective-permute-start = (bf16[448,1152]{1,0:T(8,128)(2,1)}, bf16[448,1152]{1,0:T(8,128)(2,1)S(1)}, u32[]{:S(2)}, u32[]{:S(2)}) collective-permute-start(bf16[448,1152]{1,0:T(8,128)(2,1)} %get-tuple-element.8), channel_id=1, source_target_pairs={{0,1},{1,0},{2,3},{3,2},{4,5},{5,4},{6,7},{7,6},{8,9},{9,8},{10,11... | collective-permute-start | bytes 3096584 | tf_op jit(solution)/shard_map/ppermute | solution.py:149
  46.0 15.3 %collective-permute-start.4 = (bf16[224,1152]{1,0:T(8,128)(2,1)S(1)}, bf16[224,1152]{1,0:T(8,128)(2,1)S(1)}, u32[]{:S(2)}, u32[]{:S(2)}) collective-permute-start(bf16[224,1152]{1,0:T(8,128)(2,1)S(1)} %collective-permute-done.3.y1), channel_id=1, source_target_pairs={{0,1},{1,0},{2,3},{3,2},{4,5},{5,4},{6,7},{7,6},{8,9},{9,8},{10,11... | collective-permute-start | bytes 1548296 | tf_op jit(solution)/shard_map/ppermute | solution.py:149
  52.0 13.3 %collective-permute-start.2 = (bf16[224,1152]{1,0:T(8,128)(2,1)}, bf16[224,1152]{1,0:T(8,128)(2,1)}, u32[]{:S(2)}, u32[]{:S(2)}) collective-permute-start(bf16[224,1152]{1,0:T(8,128)(2,1)} %copy-done.4), channel_id=1, source_target_pairs={{0,1},{1,0},{2,3},{3,2},{4,5},{5,4},{6,7},{7,6},{8,9},{9,8},{10,11... | collective-permute-start | bytes 1548296 | tf_op jit(solution)/shard_map/ppermute | solution.py:149
  53.9 15.7 %collective-permute-start.9 = (bf16[224,1152]{1,0:T(8,128)(2,1)}, bf16[224,1152]{1,0:T(8,128)(2,1)}, u32[]{:S(2)}, u32[]{:S(2)}) collective-permute-start(bf16[224,1152]{1,0:T(8,128)(2,1)} %collective-permute-done.8.w2), channel_id=1, source_target_pairs={{0,1},{1,0},{2,3},{3,2},{4,5},{5,4},{6,7},{7,6},{8,9},{9,8},{10,11... | collective-permute-start | bytes 1548296 | tf_op jit(solution)/shard_map/ppermute | solution.py:149
  56.4 1.0 %copy-start.5 = (bf16[224,1152]{1,0:T(8,128)(2,1)S(1)}, bf16[224,1152]{1,0:T(8,128)(2,1)}, u32[]{:S(2)}) copy-start(bf16[224,1152]{1,0:T(8,128)(2,1)} %copy-done.4) | copy-start | bytes 1548292
  60.3 1.0 %copy-start.7 = (f32[224,1152]{1,0:T(8,128)}, f32[224,1152]{1,0:T(8,128)S(1)}, u32[]{:S(2)}) copy-start(f32[224,1152]{1,0:T(8,128)S(1)} %get-tuple-element.11.part_p) | copy-start | bytes 3096580
  63.0 15.6 %collective-permute-start.7 = (bf16[224,1152]{1,0:T(8,128)(2,1)}, bf16[224,1152]{1,0:T(8,128)(2,1)}, u32[]{:S(2)}, u32[]{:S(2)}) collective-permute-start(bf16[224,1152]{1,0:T(8,128)(2,1)} %shard_map.71), channel_id=1, source_target_pairs={{0,2},{1,3},{2,0},{3,1},{4,6},{5,7},{6,4},{7,5},{8,10},{9,11},{10,... | collective-permute-start | bytes 1548296 | tf_op jit(solution)/shard_map/ppermute | solution.py:149
  65.3 1.0 %copy-start.6 = (bf16[224,1152]{1,0:T(8,128)(2,1)S(1)}, bf16[224,1152]{1,0:T(8,128)(2,1)}, u32[]{:S(2)}) copy-start(bf16[224,1152]{1,0:T(8,128)(2,1)} %copy-done.4) | copy-start | bytes 1548292
  66.3 3.3 %copy-start.1 = (bf16[224,1152]{1,0:T(8,128)(2,1)S(1)}, bf16[224,1152]{1,0:T(8,128)(2,1)}, u32[]{:S(2)}) copy-start(bf16[224,1152]{1,0:T(8,128)(2,1)} %img.5) | copy-start | bytes 1548292
  66.3 3.3 %copy-start.3 = (bf16[224,1152]{1,0:T(8,128)(2,1)S(1)}, bf16[224,1152]{1,0:T(8,128)(2,1)}, u32[]{:S(2)}) copy-start(bf16[224,1152]{1,0:T(8,128)(2,1)} %txt.5) | copy-start | bytes 1548292
  66.3 3.3 %copy-start.8 = (f32[224,1152]{1,0:T(8,128)S(1)}, f32[224,1152]{1,0:T(8,128)}, u32[]{:S(2)}) copy-start(f32[224,1152]{1,0:T(8,128)} %copy-done.7) | copy-start | bytes 3096580

commit v2 on v1

v2 whole, which is shorter than its diff:
```python
import jax
import jax.numpy as jnp
from jax import lax
from jax.experimental import pallas as pl
from jax.experimental.pallas import tpu as pltpu
from jax.sharding import PartitionSpec as P

AXES = ("loop", "narrow")
VMEM = pl.BlockSpec(memory_space=pltpu.VMEM)
SMEM = pl.BlockSpec(memory_space=pltpu.SMEM)
HBM = pl.BlockSpec(memory_space=pltpu.HBM)
NT = (((1,), (1,)), ((), ()))
NN = (((1,), (0,)), ((), ()))
PIECES = 2
JOIN = 8 * 10**9


def inv_norm(values):
    return lax.rsqrt(jnp.sum(values * values, axis=-1, keepdims=True) + 1e-06)


def dot(a, b, dims):
    return lax.dot_general(a, b, dims, preferred_element_type=jnp.float32)


def call(body, out_shape, in_specs, out_specs=None, vmem=6, flops=1, **kwargs):
    if out_specs is None:
        out_specs = jax.tree.map(lambda _: VMEM, out_shape)
    return pl.pallas_call(
        body,
        out_shape=out_shape,
        in_specs=in_specs,
        out_specs=out_specs,
        compiler_params=pltpu.CompilerParams(vmem_limit_bytes=vmem * 1024 * 1024),
        cost_estimate=pl.CostEstimate(
            flops=flops, bytes_accessed=1, transcendentals=0
        ),
        **kwargs,
    )


def unit_body(odd, img, txt, p, q, raw, sems):
    rows = img.shape[0]
    size = rows // PIECES
    copies = []
    for j in range(PIECES):
        part = pl.ds(j * size, size)
        for i, ref in enumerate((img, txt)):
            copies.append(
                pltpu.make_async_copy(ref.at[part], raw.at[i, part], sems.at[2 * j + i])
            )
    for copy in copies:
        copy.start()
    for j in range(PIECES):
        part = pl.ds(j * size, size)
        unit = []
        for i in range(2):
            copies[2 * j + i].wait()
            values = raw[i, part].astype(jnp.float32)
            unit.append((values * inv_norm(values)).astype(jnp.bfloat16))

        @pl.when(odd[0] == 0)
        def _():
            p[part] = unit[0]
            q[part] = unit[1]

        @pl.when(odd[0] == 1)
        def _():
            p[part] = unit[1]
            q[part] = unit[0]


def terms(x, ys, scale, shift, positive=None):
    total = None
    for j, y in enumerate(ys):
        g = lax.logistic(scale * dot(x, y, NT) + shift)
        if positive is not None:
            u, v = positive
            g = g - (u == v[j]).astype(jnp.float32)
        term = dot((scale * g).astype(jnp.bfloat16), y, NN)
        total = term if total is None else total + term
    return total


def first_body(scale, shift, p, q, u_p, v_p, u_q, v_q, sum_p, sum_q, again, pq):
    rows = p.shape[0]
    x, y = p[...], q[...]
    again[...] = x
    pq[:rows] = x
    pq[rows:] = y
    sum_p[...] = terms(x, [y], scale[0], shift[0], (u_p[...], [v_p[:1]]))
    sum_q[...] = terms(y, [x], scale[0], shift[0], (u_q[...], [v_q[:1]]))


def join_body(x2, y0, xy):
    rows = x2.shape[0]
    xy[:rows] = x2[...]
    xy[rows:] = y0[...]


def near_body(scale, shift, p, q, pq_c, xy, u_p, v_p, u_q, v_q, own_p, own_q, sum_p, sum_q):
    rows = p.shape[0]
    x_c, y_c, x2 = pq_c[:rows], pq_c[rows:], xy[:rows]
    sum_p[...] = own_p[...] + terms(p[...], [y_c], scale[0], shift[0], (u_p[...], [v_p[1:2]]))
    own = (u_q[...], [v_q[1:2], v_q[2:3]])
    sum_q[...] = own_q[...] + terms(q[...], [x_c, x2], scale[0], shift[0], own)


def pair_body(y1, w2, _sum, yw):
    rows = y1.shape[0]
    yw[:rows] = y1[...]
    yw[rows:] = w2[...]


def mid_body(scale, shift, xy, xy_c, y1, part):
    rows = y1.shape[0]
    ys = [xy[rows:], xy_c[rows:], y1[...]]
    part[...] = terms(xy[:rows], ys, scale[0], shift[0])


def late_body(scale, shift, x2, yw_c, part, out):
    rows = x2.shape[0]
    out[...] = (part[...] + terms(x2[...], [yw_c[:rows]], scale[0], shift[0])).astype(out.dtype)


def tangent(raw, dunit):
    values = raw.astype(jnp.float32)
    inv = inv_norm(values)
    unit = values * inv
    return (dunit - unit * jnp.sum(unit * dunit, axis=-1, keepdims=True)) * inv


def write_out(is_txt, img, txt, dunit, img_grad, txt_grad, held, sems):
    rows = img.shape[0]
    size = rows // PIECES

    def go(raw, grad):
        copies = []
        for j in range(PIECES):
            part = pl.ds(j * size, size)
            held[part] = tangent(raw[part], dunit(part))
            copies.append(pltpu.make_async_copy(held.at[part], grad.at[part], sems.at[j]))
            copies[-1].start()
        for copy in copies:
            copy.wait()

    @pl.when(jnp.logical_not(is_txt))
    def _():
        go(img, img_grad)

    @pl.when(is_txt)
    def _():
        go(txt, txt_grad)


def rest_body(
    scale, shift, odd, img, txt, p, q, xy, xy_c, yw, yw_c, u_p, v_p, u_q, v_q, own_p, own_q,
    sum_q, img_grad, txt_grad, total, held, sems
):
    rows = p.shape[0]
    x = p[...]
    own = (u_q[...], [v_q[3:]])
    sum_q[...] = own_q[...] + terms(q[...], [xy_c[:rows]], scale[0], shift[0], own)
    own = (u_p[...], [v_p[2:3], v_p[3:]])
    visiting = [xy[rows:], xy_c[rows:], yw[:rows], yw_c[:rows]]
    total[...] = (
        own_p[...]
        + terms(x, visiting, scale[0], shift[0])
        + terms(x, [yw[rows:], yw_c[rows:]], scale[0], shift[0], own)
    )
    write_out(odd[0] == 1, img, txt, lambda part: total[part], img_grad, txt_grad, held, sems)


def last_body(odd, img, txt, sum_q, back, _img, _txt, img_grad, txt_grad, held, sems):
    def dunit(part):
        return sum_q[part] + back[part].astype(jnp.float32)

    write_out(odd[0] == 0, img, txt, dunit, img_grad, txt_grad, held, sems)


def local(picture_vectors, caption_vectors, caption_position, sharpness_factor, affine_offset):
    groups = lax.axis_size("loop")
    rows, depth = picture_vectors.shape
    img, txt, scale, shift = picture_vectors, caption_vectors, sharpness_factor, affine_offset

    def swap(to):
        pairs = []
        for g in range(groups):
            for n in range(4):
                h, m = to(g, n)
                pairs.append((g * 4 + n, (h % groups) * 4 + m))
        return lambda x: lax.ppermute(x, AXES, pairs)

    core = swap(lambda g, n: (g, n ^ 1))
    chip = swap(lambda g, n: (g, n ^ 2))
    group = swap(lambda g, n: (g + 1, n - 2) if n >= 2 else (g - 1, n + 2))

    here = lax.axis_index("narrow")
    odd = here // 2
    odd1 = odd.reshape(1).astype(jnp.int32)
    block = jax.ShapeDtypeStruct((rows, depth), jnp.bfloat16)
    wide = jax.ShapeDtypeStruct((rows, depth), jnp.float32)
    both = jax.ShapeDtypeStruct((2 * rows, depth), jnp.bfloat16)

    dma = pltpu.SemaphoreType.DMA
    far = lambda x: pltpu.with_memory_space_constraint(x, pltpu.HBM)
    p, q = call(
        unit_body,
        (block, block),
        [SMEM, HBM, HBM],
        scratch_shapes=[pltpu.VMEM((2, rows, depth), jnp.bfloat16), dma((2 * PIECES,))],
    )(odd1, far(img), far(txt))
    x2 = chip(q)
    y0 = group(p)

    order = here ^ jnp.arange(4, dtype=jnp.int32)
    matches = caption_position.reshape(4, rows)[order]
    places = order[:, None] * rows + jnp.arange(rows, dtype=jnp.int32)[None, :]
    is_odd = odd == 1
    u_p = jnp.where(is_odd, places[0], matches[0])[:, None]
    u_q = jnp.where(is_odd, matches[0], places[0])[:, None]
    v_p = jnp.where(is_odd, matches, places)
    v_q = jnp.where(is_odd, places, matches)

    sums = (wide, wide)
    match = (u_p, v_p, u_q, v_q)
    sum_p, sum_q, again, pq = call(first_body, sums + (block, both), [SMEM] * 2 + [VMEM] * 6)(
        scale, shift, p, q, *match
    )
    pq_c = core(pq)
    w2 = chip(again)
    y1 = group(x2)
    xy = call(join_body, both, [VMEM] * 2, flops=JOIN)(x2, y0)
    xy_c = core(xy)
    sum_p, sum_q = call(near_body, sums, [SMEM] * 2 + [VMEM] * 10)(
        scale, shift, p, q, pq_c, xy, *match, sum_p, sum_q
    )
    yw = call(pair_body, both, [VMEM] * 3)(y1, w2, sum_q)
    yw_c = core(yw)
    part = call(mid_body, wide, [SMEM] * 2 + [VMEM] * 3)(scale, shift, xy, xy_c, y1)
    send = call(late_body, block, [SMEM] * 2 + [VMEM] * 3)(scale, shift, x2, yw_c, part)
    back = chip(send)
    out = [pltpu.VMEM((rows, depth), jnp.float32), dma((PIECES,))]
    sum_q, *grads = call(
        rest_body,
        (wide,) * 3,
        [SMEM] * 3 + [VMEM] * 14,
        (VMEM, HBM, HBM),
        scratch_shapes=[pltpu.VMEM((rows, depth), jnp.float32)] + out,
    )(scale, shift, odd1, img, txt, p, q, xy, xy_c, yw, yw_c, *match, sum_p, sum_q)
    return call(
        last_body,
        (wide, wide),
        [SMEM] + [VMEM] * 4 + [HBM] * 2,
        (HBM, HBM),
        scratch_shapes=out,
        input_output_aliases={5: 0, 6: 1},
    )(odd1, img, txt, sum_q, back, *grads)


def solution(mesh):
    return jax.shard_map(
        local,
        mesh=mesh,
        in_specs=(
            P(AXES, None),
            P(AXES, None),
            P("loop", None),
            P(),
            P(),
        ),
        out_specs=(P(AXES, None), P(AXES, None)),
        check_vma=False,
    )
```

time: 82.1 us -> 73.8 us (0.90)
  waiting for transfers between devices: 7.62 us -> 21.9 us
  starting transfers between devices: 48.8 us -> 34.9 us
  local copies, waits for them, and re-layouts: 6.01 us -> 1.57 us
  Pallas kernels: 16.6 us -> 12.8 us
    ppermute x10 -> x8, waiting for transfers between devices: 7.62 us -> 21.9 us  [swap(): return lambda x: lax.ppermute(x, AXES, pairs)]
    ppermute x10 -> x8, starting transfers between devices: 48.8 us -> 34.9 us  [swap(): return lambda x: lax.ppermute(x, AXES, pairs)]
    unnamed x20 -> x6, local copies, waits for them, and re-layouts: 5.11 us -> 0.67 us
    pallas_call x6 -> x9, Pallas kernels: 16.6 us -> 12.8 us  [the longest x1 4.43 us: local(): call(rest_body, (wide,) * 3, [SMEM] * 3 + [VMEM] * 14, (VMEM, HBM, HBM),...]
  transfers between devices with their start and end apart: 10 -> 8, of which waited for: 2 -> 4; matrix products, arithmetic and copies ran while one was open for 1% -> 1% of each run, Pallas kernels for 15% -> 12%
where the time goes in v2:
time: 73.8 us; the launch traced here: 73.5 us
  starting transfers between devices  34.9 us (47%)
  waiting for transfers between devices  21.9 us (30%)
  Pallas kernels  12.8 us (17%)
  between operations  2.19 us (3%)
  local copies, waits for them, and re-layouts  1.57 us (2%)
    ppermute x8, starting transfers between devices, swap(): return lambda x: lax.ppermute(x, AXES, pairs)  34.9 us
    ppermute x8, waiting for transfers between devices, swap(): return lambda x: lax.ppermute(x, AXES, pairs)  21.9 us
    pallas_call x1, Pallas kernels, local(): call(rest_body, (wide,) * 3, [SMEM] * 3 + [VMEM] * 14, (VMEM, HBM, HBM),...  4.43 us
    pallas_call x1, Pallas kernels, local(): call(unit_body, (block, block), [SMEM, HBM, HBM], scratch_shapes=[pltpu.V...  1.65 us
    pallas_call x1, Pallas kernels, local(): call(first_body, sums + (block, both), [SMEM] * 2 + [VMEM] * 6)  1.49 us
    pallas_call x1, Pallas kernels, local(): call(near_body, sums, [SMEM] * 2 + [VMEM] * 10)  1.48 us
  transfers between devices with their start and end apart: 8, of which 4 were waited for; matrix products, arithmetic and copies ran while one was open for 1% of the time, Pallas kernels for 12%

profile of v2, /device:TPU:1, one launch (start us, length us, event | category | flops | bytes accessed | tf_op | source)
XLA Modules:
  0.0 73.5 jit_solution(15547871173566930206)
XLA Ops:
  0.6 1.6 %shard_map.68 = (bf16[224,1152]{1,0:T(8,128)(2,1)S(1)}, bf16[224,1152]{1,0:T(8,128)(2,1)S(1)}) custom-call(s32[1]{0:T(128)} %bitcast.odd, bf16[224,1152]{1,0:T(8,128)(2,1)} %img.5, bf16[224,1152]{1,0:T(8,128)(2,1)} %txt.5), custom_call_target="tpu_custom_call" | custom-call | flops 1 | bytes 1 | tf_op jit(solution)/shard_map/pallas_call | solution.py:207
  2.3 4.8 %collective-permute-start = (bf16[224,1152]{1,0:T(8,128)(2,1)S(1)}, bf16[224,1152]{1,0:T(8,128)(2,1)S(1)}, u32[]{:S(2)}, u32[]{:S(2)}) collective-permute-start(bf16[224,1152]{1,0:T(8,128)(2,1)S(1)} %get-tuple-element.14.q), channel_id=1, source_target_pairs={{0,2},{1,3},{2,0},{3,1},{4,6},{5,7},{6,4},{7,5},{8,10},{9,11},{10,... | collective-permute-start | bytes 1548296 | tf_op jit(solution)/shard_map/ppermute | solution.py:192
  7.1 14.0 %collective-permute-start.1 = (bf16[224,1152]{1,0:T(8,128)(2,1)S(1)}, bf16[224,1152]{1,0:T(8,128)(2,1)S(1)}, u32[]{:S(2)}, u32[]{:S(2)}) collective-permute-start(bf16[224,1152]{1,0:T(8,128)(2,1)S(1)} %get-tuple-element.13.p), channel_id=1, source_target_pairs={{0,510},{1,511},{2,4},{3,5},{4,2},{5,3},{6,8},{7,9},{8,6},{9,7},{1... | collective-permute-start | bytes 1548296 | tf_op jit(solution)/shard_map/ppermute | solution.py:192
  21.1 0.0 copy-start.2
  21.1 0.7 copy-done.2
  21.8 0.1 reshape.69
  21.9 0.6 gather_fusion
  22.5 0.1 fusion
  22.5 0.1 copy.10.u_q
  22.7 0.1 copy.9.u_p
  24.1 1.5 %shard_map.70 = (f32[224,1152]{1,0:T(8,128)S(1)}, f32[224,1152]{1,0:T(8,128)S(1)}, bf16[224,1152]{1,0:T(8,128)(2,1)S(1)}, bf16[448,1152]{1,0:T(8,128)(2,1)S(1)}) custom-call(f32[1]{0:T(128)S(6)} %copy.17.scale, f32[1]{0:T(128)S(6)} %copy.18.shift, bf16[224,1152]{1,0:T(8,128)(2,1)S(1)} %get-tuple-element.13.p, bf16[224,1152]{1,0:T(8,128)(2,1)S(1)} %get-tuple-element.14.q, ...), custom_call_target="tpu_custom_call" | custom-call | flops 1 | bytes 1 | tf_op jit(solution)/shard_map/pallas_call | solution.py:227
  25.6 3.1 %collective-permute-start.5 = (bf16[448,1152]{1,0:T(8,128)(2,1)S(1)}, bf16[448,1152]{1,0:T(8,128)(2,1)S(1)}, u32[]{:S(2)}, u32[]{:S(2)}) collective-permute-start(bf16[448,1152]{1,0:T(8,128)(2,1)S(1)} %get-tuple-element.16), channel_id=1, source_target_pairs={{0,1},{1,0},{2,3},{3,2},{4,5},{5,4},{6,7},{7,6},{8,9},{9,8},{10,11... | collective-permute-start | bytes 3096584 | tf_op jit(solution)/shard_map/ppermute | solution.py:192
  28.8 1.9 %collective-permute-start.4 = (bf16[224,1152]{1,0:T(8,128)(2,1)S(1)}, bf16[224,1152]{1,0:T(8,128)(2,1)S(1)}, u32[]{:S(2)}, u32[]{:S(2)}) collective-permute-start(bf16[224,1152]{1,0:T(8,128)(2,1)S(1)} %get-tuple-element.15), channel_id=1, source_target_pairs={{0,2},{1,3},{2,0},{3,1},{4,6},{5,7},{6,4},{7,5},{8,10},{9,11},{10,... | collective-permute-start | bytes 1548296 | tf_op jit(solution)/shard_map/ppermute | solution.py:192
  30.7 0.0 collective-permute-done.x2
  30.7 2.8 %collective-permute-start.3 = (bf16[224,1152]{1,0:T(8,128)(2,1)S(1)}, bf16[224,1152]{1,0:T(8,128)(2,1)S(1)}, u32[]{:S(2)}, u32[]{:S(2)}) collective-permute-start(bf16[224,1152]{1,0:T(8,128)(2,1)S(1)} %collective-permute-done.x2), channel_id=1, source_target_pairs={{0,510},{1,511},{2,4},{3,5},{4,2},{5,3},{6,8},{7,9},{8,6},{9,7},{1... | collective-permute-start | bytes 1548296 | tf_op jit(solution)/shard_map/ppermute | solution.py:192
  33.5 0.0 collective-permute-done.1.y0
  33.5 0.1 shard_map.69.xy
  33.6 3.6 %collective-permute-start.2 = (bf16[448,1152]{1,0:T(8,128)(2,1)S(1)}, bf16[448,1152]{1,0:T(8,128)(2,1)S(1)}, u32[]{:S(2)}, u32[]{:S(2)}) collective-permute-start(bf16[448,1152]{1,0:T(8,128)(2,1)S(1)} %shard_map.69.xy), channel_id=1, source_target_pairs={{0,1},{1,0},{2,3},{3,2},{4,5},{5,4},{6,7},{7,6},{8,9},{9,8},{10,11... | collective-permute-start | bytes 3096584 | tf_op jit(solution)/shard_map/ppermute | solution.py:192
  37.2 0.0 collective-permute-done.5.pq_c
  37.2 1.5 %shard_map.71 = (f32[224,1152]{1,0:T(8,128)S(1)}, f32[224,1152]{1,0:T(8,128)S(1)}) custom-call(f32[1]{0:T(128)S(6)} %copy.17.scale, f32[1]{0:T(128)S(6)} %copy.18.shift, bf16[224,1152]{1,0:T(8,128)(2,1)S(1)} %get-tuple-element.13.p, bf16[224,1152]{1,0:T(8,128)(2,1)S(1)} %get-tuple-element.14.q, bf16[448,1152]{1,0:T(8,128)(2,1)S(1)} %collective-permute-done.5.pq_c, ...), custom_call_target="tpu_custom_call" | custom-call | flops 1 | bytes 1 | tf_op jit(solution)/shard_map/pallas_call | solution.py:235
  38.7 5.3 %collective-permute-done.4.w2 = bf16[224,1152]{1,0:T(8,128)(2,1)S(1)} collective-permute-done((bf16[224,1152]{1,0:T(8,128)(2,1)S(1)}, bf16[224,1152]{1,0:T(8,128)(2,1)S(1)}, u32[]{:S(2)}, u32[]{:S(2)}) %collective-permute-start.4) | collective-permute-done | bytes 516128 | tf_op jit(solution)/shard_map/ppermute | solution.py:192
  44.0 7.4 %collective-permute-done.3.y1 = bf16[224,1152]{1,0:T(8,128)(2,1)S(1)} collective-permute-done((bf16[224,1152]{1,0:T(8,128)(2,1)S(1)}, bf16[224,1152]{1,0:T(8,128)(2,1)S(1)}, u32[]{:S(2)}, u32[]{:S(2)}) %collective-permute-start.3) | collective-permute-done | bytes 516128 | tf_op jit(solution)/shard_map/ppermute | solution.py:192
  51.4 0.1 shard_map.72.yw
  51.5 2.7 %collective-permute-start.6 = (bf16[448,1152]{1,0:T(8,128)(2,1)S(1)}, bf16[448,1152]{1,0:T(8,128)(2,1)S(1)}, u32[]{:S(2)}, u32[]{:S(2)}) collective-permute-start(bf16[448,1152]{1,0:T(8,128)(2,1)S(1)} %shard_map.72.yw), channel_id=1, source_target_pairs={{0,1},{1,0},{2,3},{3,2},{4,5},{5,4},{6,7},{7,6},{8,9},{9,8},{10,11... | collective-permute-start | bytes 3096584 | tf_op jit(solution)/shard_map/ppermute | solution.py:192
  54.2 0.0 collective-permute-done.2.xy_c
  54.2 1.4 %shard_map.74.part = f32[224,1152]{1,0:T(8,128)S(1)} custom-call(f32[1]{0:T(128)S(6)} %copy.17.scale, f32[1]{0:T(128)S(6)} %copy.18.shift, bf16[448,1152]{1,0:T(8,128)(2,1)S(1)} %shard_map.69.xy, bf16[448,1152]{1,0:T(8,128)(2,1)S(1)} %collective-permute-done.2.xy_c, bf16[224,1152]{1,0:T(8,128)(2,1)S(1)} %collective-permute-done.3.y1), custom_call_target="tpu_custom_call" | custom-call | flops 1 | bytes 1 | tf_op jit(solution)/shard_map/pallas_call | solution.py:240
  55.6 0.0 copy-start
  55.6 0.0 copy-start.1
  55.7 0.8 %collective-permute-done.6.yw_c = bf16[448,1152]{1,0:T(8,128)(2,1)S(1)} collective-permute-done((bf16[448,1152]{1,0:T(8,128)(2,1)S(1)}, bf16[448,1152]{1,0:T(8,128)(2,1)S(1)}, u32[]{:S(2)}, u32[]{:S(2)}) %collective-permute-start.6) | collective-permute-done | bytes 1032224 | tf_op jit(solution)/shard_map/ppermute | solution.py:192
  56.4 0.8 %shard_map.75 = bf16[224,1152]{1,0:T(8,128)(2,1)S(1)} custom-call(f32[1]{0:T(128)S(6)} %copy.17.scale, f32[1]{0:T(128)S(6)} %copy.18.shift, bf16[224,1152]{1,0:T(8,128)(2,1)S(1)} %collective-permute-done.x2, bf16[448,1152]{1,0:T(8,128)(2,1)S(1)} %collective-permute-done.6.yw_c, f32[224,1152]{1,0:T(8,128)S(1)} %shard_map.74.part), custom_call_target="tpu_custom_call" | custom-call | flops 1 | bytes 1 | tf_op jit(solution)/shard_map/pallas_call | solution.py:241
  57.3 1.9 %collective-permute-start.7 = (bf16[224,1152]{1,0:T(8,128)(2,1)S(1)}, bf16[224,1152]{1,0:T(8,128)(2,1)S(1)}, u32[]{:S(2)}, u32[]{:S(2)}) collective-permute-start(bf16[224,1152]{1,0:T(8,128)(2,1)S(1)} %shard_map.75), channel_id=1, source_target_pairs={{0,2},{1,3},{2,0},{3,1},{4,6},{5,7},{6,4},{7,5},{8,10},{9,11},{10,... | collective-permute-start | bytes 1548296 | tf_op jit(solution)/shard_map/ppermute | solution.py:192
  59.2 0.0 copy-done
  59.2 0.0 copy-done.1
  59.2 4.4 %shard_map.73 = (f32[224,1152]{1,0:T(8,128)S(1)}, f32[224,1152]{1,0:T(8,128)}, f32[224,1152]{1,0:T(8,128)}) custom-call(f32[1]{0:T(128)S(6)} %copy.17.scale, f32[1]{0:T(128)S(6)} %copy.18.shift, s32[1]{0:T(128)} %bitcast.odd, bf16[224,1152]{1,0:T(8,128)(2,1)S(1)} %copy-done, bf16[224,1152]{1,0:T(8,128)(2,1)S(1)} %copy-done.1, ...), custom_call_target="tpu_custom_call" | custom-call | flops 1 | bytes 1 | tf_op jit(solution)/shard_map/pallas_call | solution.py:244
  63.7 8.5 %collective-permute-done.7.back = bf16[224,1152]{1,0:T(8,128)(2,1)S(1)} collective-permute-done((bf16[224,1152]{1,0:T(8,128)(2,1)S(1)}, bf16[224,1152]{1,0:T(8,128)(2,1)S(1)}, u32[]{:S(2)}, u32[]{:S(2)}) %collective-permute-start.7) | collective-permute-done | bytes 516128 | tf_op jit(solution)/shard_map/ppermute | solution.py:192
  72.1 1.3 %shard_map.76 = (f32[224,1152]{1,0:T(8,128)}, f32[224,1152]{1,0:T(8,128)}) custom-call(s32[1]{0:T(128)} %bitcast.odd, bf16[224,1152]{1,0:T(8,128)(2,1)S(1)} %copy-done, bf16[224,1152]{1,0:T(8,128)(2,1)S(1)} %copy-done.1, f32[224,1152]{1,0:T(8,128)S(1)} %get-tuple-element.21.sum_q, ...), custom_call_target="tpu_custom_call", output_to_operand_aliasing={{0}: (5, {}), {1}: (6, {})} | custom-call | flops 1 | bytes 1 | tf_op jit(solution)/shard_map/pallas_call | solution.py:251
  (5 shorter events, 0.0 us)
Async XLA Ops:
  2.3 28.4 %collective-permute-start = (bf16[224,1152]{1,0:T(8,128)(2,1)S(1)}, bf16[224,1152]{1,0:T(8,128)(2,1)S(1)}, u32[]{:S(2)}, u32[]{:S(2)}) collective-permute-start(bf16[224,1152]{1,0:T(8,128)(2,1)S(1)} %get-tuple-element.14.q), channel_id=1, source_target_pairs={{0,2},{1,3},{2,0},{3,1},{4,6},{5,7},{6,4},{7,5},{8,10},{9,11},{10,... | collective-permute-start | bytes 1548296 | tf_op jit(solution)/shard_map/ppermute | solution.py:192
  7.1 26.4 %collective-permute-start.1 = (bf16[224,1152]{1,0:T(8,128)(2,1)S(1)}, bf16[224,1152]{1,0:T(8,128)(2,1)S(1)}, u32[]{:S(2)}, u32[]{:S(2)}) collective-permute-start(bf16[224,1152]{1,0:T(8,128)(2,1)S(1)} %get-tuple-element.13.p), channel_id=1, source_target_pairs={{0,510},{1,511},{2,4},{3,5},{4,2},{5,3},{6,8},{7,9},{8,6},{9,7},{1... | collective-permute-start | bytes 1548296 | tf_op jit(solution)/shard_map/ppermute | solution.py:192
  21.1 0.7 copy-start.2
  25.6 11.6 %collective-permute-start.5 = (bf16[448,1152]{1,0:T(8,128)(2,1)S(1)}, bf16[448,1152]{1,0:T(8,128)(2,1)S(1)}, u32[]{:S(2)}, u32[]{:S(2)}) collective-permute-start(bf16[448,1152]{1,0:T(8,128)(2,1)S(1)} %get-tuple-element.16), channel_id=1, source_target_pairs={{0,1},{1,0},{2,3},{3,2},{4,5},{5,4},{6,7},{7,6},{8,9},{9,8},{10,11... | collective-permute-start | bytes 3096584 | tf_op jit(solution)/shard_map/ppermute | solution.py:192
  28.8 15.3 %collective-permute-start.4 = (bf16[224,1152]{1,0:T(8,128)(2,1)S(1)}, bf16[224,1152]{1,0:T(8,128)(2,1)S(1)}, u32[]{:S(2)}, u32[]{:S(2)}) collective-permute-start(bf16[224,1152]{1,0:T(8,128)(2,1)S(1)} %get-tuple-element.15), channel_id=1, source_target_pairs={{0,2},{1,3},{2,0},{3,1},{4,6},{5,7},{6,4},{7,5},{8,10},{9,11},{10,... | collective-permute-start | bytes 1548296 | tf_op jit(solution)/shard_map/ppermute | solution.py:192
  30.7 20.7 %collective-permute-start.3 = (bf16[224,1152]{1,0:T(8,128)(2,1)S(1)}, bf16[224,1152]{1,0:T(8,128)(2,1)S(1)}, u32[]{:S(2)}, u32[]{:S(2)}) collective-permute-start(bf16[224,1152]{1,0:T(8,128)(2,1)S(1)} %collective-permute-done.x2), channel_id=1, source_target_pairs={{0,510},{1,511},{2,4},{3,5},{4,2},{5,3},{6,8},{7,9},{8,6},{9,7},{1... | collective-permute-start | bytes 1548296 | tf_op jit(solution)/shard_map/ppermute | solution.py:192
  33.6 20.6 %collective-permute-start.2 = (bf16[448,1152]{1,0:T(8,128)(2,1)S(1)}, bf16[448,1152]{1,0:T(8,128)(2,1)S(1)}, u32[]{:S(2)}, u32[]{:S(2)}) collective-permute-start(bf16[448,1152]{1,0:T(8,128)(2,1)S(1)} %shard_map.69.xy), channel_id=1, source_target_pairs={{0,1},{1,0},{2,3},{3,2},{4,5},{5,4},{6,7},{7,6},{8,9},{9,8},{10,11... | collective-permute-start | bytes 3096584 | tf_op jit(solution)/shard_map/ppermute | solution.py:192
  51.5 5.0 %collective-permute-start.6 = (bf16[448,1152]{1,0:T(8,128)(2,1)S(1)}, bf16[448,1152]{1,0:T(8,128)(2,1)S(1)}, u32[]{:S(2)}, u32[]{:S(2)}) collective-permute-start(bf16[448,1152]{1,0:T(8,128)(2,1)S(1)} %shard_map.72.yw), channel_id=1, source_target_pairs={{0,1},{1,0},{2,3},{3,2},{4,5},{5,4},{6,7},{7,6},{8,9},{9,8},{10,11... | collective-permute-start | bytes 3096584 | tf_op jit(solution)/shard_map/ppermute | solution.py:192
  55.6 3.6 %copy-start = (bf16[224,1152]{1,0:T(8,128)(2,1)S(1)}, bf16[224,1152]{1,0:T(8,128)(2,1)}, u32[]{:S(2)}) copy-start(bf16[224,1152]{1,0:T(8,128)(2,1)} %img.5) | copy-start | bytes 1548292
  55.6 3.6 %copy-start.1 = (bf16[224,1152]{1,0:T(8,128)(2,1)S(1)}, bf16[224,1152]{1,0:T(8,128)(2,1)}, u32[]{:S(2)}) copy-start(bf16[224,1152]{1,0:T(8,128)(2,1)} %txt.5) | copy-start | bytes 1548292
  57.3 14.9 %collective-permute-start.7 = (bf16[224,1152]{1,0:T(8,128)(2,1)S(1)}, bf16[224,1152]{1,0:T(8,128)(2,1)S(1)}, u32[]{:S(2)}, u32[]{:S(2)}) collective-permute-start(bf16[224,1152]{1,0:T(8,128)(2,1)S(1)} %shard_map.75), channel_id=1, source_target_pairs={{0,2},{1,3},{2,0},{3,1},{4,6},{5,7},{6,4},{7,5},{8,10},{9,11},{10,... | collective-permute-start | bytes 1548296 | tf_op jit(solution)/shard_map/ppermute | solution.py:192

commit v3 on v2

v3 whole, which is shorter than its diff:
```python
import jax
import jax.numpy as jnp
from jax import lax
from jax.experimental import pallas as pl
from jax.experimental.pallas import tpu as pltpu
from jax.sharding import PartitionSpec as P

AXES = ("loop", "narrow")
VMEM = pl.BlockSpec(memory_space=pltpu.VMEM)
SMEM = pl.BlockSpec(memory_space=pltpu.SMEM)
HBM = pl.BlockSpec(memory_space=pltpu.HBM)
NT = (((1,), (1,)), ((), ()))
NN = (((1,), (0,)), ((), ()))
PIECES = 2
COST = {"pair": 32 * 10**9, "mid": 8 * 10**9, "late": 64 * 10**9, "visit": 32 * 10**9, "last": 4 * 10**9}


def inv_norm(values):
    return lax.rsqrt(jnp.sum(values * values, axis=-1, keepdims=True) + 1e-06)


def dot(a, b, dims):
    return lax.dot_general(a, b, dims, preferred_element_type=jnp.float32)


def call(body, out_shape, in_specs, out_specs=None, vmem=6, **kwargs):
    if out_specs is None:
        out_specs = jax.tree.map(lambda _: VMEM, out_shape)
    name = body.__name__.removesuffix("_body")
    return pl.pallas_call(
        body,
        name=name,
        out_shape=out_shape,
        in_specs=in_specs,
        out_specs=out_specs,
        compiler_params=pltpu.CompilerParams(vmem_limit_bytes=vmem * 1024 * 1024),
        cost_estimate=pl.CostEstimate(flops=COST.get(name, 1), bytes_accessed=1, transcendentals=0),
        **kwargs,
    )


def unit_body(odd, img, txt, p, q_lo, q_hi, raw, sems):
    rows = img.shape[0]
    size = rows // PIECES
    half = rows // 2
    copies = []
    for j in range(PIECES):
        part = pl.ds(j * size, size)
        for i, ref in enumerate((img, txt)):
            copies.append(
                pltpu.make_async_copy(ref.at[part], raw.at[i, part], sems.at[2 * j + i])
            )
    for copy in copies:
        copy.start()
    for j in range(PIECES):
        part = pl.ds(j * size, size)
        unit = []
        for i in range(2):
            copies[2 * j + i].wait()
            values = raw[i, part].astype(jnp.float32)
            unit.append((values * inv_norm(values)).astype(jnp.bfloat16))
        q, start = (q_lo, j * size) if j * size < half else (q_hi, j * size - half)

        def put(first, second):
            p[part] = first
            q[pl.ds(start, size)] = second

        @pl.when(odd[0] == 0)
        def _():
            put(unit[0], unit[1])

        @pl.when(odd[0] == 1)
        def _():
            put(unit[1], unit[0])


def match_body(here, scale, shift, pos, sc, u_p, v_p, u_q, v_q):
    rows = u_p.shape[0]
    sc[0:1] = jnp.full((1, sc.shape[1]), scale[0], jnp.float32)
    sc[1:2] = jnp.full((1, sc.shape[1]), shift[0], jnp.float32)
    me = here[0]
    lane = lax.broadcasted_iota(jnp.int32, (1, rows), 1)
    square = (rows, rows)
    diagonal = lax.broadcasted_iota(jnp.int32, square, 0) == lax.broadcasted_iota(
        jnp.int32, square, 1
    )

    def column(row):
        spread = jnp.where(diagonal, jnp.broadcast_to(row, square).astype(jnp.float32), 0.0)
        return jnp.sum(spread, axis=1, keepdims=True).astype(jnp.int32)

    matches, places = [], []
    for j in range(4):
        block = me ^ j
        matches.append(pos[pl.ds(block, 1)])
        places.append(block * rows + lane)

    def put(u_img, v_img, u_txt, v_txt):
        u_img[...] = column(matches[0])
        u_txt[...] = column(places[0])
        for j in range(4):
            v_img[j : j + 1] = places[j]
            v_txt[j : j + 1] = matches[j]

    @pl.when(me < 2)
    def _():
        put(u_p, v_p, u_q, v_q)

    @pl.when(me >= 2)
    def _():
        put(u_q, v_q, u_p, v_p)


def terms(x, ys, sc, positive=None):
    scale, shift = sc[0:1, 0:1], sc[1:2, 0:1]
    total = None
    for j, y in enumerate(ys):
        g = lax.logistic(scale * dot(x, y, NT) + shift)
        if positive is not None:
            u, v = positive
            g = g - (u == v[j]).astype(jnp.float32)
        term = dot((scale * g).astype(jnp.bfloat16), y, NN)
        total = term if total is None else total + term
    return total


def join_body(p, q_lo, q_hi, x2_lo, x2_hi, y0, out):
    row = 0
    for part in (p, q_lo, q_hi, x2_lo, x2_hi, y0):
        out[pl.ds(row, part.shape[0])] = part[...]
        row += part.shape[0]


def pair_body(y_lo, y_hi, _w2, y1):
    half = y_lo.shape[0]
    y1[:half] = y_lo[...]
    y1[half:] = y_hi[...]


def block(ref, j):
    rows = ref.shape[0] // 4
    return ref[j * rows : (j + 1) * rows]


def mid_body(sc, near, near_c, y1, part):
    part[...] = terms(block(near, 2), [block(near, 3), block(near_c, 3), y1[...]], sc)


def late_body(sc, near, y1_c, part, out):
    out[...] = (part[...] + terms(block(near, 2), [y1_c[...]], sc)).astype(out.dtype)


def tangent(raw, dunit):
    values = raw.astype(jnp.float32)
    inv = inv_norm(values)
    unit = values * inv
    return (dunit - unit * jnp.sum(unit * dunit, axis=-1, keepdims=True)) * inv


def write_out(is_txt, img, txt, dunit, img_grad, txt_grad, held, sems):
    rows = img.shape[0]
    size = rows // PIECES

    def go(raw, grad):
        copies = []
        for j in range(PIECES):
            part = pl.ds(j * size, size)
            held[part] = tangent(raw[part], dunit(part))
            copies.append(pltpu.make_async_copy(held.at[part], grad.at[part], sems.at[j]))
            copies[-1].start()
        for copy in copies:
            copy.wait()

    @pl.when(jnp.logical_not(is_txt))
    def _():
        go(img, img_grad)

    @pl.when(is_txt)
    def _():
        go(txt, txt_grad)


def visit_body(
    sc, near, near_c, y1, y1_c, w2, _send, u_p, v_p, u_q, v_q, sum_p, sum_q, w2_lo, w2_hi
):
    half = w2_lo.shape[0]
    w2_lo[...] = w2[:half]
    w2_hi[...] = w2[half:]
    x, y, x2, y0 = (block(near, j) for j in range(4))
    x_c, y_c, x2_c, y0_c = (block(near_c, j) for j in range(4))
    columns = [v_p[j : j + 1] for j in range(3)]
    sum_p[...] = terms(x, [y, y_c, w2[...]], sc, (u_p[...], columns)) + terms(
        x, [y0, y0_c, y1[...], y1_c[...]], sc
    )
    columns = [v_q[j : j + 1] for j in range(4)]
    sum_q[...] = terms(y, [x, x_c, x2, x2_c], sc, (u_q[...], columns))


def rest_body(
    sc, odd, img, txt, p, w2_lo_c, w2_hi_c, u_p, v_p, sum_p, img_grad, txt_grad, total, held, sems
):
    half = p.shape[0] // 2
    own = (u_p[...], [v_p[3:4, :half], v_p[3:4, half:]])
    total[...] = sum_p[...] + terms(p[...], [w2_lo_c[...], w2_hi_c[...]], sc, own)
    write_out(odd[0] == 1, img, txt, lambda part: total[part], img_grad, txt_grad, held, sems)


def last_body(odd, img, txt, sum_q, back, _img, _txt, img_grad, txt_grad, held, sems):
    def dunit(part):
        return sum_q[part] + back[part].astype(jnp.float32)

    write_out(odd[0] == 0, img, txt, dunit, img_grad, txt_grad, held, sems)


def local(picture_vectors, caption_vectors, caption_position, sharpness_factor, affine_offset):
    groups = lax.axis_size("loop")
    rows, depth = picture_vectors.shape
    half = rows // 2
    img, txt, scale, shift = picture_vectors, caption_vectors, sharpness_factor, affine_offset

    def swap(to):
        pairs = []
        for g in range(groups):
            for n in range(4):
                h, m = to(g, n)
                pairs.append((g * 4 + n, (h % groups) * 4 + m))
        def go(x, name):
            with jax.named_scope(name):
                return lax.ppermute(x, AXES, pairs)

        return go

    core = swap(lambda g, n: (g, n ^ 1))
    chip = swap(lambda g, n: (g, n ^ 2))
    group = swap(lambda g, n: (g + 1, n - 2) if n >= 2 else (g - 1, n + 2))

    def of(shape, dtype=jnp.float32):
        return jax.ShapeDtypeStruct(shape, dtype)

    here = lax.axis_index("narrow").astype(jnp.int32).reshape(1)
    odd = here // 2
    bf16 = jnp.bfloat16
    one, wide = of((rows, depth), bf16), of((rows, depth))
    part, four = of((half, depth), bf16), of((4 * rows, depth), bf16)
    dma = pltpu.SemaphoreType.DMA
    far = lambda x: pltpu.with_memory_space_constraint(x, pltpu.HBM)

    p, q_lo, q_hi = call(
        unit_body,
        (one, part, part),
        [SMEM, HBM, HBM],
        scratch_shapes=[pltpu.VMEM((2, rows, depth), bf16), dma((2 * PIECES,))],
    )(odd, far(img), far(txt))
    y0 = group(p, "group_p")
    x2_lo, x2_hi = chip(q_lo, "chip_lo"), chip(q_hi, "chip_hi")
    w2 = chip(p, "chip_p")
    y_lo, y_hi = group(x2_lo, "group_lo"), group(x2_hi, "group_hi")

    place = (of((rows, 1), jnp.int32), of((4, rows), jnp.int32))
    sc, *match = call(match_body, (of((2, 128)),) + place + place, [SMEM] * 3 + [VMEM])(
        here, scale, shift, caption_position.reshape(4, rows)
    )
    near = call(join_body, four, [VMEM] * 6)(p, q_lo, q_hi, x2_lo, x2_hi, y0)
    near_c = core(near, "core_xy")
    y1 = call(pair_body, one, [VMEM] * 3)(y_lo, y_hi, w2)
    y1_c = core(y1, "core_y")
    part_x = call(mid_body, wide, [VMEM] * 4)(sc, near, near_c, y1)
    send = call(late_body, one, [VMEM] * 4)(sc, near, y1_c, part_x)
    back = chip(send, "chip_send")
    sum_p, sum_q, w2_lo, w2_hi = call(visit_body, (wide, wide, part, part), [VMEM] * 11)(
        sc, near, near_c, y1, y1_c, w2, send, *match
    )
    out = [pltpu.VMEM((rows, depth), jnp.float32), dma((PIECES,))]
    grads = call(
        rest_body,
        (wide, wide),
        [VMEM, SMEM] + [VMEM] * 8,
        (HBM, HBM),
        scratch_shapes=[pltpu.VMEM((rows, depth), jnp.float32)] + out,
    )(sc, odd, img, txt, p, core(w2_lo, "core_w_lo"), core(w2_hi, "core_w_hi"), *match[:2], sum_p)
    return call(
        last_body,
        (wide, wide),
        [SMEM] + [VMEM] * 4 + [HBM] * 2,
        (HBM, HBM),
        scratch_shapes=out,
        input_output_aliases={5: 0, 6: 1},
    )(odd, img, txt, sum_q, back, *grads)


def solution(mesh):
    return jax.shard_map(
        local,
        mesh=mesh,
        in_specs=(
            P(AXES, None),
            P(AXES, None),
            P("loop", None),
            P(),
            P(),
        ),
        out_specs=(P(AXES, None), P(AXES, None)),
        check_vma=False,
    )
```

time: 73.8 us -> 71 us (0.962)
  waiting for transfers between devices: 21.9 us -> 6.28 us
  starting transfers between devices: 34.9 us -> 48.6 us
  local copies, waits for them, and re-layouts: 1.57 us -> 0.09 us
    ppermute x8 -> x11, waiting for transfers between devices: 21.9 us -> 6.28 us  [go(): return lax.ppermute(x, AXES, pairs)]
    ppermute x8 -> x11, starting transfers between devices: 34.9 us -> 48.6 us  [go(): return lax.ppermute(x, AXES, pairs)]
  transfers between devices with their start and end apart: 8 -> 11, of which waited for: 4 -> 5; matrix products, arithmetic and copies ran while one was open for 1% -> 1% of each run, Pallas kernels for 12% -> 13%
where the time goes in v3:
time: 71 us; the launch traced here: 70.6 us
  starting transfers between devices  48.6 us (68%)
  Pallas kernels  12.7 us (18%)
  waiting for transfers between devices  6.28 us (9%)
  between operations  2.13 us (3%)
    ppermute x11, starting transfers between devices, go(): return lax.ppermute(x, AXES, pairs)  48.6 us
    ppermute x11, waiting for transfers between devices, go(): return lax.ppermute(x, AXES, pairs)  6.28 us
    pallas_call x1, Pallas kernels, local(): call(visit_body, (wide, wide, part, part), [VMEM] * 11)  5.02 us
    pallas_call x1, Pallas kernels, local(): call(rest_body, (wide, wide), [VMEM, SMEM] + [VMEM] * 8, (HBM, HBM), scra...  2.11 us
    pallas_call x1, Pallas kernels, local(): call(unit_body, (one, part, part), [SMEM, HBM, HBM], scratch_shapes=[pltp...  1.65 us
    pallas_call x1, Pallas kernels, local(): part_x = call(mid_body, wide, [VMEM] * 4)(sc, near, near_c, y1)  1.43 us
  transfers between devices with their start and end apart: 11, of which 5 were waited for; matrix products, arithmetic and copies ran while one was open for 1% of the time, Pallas kernels for 13%

profile of v3, /device:TPU:1, one launch (start us, length us, event | category | flops | bytes accessed | tf_op | source)
XLA Modules:
  0.0 70.6 jit_solution(6099477471127342279)
XLA Ops:
  0.6 1.6 %unit.1 = (bf16[224,1152]{1,0:T(8,128)(2,1)S(1)}, bf16[112,1152]{1,0:T(8,128)(2,1)S(1)}, bf16[112,1152]{1,0:T(8,128)(2,1)S(1)}) custom-call(s32[1]{0:T(128)S(6)} %select_n.5.odd, bf16[224,1152]{1,0:T(8,128)(2,1)} %img.5, bf16[224,1152]{1,0:T(8,128)(2,1)} %txt.5), custom_call_target="tpu_custom_call" | custom-call | flops 1 | bytes 1 | tf_op jit(solution)/shard_map/unit/pallas_call | solution.py:248
  2.3 16.6 %collective-permute-start.2 = (bf16[224,1152]{1,0:T(8,128)(2,1)S(1)}, bf16[224,1152]{1,0:T(8,128)(2,1)S(1)}, u32[]{:S(2)}, u32[]{:S(2)}) collective-permute-start(bf16[224,1152]{1,0:T(8,128)(2,1)S(1)} %get-tuple-element.17.p), channel_id=1, source_target_pairs={{0,510},{1,511},{2,4},{3,5},{4,2},{5,3},{6,8},{7,9},{8,6},{9,7},{1... | collective-permute-start | bytes 1548296 | tf_op jit(solution)/shard_map/group_p/ppermute | solution.py:229
  18.9 1.9 %collective-permute-start = (bf16[112,1152]{1,0:T(8,128)(2,1)S(1)}, bf16[112,1152]{1,0:T(8,128)(2,1)S(1)}, u32[]{:S(2)}, u32[]{:S(2)}) collective-permute-start(bf16[112,1152]{1,0:T(8,128)(2,1)S(1)} %get-tuple-element.18.q_lo), channel_id=1, source_target_pairs={{0,2},{1,3},{2,0},{3,1},{4,6},{5,7},{6,4},{7,5},{8,10},{9,11},{10,... | collective-permute-start | bytes 774152 | tf_op jit(solution)/shard_map/chip_lo/ppermute | solution.py:229
  20.8 3.4 %collective-permute-start.1 = (bf16[112,1152]{1,0:T(8,128)(2,1)S(1)}, bf16[112,1152]{1,0:T(8,128)(2,1)S(1)}, u32[]{:S(2)}, u32[]{:S(2)}) collective-permute-start(bf16[112,1152]{1,0:T(8,128)(2,1)S(1)} %get-tuple-element.19.q_hi), channel_id=1, source_target_pairs={{0,2},{1,3},{2,0},{3,1},{4,6},{5,7},{6,4},{7,5},{8,10},{9,11},{10,... | collective-permute-start | bytes 774152 | tf_op jit(solution)/shard_map/chip_hi/ppermute | solution.py:229
  24.2 1.9 %collective-permute-start.6 = (bf16[224,1152]{1,0:T(8,128)(2,1)S(1)}, bf16[224,1152]{1,0:T(8,128)(2,1)S(1)}, u32[]{:S(2)}, u32[]{:S(2)}) collective-permute-start(bf16[224,1152]{1,0:T(8,128)(2,1)S(1)} %get-tuple-element.17.p), channel_id=1, source_target_pairs={{0,2},{1,3},{2,0},{3,1},{4,6},{5,7},{6,4},{7,5},{8,10},{9,11},{10,... | collective-permute-start | bytes 1548296 | tf_op jit(solution)/shard_map/chip_p/ppermute | solution.py:229
  26.1 1.4 %collective-permute-done.x2_lo = bf16[112,1152]{1,0:T(8,128)(2,1)S(1)} collective-permute-done((bf16[112,1152]{1,0:T(8,128)(2,1)S(1)}, bf16[112,1152]{1,0:T(8,128)(2,1)S(1)}, u32[]{:S(2)}, u32[]{:S(2)}) %collective-permute-start) | collective-permute-done | bytes 258080 | tf_op jit(solution)/shard_map/chip_lo/ppermute | solution.py:229
  27.6 2.2 %collective-permute-start.4 = (bf16[112,1152]{1,0:T(8,128)(2,1)S(1)}, bf16[112,1152]{1,0:T(8,128)(2,1)S(1)}, u32[]{:S(2)}, u32[]{:S(2)}) collective-permute-start(bf16[112,1152]{1,0:T(8,128)(2,1)S(1)} %collective-permute-done.x2_lo), channel_id=1, source_target_pairs={{0,510},{1,511},{2,4},{3,5},{4,2},{5,3},{6,8},{7,9},{8,6},{9,7},{1... | collective-permute-start | bytes 774152 | tf_op jit(solution)/shard_map/group_lo/ppermute | solution.py:229
  29.8 3.3 %collective-permute-done.1.x2_hi = bf16[112,1152]{1,0:T(8,128)(2,1)S(1)} collective-permute-done((bf16[112,1152]{1,0:T(8,128)(2,1)S(1)}, bf16[112,1152]{1,0:T(8,128)(2,1)S(1)}, u32[]{:S(2)}, u32[]{:S(2)}) %collective-permute-start.1) | collective-permute-done | bytes 258080 | tf_op jit(solution)/shard_map/chip_hi/ppermute | solution.py:229
  33.1 5.2 %collective-permute-start.5 = (bf16[112,1152]{1,0:T(8,128)(2,1)S(1)}, bf16[112,1152]{1,0:T(8,128)(2,1)S(1)}, u32[]{:S(2)}, u32[]{:S(2)}) collective-permute-start(bf16[112,1152]{1,0:T(8,128)(2,1)S(1)} %collective-permute-done.1.x2_hi), channel_id=1, source_target_pairs={{0,510},{1,511},{2,4},{3,5},{4,2},{5,3},{6,8},{7,9},{8,6},{9,7},{1... | collective-permute-start | bytes 774152 | tf_op jit(solution)/shard_map/group_hi/ppermute | solution.py:229
  39.6 0.7 reduce
  40.3 0.1 reshape.15.pos
  40.4 0.2 match.1
  40.5 0.0 collective-permute-done.2.y0
  40.5 0.2 join.1.near
  40.7 5.8 %collective-permute-start.3 = (bf16[896,1152]{1,0:T(8,128)(2,1)S(1)}, bf16[896,1152]{1,0:T(8,128)(2,1)S(1)}, u32[]{:S(2)}, u32[]{:S(2)}) collective-permute-start(bf16[896,1152]{1,0:T(8,128)(2,1)S(1)} %join.1.near), channel_id=1, source_target_pairs={{0,1},{1,0},{2,3},{3,2},{4,5},{5,4},{6,7},{7,6},{8,9},{9,8},{10,11... | collective-permute-start | bytes 6193160 | tf_op jit(solution)/shard_map/core_xy/ppermute | solution.py:229
  46.5 0.0 collective-permute-done.4.y_lo
  46.5 0.1 collective-permute-done.5.y_hi
  46.6 0.0 collective-permute-done.6._w2.w2
  46.7 5.4 %collective-permute-start.7 = (bf16[224,1152]{1,0:T(8,128)(2,1)S(1)}, bf16[224,1152]{1,0:T(8,128)(2,1)S(1)}, u32[]{:S(2)}, u32[]{:S(2)}) collective-permute-start(bf16[224,1152]{1,0:T(8,128)(2,1)S(1)} %pair.1.y1), channel_id=1, source_target_pairs={{0,1},{1,0},{2,3},{3,2},{4,5},{5,4},{6,7},{7,6},{8,9},{9,8},{10,11... | collective-permute-start | bytes 1548296 | tf_op jit(solution)/shard_map/core_y/ppermute | solution.py:229
  52.0 0.0 collective-permute-done.3.near_c
  52.0 1.4 %mid.1.part = f32[224,1152]{1,0:T(8,128)S(1)} custom-call(f32[2,128]{1,0:T(2,128)S(1)} %get-tuple-element.16.sc, bf16[896,1152]{1,0:T(8,128)(2,1)S(1)} %join.1.near, bf16[896,1152]{1,0:T(8,128)(2,1)S(1)} %collective-permute-done.3.near_c, bf16[224,1152]{1,0:T(8,128)(2,1)S(1)} %pair.1.y1), custom_call_target="tpu_custom_call" | custom-call | flops 8000000000 | bytes 1 | tf_op jit(solution)/shard_map/mid/pallas_call | solution.py:267
  53.5 0.1 collective-permute-done.7.y1_c
  53.5 0.8 %late.1._send = bf16[224,1152]{1,0:T(8,128)(2,1)S(1)} custom-call(f32[2,128]{1,0:T(2,128)S(1)} %get-tuple-element.16.sc, bf16[896,1152]{1,0:T(8,128)(2,1)S(1)} %join.1.near, bf16[224,1152]{1,0:T(8,128)(2,1)S(1)} %collective-permute-done.7.y1_c, f32[224,1152]{1,0:T(8,128)S(1)} %mid.1.part), custom_call_target="tpu_custom_call" | custom-call | flops 64000000000 | bytes 1 | tf_op jit(solution)/shard_map/late/pallas_call | solution.py:268
  54.4 1.9 %collective-permute-start.8 = (bf16[224,1152]{1,0:T(8,128)(2,1)S(1)}, bf16[224,1152]{1,0:T(8,128)(2,1)S(1)}, u32[]{:S(2)}, u32[]{:S(2)}) collective-permute-start(bf16[224,1152]{1,0:T(8,128)(2,1)S(1)} %late.1._send), channel_id=1, source_target_pairs={{0,2},{1,3},{2,0},{3,1},{4,6},{5,7},{6,4},{7,5},{8,10},{9,11},{10,... | collective-permute-start | bytes 1548296 | tf_op jit(solution)/shard_map/chip_send/ppermute | solution.py:229
  56.3 0.0 copy-start
  56.3 0.0 copy-start.1
  56.3 5.0 %visit.1 = (f32[224,1152]{1,0:T(8,128)S(1)}, f32[224,1152]{1,0:T(8,128)S(1)}, bf16[112,1152]{1,0:T(8,128)(2,1)S(1)}, bf16[112,1152]{1,0:T(8,128)(2,1)S(1)}) custom-call(f32[2,128]{1,0:T(2,128)S(1)} %get-tuple-element.16.sc, bf16[896,1152]{1,0:T(8,128)(2,1)S(1)} %join.1.near, bf16[896,1152]{1,0:T(8,128)(2,1)S(1)} %collective-permute-done.3.near_c, ...), custom_call_target="tpu_custom_call" | custom-call | flops 32000000000 | bytes 1 | tf_op jit(solution)/shard_map/visit/pallas_call | solution.py:270
  61.4 2.3 %collective-permute-start.9 = (bf16[112,1152]{1,0:T(8,128)(2,1)S(1)}, bf16[112,1152]{1,0:T(8,128)(2,1)S(1)}, u32[]{:S(2)}, u32[]{:S(2)}) collective-permute-start(bf16[112,1152]{1,0:T(8,128)(2,1)S(1)} %get-tuple-element.25), channel_id=1, source_target_pairs={{0,1},{1,0},{2,3},{3,2},{4,5},{5,4},{6,7},{7,6},{8,9},{9,8},{10,11... | collective-permute-start | bytes 774152 | tf_op jit(solution)/shard_map/core_w_lo/ppermute | solution.py:229
  63.6 2.0 %collective-permute-start.10 = (bf16[112,1152]{1,0:T(8,128)(2,1)S(1)}, bf16[112,1152]{1,0:T(8,128)(2,1)S(1)}, u32[]{:S(2)}, u32[]{:S(2)}) collective-permute-start(bf16[112,1152]{1,0:T(8,128)(2,1)S(1)} %get-tuple-element.26), channel_id=1, source_target_pairs={{0,1},{1,0},{2,3},{3,2},{4,5},{5,4},{6,7},{7,6},{8,9},{9,8},{10,11... | collective-permute-start | bytes 774152 | tf_op jit(solution)/shard_map/core_w_hi/ppermute | solution.py:229
  65.7 0.0 collective-permute-done.9.w2_lo_c
  65.7 1.4 %collective-permute-done.10.w2_hi_c = bf16[112,1152]{1,0:T(8,128)(2,1)S(1)} collective-permute-done((bf16[112,1152]{1,0:T(8,128)(2,1)S(1)}, bf16[112,1152]{1,0:T(8,128)(2,1)S(1)}, u32[]{:S(2)}, u32[]{:S(2)}) %collective-permute-start.10) | collective-permute-done | bytes 258080 | tf_op jit(solution)/shard_map/core_w_hi/ppermute | solution.py:229
  67.1 0.0 copy-done
  67.1 0.0 copy-done.1
  67.1 2.1 %rest.1 = (f32[224,1152]{1,0:T(8,128)}, f32[224,1152]{1,0:T(8,128)}) custom-call(f32[2,128]{1,0:T(2,128)S(1)} %get-tuple-element.16.sc, s32[1]{0:T(128)S(6)} %select_n.5.odd, bf16[224,1152]{1,0:T(8,128)(2,1)S(1)} %copy-done, bf16[224,1152]{1,0:T(8,128)(2,1)S(1)} %copy-done.1, bf16[224,1152]{1,0:T(8,128)(2,1)S(1)} %get-tuple-element.17.p, ...), custom_call_target="tpu_custom_call" | custom-call | flops 1 | bytes 1 | tf_op jit(solution)/shard_map/rest/pallas_call | solution.py:274
  69.2 0.0 collective-permute-done.8.back
  69.2 1.3 %last.1 = (f32[224,1152]{1,0:T(8,128)}, f32[224,1152]{1,0:T(8,128)}) custom-call(s32[1]{0:T(128)S(6)} %select_n.5.odd, bf16[224,1152]{1,0:T(8,128)(2,1)S(1)} %copy-done, bf16[224,1152]{1,0:T(8,128)(2,1)S(1)} %copy-done.1, f32[224,1152]{1,0:T(8,128)S(1)} %get-tuple-element.24.sum_q, ...), custom_call_target="tpu_custom_call", output_to_operand_aliasing={{0}: (5, {}), {1}: (6, {})} | custom-call | flops 4000000000 | bytes 1 | tf_op jit(solution)/shard_map/last/pallas_call | solution.py:281
  (1 shorter events, 0.0 us)
Async XLA Ops:
  2.3 38.2 %collective-permute-start.2 = (bf16[224,1152]{1,0:T(8,128)(2,1)S(1)}, bf16[224,1152]{1,0:T(8,128)(2,1)S(1)}, u32[]{:S(2)}, u32[]{:S(2)}) collective-permute-start(bf16[224,1152]{1,0:T(8,128)(2,1)S(1)} %get-tuple-element.17.p), channel_id=1, source_target_pairs={{0,510},{1,511},{2,4},{3,5},{4,2},{5,3},{6,8},{7,9},{8,6},{9,7},{1... | collective-permute-start | bytes 1548296 | tf_op jit(solution)/shard_map/group_p/ppermute | solution.py:229
  18.9 8.7 %collective-permute-start = (bf16[112,1152]{1,0:T(8,128)(2,1)S(1)}, bf16[112,1152]{1,0:T(8,128)(2,1)S(1)}, u32[]{:S(2)}, u32[]{:S(2)}) collective-permute-start(bf16[112,1152]{1,0:T(8,128)(2,1)S(1)} %get-tuple-element.18.q_lo), channel_id=1, source_target_pairs={{0,2},{1,3},{2,0},{3,1},{4,6},{5,7},{6,4},{7,5},{8,10},{9,11},{10,... | collective-permute-start | bytes 774152 | tf_op jit(solution)/shard_map/chip_lo/ppermute | solution.py:229
  20.8 12.3 %collective-permute-start.1 = (bf16[112,1152]{1,0:T(8,128)(2,1)S(1)}, bf16[112,1152]{1,0:T(8,128)(2,1)S(1)}, u32[]{:S(2)}, u32[]{:S(2)}) collective-permute-start(bf16[112,1152]{1,0:T(8,128)(2,1)S(1)} %get-tuple-element.19.q_hi), channel_id=1, source_target_pairs={{0,2},{1,3},{2,0},{3,1},{4,6},{5,7},{6,4},{7,5},{8,10},{9,11},{10,... | collective-permute-start | bytes 774152 | tf_op jit(solution)/shard_map/chip_hi/ppermute | solution.py:229
  24.2 22.4 %collective-permute-start.6 = (bf16[224,1152]{1,0:T(8,128)(2,1)S(1)}, bf16[224,1152]{1,0:T(8,128)(2,1)S(1)}, u32[]{:S(2)}, u32[]{:S(2)}) collective-permute-start(bf16[224,1152]{1,0:T(8,128)(2,1)S(1)} %get-tuple-element.17.p), channel_id=1, source_target_pairs={{0,2},{1,3},{2,0},{3,1},{4,6},{5,7},{6,4},{7,5},{8,10},{9,11},{10,... | collective-permute-start | bytes 1548296 | tf_op jit(solution)/shard_map/chip_p/ppermute | solution.py:229
  27.6 18.9 %collective-permute-start.4 = (bf16[112,1152]{1,0:T(8,128)(2,1)S(1)}, bf16[112,1152]{1,0:T(8,128)(2,1)S(1)}, u32[]{:S(2)}, u32[]{:S(2)}) collective-permute-start(bf16[112,1152]{1,0:T(8,128)(2,1)S(1)} %collective-permute-done.x2_lo), channel_id=1, source_target_pairs={{0,510},{1,511},{2,4},{3,5},{4,2},{5,3},{6,8},{7,9},{8,6},{9,7},{1... | collective-permute-start | bytes 774152 | tf_op jit(solution)/shard_map/group_lo/ppermute | solution.py:229
  33.1 13.5 %collective-permute-start.5 = (bf16[112,1152]{1,0:T(8,128)(2,1)S(1)}, bf16[112,1152]{1,0:T(8,128)(2,1)S(1)}, u32[]{:S(2)}, u32[]{:S(2)}) collective-permute-start(bf16[112,1152]{1,0:T(8,128)(2,1)S(1)} %collective-permute-done.1.x2_hi), channel_id=1, source_target_pairs={{0,510},{1,511},{2,4},{3,5},{4,2},{5,3},{6,8},{7,9},{8,6},{9,7},{1... | collective-permute-start | bytes 774152 | tf_op jit(solution)/shard_map/group_hi/ppermute | solution.py:229
  40.7 11.3 %collective-permute-start.3 = (bf16[896,1152]{1,0:T(8,128)(2,1)S(1)}, bf16[896,1152]{1,0:T(8,128)(2,1)S(1)}, u32[]{:S(2)}, u32[]{:S(2)}) collective-permute-start(bf16[896,1152]{1,0:T(8,128)(2,1)S(1)} %join.1.near), channel_id=1, source_target_pairs={{0,1},{1,0},{2,3},{3,2},{4,5},{5,4},{6,7},{7,6},{8,9},{9,8},{10,11... | collective-permute-start | bytes 6193160 | tf_op jit(solution)/shard_map/core_xy/ppermute | solution.py:229
  46.7 6.9 %collective-permute-start.7 = (bf16[224,1152]{1,0:T(8,128)(2,1)S(1)}, bf16[224,1152]{1,0:T(8,128)(2,1)S(1)}, u32[]{:S(2)}, u32[]{:S(2)}) collective-permute-start(bf16[224,1152]{1,0:T(8,128)(2,1)S(1)} %pair.1.y1), channel_id=1, source_target_pairs={{0,1},{1,0},{2,3},{3,2},{4,5},{5,4},{6,7},{7,6},{8,9},{9,8},{10,11... | collective-permute-start | bytes 1548296 | tf_op jit(solution)/shard_map/core_y/ppermute | solution.py:229
  54.4 14.9 %collective-permute-start.8 = (bf16[224,1152]{1,0:T(8,128)(2,1)S(1)}, bf16[224,1152]{1,0:T(8,128)(2,1)S(1)}, u32[]{:S(2)}, u32[]{:S(2)}) collective-permute-start(bf16[224,1152]{1,0:T(8,128)(2,1)S(1)} %late.1._send), channel_id=1, source_target_pairs={{0,2},{1,3},{2,0},{3,1},{4,6},{5,7},{6,4},{7,5},{8,10},{9,11},{10,... | collective-permute-start | bytes 1548296 | tf_op jit(solution)/shard_map/chip_send/ppermute | solution.py:229
  56.3 10.8 %copy-start = (bf16[224,1152]{1,0:T(8,128)(2,1)S(1)}, bf16[224,1152]{1,0:T(8,128)(2,1)}, u32[]{:S(2)}) copy-start(bf16[224,1152]{1,0:T(8,128)(2,1)} %img.5) | copy-start | bytes 1548292
  56.3 10.8 %copy-start.1 = (bf16[224,1152]{1,0:T(8,128)(2,1)S(1)}, bf16[224,1152]{1,0:T(8,128)(2,1)}, u32[]{:S(2)}) copy-start(bf16[224,1152]{1,0:T(8,128)(2,1)} %txt.5) | copy-start | bytes 1548292
  61.4 4.3 %collective-permute-start.9 = (bf16[112,1152]{1,0:T(8,128)(2,1)S(1)}, bf16[112,1152]{1,0:T(8,128)(2,1)S(1)}, u32[]{:S(2)}, u32[]{:S(2)}) collective-permute-start(bf16[112,1152]{1,0:T(8,128)(2,1)S(1)} %get-tuple-element.25), channel_id=1, source_target_pairs={{0,1},{1,0},{2,3},{3,2},{4,5},{5,4},{6,7},{7,6},{8,9},{9,8},{10,11... | collective-permute-start | bytes 774152 | tf_op jit(solution)/shard_map/core_w_lo/ppermute | solution.py:229
  63.6 3.4 %collective-permute-start.10 = (bf16[112,1152]{1,0:T(8,128)(2,1)S(1)}, bf16[112,1152]{1,0:T(8,128)(2,1)S(1)}, u32[]{:S(2)}, u32[]{:S(2)}) collective-permute-start(bf16[112,1152]{1,0:T(8,128)(2,1)S(1)} %get-tuple-element.26), channel_id=1, source_target_pairs={{0,1},{1,0},{2,3},{3,2},{4,5},{5,4},{6,7},{7,6},{8,9},{9,8},{10,11... | collective-permute-start | bytes 774152 | tf_op jit(solution)/shard_map/core_w_hi/ppermute | solution.py:229

commit v4 on v3

--- a/solution.py
+++ b/solution.py
@@ -11,8 +11,14 @@
 HBM = pl.BlockSpec(memory_space=pltpu.HBM)
 NT = (((1,), (1,)), ((), ()))
 NN = (((1,), (0,)), ((), ()))
-PIECES = 2
-COST = {"pair": 32 * 10**9, "mid": 8 * 10**9, "late": 64 * 10**9, "visit": 32 * 10**9, "last": 4 * 10**9}
+COST = {"pair": 16 * 10**9, "late": 8 * 10**9, "rest": 1 * 10**9, "last": 16 * 10**9}
+
+
+def pieces_of(rows):
+    half = rows // 2
+    first = half // 32 * 16
+    edges = [0, first, half, half + first, rows]
+    return [(low, high - low) for low, high in zip(edges, edges[1:])]
 
 
 def inv_norm(values):
@@ -39,39 +45,37 @@
     )
 
 
-def unit_body(odd, img, txt, p, q_lo, q_hi, raw, sems):
-    rows = img.shape[0]
-    size = rows // PIECES
-    half = rows // 2
-    copies = []
-    for j in range(PIECES):
-        part = pl.ds(j * size, size)
-        for i, ref in enumerate((img, txt)):
-            copies.append(
-                pltpu.make_async_copy(ref.at[part], raw.at[i, part], sems.at[2 * j + i])
-            )
-    for copy in copies:
-        copy.start()
-    for j in range(PIECES):
-        part = pl.ds(j * size, size)
-        unit = []
-        for i in range(2):
-            copies[2 * j + i].wait()
-            values = raw[i, part].astype(jnp.float32)
-            unit.append((values * inv_norm(values)).astype(jnp.bfloat16))
-        q, start = (q_lo, j * size) if j * size < half else (q_hi, j * size - half)
-
-        def put(first, second):
-            p[part] = first
-            q[pl.ds(start, size)] = second
-
-        @pl.when(odd[0] == 0)
-        def _():
-            put(unit[0], unit[1])
-
-        @pl.when(odd[0] == 1)
-        def _():
-            put(unit[1], unit[0])
+def unit_rows(take_txt, img, txt, outs, raw, sems):
+    pieces = pieces_of(img.shape[0])
+
+    def go(ref):
+        copies = []
+        for j, (start, size) in enumerate(pieces):
+            part = pl.ds(start, size)
+            copies.append(pltpu.make_async_copy(ref.at[part], raw.at[part], sems.at[j]))
+            copies[-1].start()
+        for copy, (start, size) in zip(copies, pieces):
+            copy.wait()
+            values = raw[pl.ds(start, size)].astype(jnp.float32)
+            out = outs[start // outs[0].shape[0]]
+            into = pl.ds(start % out.shape[0], size)
+            out[into] = (values * inv_norm(values)).astype(jnp.bfloat16)
+
+    @pl.when(jnp.logical_not(take_txt))
+    def _():
+        go(img)
+
+    @pl.when(take_txt)
+    def _():
+        go(txt)
+
+
+def unit_p_body(odd, img, txt, p, raw, sems):
+    unit_rows(odd[0] == 1, img, txt, [p], raw, sems)
+
+
+def unit_q_body(odd, img, txt, q_lo, q_hi, raw, sems):
+    unit_rows(odd[0] == 0, img, txt, [q_lo, q_hi], raw, sems)
 
 
 def match_body(here, scale, shift, pos, sc, u_p, v_p, u_q, v_q):
@@ -131,7 +135,13 @@
         row += part.shape[0]
 
 
-def pair_body(y_lo, y_hi, _w2, y1):
+def own_body(sc, near, u_p, v_p, u_q, v_q, sum_p, sum_q):
+    x, y, x2, y0 = (block(near, j) for j in range(4))
+    sum_p[...] = terms(x, [y], sc, (u_p[...], [v_p[0:1]])) + terms(x, [y0], sc)
+    sum_q[...] = terms(y, [x, x2], sc, (u_q[...], [v_q[0:1], v_q[2:3]]))
+
+
+def pair_body(y_lo, y_hi, _w2, _sum, y1):
     half = y_lo.shape[0]
     y1[:half] = y_lo[...]
     y1[half:] = y_hi[...]
@@ -146,7 +156,10 @@
     part[...] = terms(block(near, 2), [block(near, 3), block(near_c, 3), y1[...]], sc)
 
 
-def late_body(sc, near, y1_c, part, out):
+def late_body(sc, near, y1_c, part, w2, out, w2_lo, w2_hi):
+    half = w2_lo.shape[0]
+    w2_lo[...] = w2[:half]
+    w2_hi[...] = w2[half:]
     out[...] = (part[...] + terms(block(near, 2), [y1_c[...]], sc)).astype(out.dtype)
 
 
@@ -158,13 +171,10 @@
 
 
 def write_out(is_txt, img, txt, dunit, img_grad, txt_grad, held, sems):
-    rows = img.shape[0]
-    size = rows // PIECES
-
     def go(raw, grad):
         copies = []
-        for j in range(PIECES):
-            part = pl.ds(j * size, size)
+        for j, (start, size) in enumerate(pieces_of(raw.shape[0])):
+            part = pl.ds(start, size)
             held[part] = tangent(raw[part], dunit(part))
             copies.append(pltpu.make_async_copy(held.at[part], grad.at[part], sems.at[j]))
             copies[-1].start()
@@ -181,19 +191,17 @@
 
 
 def visit_body(
-    sc, near, near_c, y1, y1_c, w2, _send, u_p, v_p, u_q, v_q, sum_p, sum_q, w2_lo, w2_hi
+    sc, near, near_c, y1, y1_c, w2, _send, u_p, v_p, u_q, v_q, own_p, own_q, sum_p, sum_q
 ):
-    half = w2_lo.shape[0]
-    w2_lo[...] = w2[:half]
-    w2_hi[...] = w2[half:]
-    x, y, x2, y0 = (block(near, j) for j in range(4))
+    x, y = block(near, 0), block(near, 1)
     x_c, y_c, x2_c, y0_c = (block(near_c, j) for j in range(4))
-    columns = [v_p[j : j + 1] for j in range(3)]
-    sum_p[...] = terms(x, [y, y_c, w2[...]], sc, (u_p[...], columns)) + terms(
-        x, [y0, y0_c, y1[...], y1_c[...]], sc
-    )
-    columns = [v_q[j : j + 1] for j in range(4)]
-    sum_q[...] = terms(y, [x, x_c, x2, x2_c], sc, (u_q[...], columns))
+    sum_p[...] = (
+        own_p[...]
+        + terms(x, [y_c, w2[...]], sc, (u_p[...], [v_p[1:2], v_p[2:3]]))
+        + terms(x, [y0_c, y1[...], y1_c[...]], sc)
+    )
+    own = (u_q[...], [v_q[1:2], v_q[3:4]])
+    sum_q[...] = own_q[...] + terms(y, [x_c, x2_c], sc, own)
 
 
 def rest_body(
@@ -245,12 +253,12 @@
     dma = pltpu.SemaphoreType.DMA
     far = lambda x: pltpu.with_memory_space_constraint(x, pltpu.HBM)
 
-    p, q_lo, q_hi = call(
-        unit_body,
-        (one, part, part),
-        [SMEM, HBM, HBM],
-        scratch_shapes=[pltpu.VMEM((2, rows, depth), bf16), dma((2 * PIECES,))],
-    )(odd, far(img), far(txt))
+    img_far, txt_far = far(img), far(txt)
+    scratch = [pltpu.VMEM((rows, depth), bf16), dma((4,))]
+    p = call(unit_p_body, one, [SMEM, HBM, HBM], scratch_shapes=scratch)(odd, img_far, txt_far)
+    q_lo, q_hi = call(unit_q_body, (part, part), [SMEM, HBM, HBM], scratch_shapes=scratch)(
+        odd, img_far, txt_far
+    )
     y0 = group(p, "group_p")
     x2_lo, x2_hi = chip(q_lo, "chip_lo"), chip(q_hi, "chip_hi")
     w2 = chip(p, "chip_p")
@@ -262,15 +270,18 @@
     )
     near = call(join_body, four, [VMEM] * 6)(p, q_lo, q_hi, x2_lo, x2_hi, y0)
     near_c = core(near, "core_xy")
-    y1 = call(pair_body, one, [VMEM] * 3)(y_lo, y_hi, w2)
+    own_p, own_q = call(own_body, (wide, wide), [VMEM] * 6)(sc, near, *match)
+    y1 = call(pair_body, one, [VMEM] * 4)(y_lo, y_hi, w2, own_q)
     y1_c = core(y1, "core_y")
     part_x = call(mid_body, wide, [VMEM] * 4)(sc, near, near_c, y1)
-    send = call(late_body, one, [VMEM] * 4)(sc, near, y1_c, part_x)
+    send, w2_lo, w2_hi = call(late_body, (one, part, part), [VMEM] * 5)(
+        sc, near, y1_c, part_x, w2
+    )
     back = chip(send, "chip_send")
-    sum_p, sum_q, w2_lo, w2_hi = call(visit_body, (wide, wide, part, part), [VMEM] * 11)(
-        sc, near, near_c, y1, y1_c, w2, send, *match
-    )
-    out = [pltpu.VMEM((rows, depth), jnp.float32), dma((PIECES,))]
+    sum_p, sum_q = call(visit_body, (wide, wide), [VMEM] * 13)(
+        sc, near, near_c, y1, y1_c, w2, send, *match, own_p, own_q
+    )
+    out = [pltpu.VMEM((rows, depth), jnp.float32), dma((4,))]
     grads = call(
         rest_body,
         (wide, wide),

time: 71 us -> 75.8 us (1.068)
  Pallas kernels: 12.7 us -> 18.8 us
  starting transfers between devices: 48.6 us -> 47 us
  waiting for transfers between devices: 6.28 us -> 7.17 us
    pallas_call x4 -> x6, Pallas kernels: 7.56 us -> 11 us  [the longest x1 4.5 us: local(): call(visit_body, (wide, wide), [VMEM] * 13)]
    ppermute x11, starting transfers between devices: 48.6 us -> 47 us  [go(): return lax.ppermute(x, AXES, pairs)]
    pallas_call x1, Pallas kernels: 1.43 us -> 3.03 us  [local(): part_x = call(mid_body, wide, [VMEM] * 4)(sc, near, near_c, y1)]
    pallas_call x1, Pallas kernels: 0.15 us -> 1.14 us  [local(): near = call(join_body, four, [VMEM] * 6)(p, q_lo, q_hi, x2_lo, x2_hi, y0)]
    ppermute x11, waiting for transfers between devices: 6.28 us -> 7.17 us  [go(): return lax.ppermute(x, AXES, pairs)]
  transfers between devices with their start and end apart: 11 -> 11, of which waited for: 5 -> 3; matrix products, arithmetic and copies ran while one was open for 1% -> 0% of each run, Pallas kernels for 13% -> 20%
where the time goes in v4:
time: 75.8 us; the launch traced here: 75.2 us
  starting transfers between devices  47 us (62%)
  Pallas kernels  18.8 us (25%)
  waiting for transfers between devices  7.17 us (9%)
  between operations  2.2 us (3%)
    ppermute x11, starting transfers between devices, go(): return lax.ppermute(x, AXES, pairs)  47 us
    ppermute x11, waiting for transfers between devices, go(): return lax.ppermute(x, AXES, pairs)  7.17 us
    pallas_call x1, Pallas kernels, local(): call(visit_body, (wide, wide), [VMEM] * 13)  4.5 us
    pallas_call x1, Pallas kernels, local(): part_x = call(mid_body, wide, [VMEM] * 4)(sc, near, near_c, y1)  3.03 us
    pallas_call x1, Pallas kernels, local(): call(rest_body, (wide, wide), [VMEM, SMEM] + [VMEM] * 8, (HBM, HBM), scra...  2.09 us
    pallas_call x1, Pallas kernels, local(): own_p, own_q = call(own_body, (wide, wide), [VMEM] * 6)(sc, near, *match)  1.73 us
  transfers between devices with their start and end apart: 11, of which 3 were waited for; matrix products, arithmetic and copies ran while one was open for 0% of the time, Pallas kernels for 20%

profile of v4, /device:TPU:1, one launch (start us, length us, event | category | flops | bytes accessed | tf_op | source)
XLA Modules:
  0.0 75.2 jit_solution(14302084208945425263)
XLA Ops:
  0.6 1.4 %unit_p.1.p = bf16[224,1152]{1,0:T(8,128)(2,1)S(1)} custom-call(s32[1]{0:T(128)S(6)} %select_n.5.odd, bf16[224,1152]{1,0:T(8,128)(2,1)} %img.7, bf16[224,1152]{1,0:T(8,128)(2,1)} %txt.7), custom_call_target="tpu_custom_call" | custom-call | flops 1 | bytes 1 | tf_op jit(solution)/shard_map/unit_p/pallas_call | solution.py:258
  2.1 16.6 %collective-permute-start.2 = (bf16[224,1152]{1,0:T(8,128)(2,1)S(1)}, bf16[224,1152]{1,0:T(8,128)(2,1)S(1)}, u32[]{:S(2)}, u32[]{:S(2)}) collective-permute-start(bf16[224,1152]{1,0:T(8,128)(2,1)S(1)} %unit_p.1.p), channel_id=1, source_target_pairs={{0,510},{1,511},{2,4},{3,5},{4,2},{5,3},{6,8},{7,9},{8,6},{9,7},{1... | collective-permute-start | bytes 1548296 | tf_op jit(solution)/shard_map/group_p/ppermute | solution.py:237
  18.7 1.4 %unit_q.1 = (bf16[112,1152]{1,0:T(8,128)(2,1)S(1)}, bf16[112,1152]{1,0:T(8,128)(2,1)S(1)}) custom-call(s32[1]{0:T(128)S(6)} %select_n.5.odd, bf16[224,1152]{1,0:T(8,128)(2,1)} %img.7, bf16[224,1152]{1,0:T(8,128)(2,1)} %txt.7), custom_call_target="tpu_custom_call" | custom-call | flops 1 | bytes 1 | tf_op jit(solution)/shard_map/unit_q/pallas_call | solution.py:259
  20.1 1.9 %collective-permute-start = (bf16[112,1152]{1,0:T(8,128)(2,1)S(1)}, bf16[112,1152]{1,0:T(8,128)(2,1)S(1)}, u32[]{:S(2)}, u32[]{:S(2)}) collective-permute-start(bf16[112,1152]{1,0:T(8,128)(2,1)S(1)} %get-tuple-element.19.q_lo), channel_id=1, source_target_pairs={{0,2},{1,3},{2,0},{3,1},{4,6},{5,7},{6,4},{7,5},{8,10},{9,11},{10,... | collective-permute-start | bytes 774152 | tf_op jit(solution)/shard_map/chip_lo/ppermute | solution.py:237
  22.0 0.0 copy-start.2
  22.0 3.4 %collective-permute-start.1 = (bf16[112,1152]{1,0:T(8,128)(2,1)S(1)}, bf16[112,1152]{1,0:T(8,128)(2,1)}, u32[]{:S(2)}, u32[]{:S(2)}) collective-permute-start(bf16[112,1152]{1,0:T(8,128)(2,1)S(1)} %get-tuple-element.20.q_hi), channel_id=1, source_target_pairs={{0,2},{1,3},{2,0},{3,1},{4,6},{5,7},{6,4},{7,5},{8,10},{9,11},{10,... | collective-permute-start | bytes 774152 | tf_op jit(solution)/shard_map/chip_hi/ppermute | solution.py:237
  25.4 1.9 %collective-permute-start.6 = (bf16[224,1152]{1,0:T(8,128)(2,1)S(1)}, bf16[224,1152]{1,0:T(8,128)(2,1)S(1)}, u32[]{:S(2)}, u32[]{:S(2)}) collective-permute-start(bf16[224,1152]{1,0:T(8,128)(2,1)S(1)} %unit_p.1.p), channel_id=1, source_target_pairs={{0,2},{1,3},{2,0},{3,1},{4,6},{5,7},{6,4},{7,5},{8,10},{9,11},{10,... | collective-permute-start | bytes 1548296 | tf_op jit(solution)/shard_map/chip_p/ppermute | solution.py:237
  27.3 1.4 %collective-permute-done.x2_lo = bf16[112,1152]{1,0:T(8,128)(2,1)S(1)} collective-permute-done((bf16[112,1152]{1,0:T(8,128)(2,1)S(1)}, bf16[112,1152]{1,0:T(8,128)(2,1)S(1)}, u32[]{:S(2)}, u32[]{:S(2)}) %collective-permute-start) | collective-permute-done | bytes 258080 | tf_op jit(solution)/shard_map/chip_lo/ppermute | solution.py:237
  28.7 2.2 %collective-permute-start.4 = (bf16[112,1152]{1,0:T(8,128)(2,1)S(1)}, bf16[112,1152]{1,0:T(8,128)(2,1)}, u32[]{:S(2)}, u32[]{:S(2)}) collective-permute-start(bf16[112,1152]{1,0:T(8,128)(2,1)S(1)} %collective-permute-done.x2_lo), channel_id=1, source_target_pairs={{0,510},{1,511},{2,4},{3,5},{4,2},{5,3},{6,8},{7,9},{8,6},{9,7},{1... | collective-permute-start | bytes 774152 | tf_op jit(solution)/shard_map/group_lo/ppermute | solution.py:237
  31.0 3.4 %collective-permute-done.1.x2_hi = bf16[112,1152]{1,0:T(8,128)(2,1)} collective-permute-done((bf16[112,1152]{1,0:T(8,128)(2,1)S(1)}, bf16[112,1152]{1,0:T(8,128)(2,1)}, u32[]{:S(2)}, u32[]{:S(2)}) %collective-permute-start.1) | collective-permute-done | bytes 258080 | tf_op jit(solution)/shard_map/chip_hi/ppermute | solution.py:237
  34.4 5.1 %collective-permute-start.5 = (bf16[112,1152]{1,0:T(8,128)(2,1)}, bf16[112,1152]{1,0:T(8,128)(2,1)}, u32[]{:S(2)}, u32[]{:S(2)}) collective-permute-start(bf16[112,1152]{1,0:T(8,128)(2,1)} %collective-permute-done.1.x2_hi), channel_id=1, source_target_pairs={{0,510},{1,511},{2,4},{3,5},{4,2},{5,3},{6,8},{7,9},{8,6},{9,7},{1... | collective-permute-start | bytes 774152 | tf_op jit(solution)/shard_map/group_hi/ppermute | solution.py:237
  39.5 0.0 collective-permute-done.2.y0
  39.5 1.1 %join.1.near = bf16[896,1152]{1,0:T(8,128)(2,1)S(1)} custom-call(bf16[224,1152]{1,0:T(8,128)(2,1)S(1)} %unit_p.1.p, bf16[112,1152]{1,0:T(8,128)(2,1)S(1)} %get-tuple-element.19.q_lo, bf16[112,1152]{1,0:T(8,128)(2,1)S(1)} %get-tuple-element.20.q_hi, bf16[112,1152]{1,0:T(8,128)(2,1)S(1)} %collective-permute-done.x2_lo, ...), custom_call_target="tpu_custom_call" | custom-call | flops 1 | bytes 1 | tf_op jit(solution)/shard_map/join/pallas_call | solution.py:271
  40.6 5.8 %collective-permute-start.3 = (bf16[896,1152]{1,0:T(8,128)(2,1)S(1)}, bf16[896,1152]{1,0:T(8,128)(2,1)}, u32[]{:S(2)}, u32[]{:S(2)}) collective-permute-start(bf16[896,1152]{1,0:T(8,128)(2,1)S(1)} %join.1.near), channel_id=1, source_target_pairs={{0,1},{1,0},{2,3},{3,2},{4,5},{5,4},{6,7},{7,6},{8,9},{9,8},{10,11... | collective-permute-start | bytes 6193160 | tf_op jit(solution)/shard_map/core_xy/ppermute | solution.py:237
  47.7 0.0 copy-done.2
  47.8 0.1 reshape.15.pos
  47.8 0.2 match.1
  48.0 1.7 %own.1 = (f32[224,1152]{1,0:T(8,128)S(1)}, f32[224,1152]{1,0:T(8,128)S(1)}) custom-call(f32[2,128]{1,0:T(2,128)S(1)} %get-tuple-element.18.sc, bf16[896,1152]{1,0:T(8,128)(2,1)S(1)} %join.1.near, s32[224,1]{1,0:T(8,128)S(1)} %get-tuple-element.21.u_p, s32[4,224]{1,0:T(4,128)S(1)} %get-tuple-element.22.v_p, s32[224,1]{1,0:T(8,128)S(1)} %get-tuple-element.23.u_q, ...), custom_call_target="tpu_custom_call" | custom-call | flops 1 | bytes 1 | tf_op jit(solution)/shard_map/own/pallas_call | solution.py:273
  49.7 0.0 collective-permute-done.4.y_lo
  49.7 0.0 collective-permute-done.5.y_hi
  49.8 0.0 collective-permute-done.6._w2.w2
  49.8 1.1 %pair.1.y1 = bf16[224,1152]{1,0:T(8,128)(2,1)S(1)} custom-call(bf16[112,1152]{1,0:T(8,128)(2,1)} %collective-permute-done.4.y_lo, bf16[112,1152]{1,0:T(8,128)(2,1)} %collective-permute-done.5.y_hi, bf16[224,1152]{1,0:T(8,128)(2,1)S(1)} %collective-permute-done.6._w2.w2, f32[224,1152]{1,0:T(8,128)S(1)} %get-tuple-element.25._sum.own_q), custom_call_target="tpu_custom_call" | custom-call | flops 16000000000 | bytes 1 | tf_op jit(solution)/shard_map/pair/pallas_call | solution.py:274
  50.9 3.8 %collective-permute-start.7 = (bf16[224,1152]{1,0:T(8,128)(2,1)S(1)}, bf16[224,1152]{1,0:T(8,128)(2,1)S(1)}, u32[]{:S(2)}, u32[]{:S(2)}) collective-permute-start(bf16[224,1152]{1,0:T(8,128)(2,1)S(1)} %pair.1.y1), channel_id=1, source_target_pairs={{0,1},{1,0},{2,3},{3,2},{4,5},{5,4},{6,7},{7,6},{8,9},{9,8},{10,11... | collective-permute-start | bytes 1548296 | tf_op jit(solution)/shard_map/core_y/ppermute | solution.py:237
  54.7 0.0 collective-permute-done.3.near_c
  54.7 3.0 %mid.1.part = f32[224,1152]{1,0:T(8,128)S(1)} custom-call(f32[2,128]{1,0:T(2,128)S(1)} %get-tuple-element.18.sc, bf16[896,1152]{1,0:T(8,128)(2,1)S(1)} %join.1.near, bf16[896,1152]{1,0:T(8,128)(2,1)} %collective-permute-done.3.near_c, bf16[224,1152]{1,0:T(8,128)(2,1)S(1)} %pair.1.y1), custom_call_target="tpu_custom_call" | custom-call | flops 1 | bytes 1 | tf_op jit(solution)/shard_map/mid/pallas_call | solution.py:276
  57.7 0.0 collective-permute-done.7.y1_c
  57.8 0.9 %late.1 = (bf16[224,1152]{1,0:T(8,128)(2,1)S(1)}, bf16[112,1152]{1,0:T(8,128)(2,1)S(1)}, bf16[112,1152]{1,0:T(8,128)(2,1)S(1)}) custom-call(f32[2,128]{1,0:T(2,128)S(1)} %get-tuple-element.18.sc, bf16[896,1152]{1,0:T(8,128)(2,1)S(1)} %join.1.near, bf16[224,1152]{1,0:T(8,128)(2,1)S(1)} %collective-permute-done.7.y1_c, f32[224,1152]{1,0:T(8,128)S(1)} %mid.1.part, ...), custom_call_target="tpu_custom_call" | custom-call | flops 8000000000 | bytes 1 | tf_op jit(solution)/shard_map/late/pallas_call | solution.py:277
  58.6 1.9 %collective-permute-start.8 = (bf16[224,1152]{1,0:T(8,128)(2,1)S(1)}, bf16[224,1152]{1,0:T(8,128)(2,1)S(1)}, u32[]{:S(2)}, u32[]{:S(2)}) collective-permute-start(bf16[224,1152]{1,0:T(8,128)(2,1)S(1)} %get-tuple-element.26._send), channel_id=1, source_target_pairs={{0,2},{1,3},{2,0},{3,1},{4,6},{5,7},{6,4},{7,5},{8,10},{9,11},{10,... | collective-permute-start | bytes 1548296 | tf_op jit(solution)/shard_map/chip_send/ppermute | solution.py:237
  60.6 1.9 %collective-permute-start.9 = (bf16[112,1152]{1,0:T(8,128)(2,1)S(1)}, bf16[112,1152]{1,0:T(8,128)(2,1)S(1)}, u32[]{:S(2)}, u32[]{:S(2)}) collective-permute-start(bf16[112,1152]{1,0:T(8,128)(2,1)S(1)} %get-tuple-element.29), channel_id=1, source_target_pairs={{0,1},{1,0},{2,3},{3,2},{4,5},{5,4},{6,7},{7,6},{8,9},{9,8},{10,11... | collective-permute-start | bytes 774152 | tf_op jit(solution)/shard_map/core_w_lo/ppermute | solution.py:237
  62.5 2.4 %collective-permute-start.10 = (bf16[112,1152]{1,0:T(8,128)(2,1)S(1)}, bf16[112,1152]{1,0:T(8,128)(2,1)S(1)}, u32[]{:S(2)}, u32[]{:S(2)}) collective-permute-start(bf16[112,1152]{1,0:T(8,128)(2,1)S(1)} %get-tuple-element.30), channel_id=1, source_target_pairs={{0,1},{1,0},{2,3},{3,2},{4,5},{5,4},{6,7},{7,6},{8,9},{9,8},{10,11... | collective-permute-start | bytes 774152 | tf_op jit(solution)/shard_map/core_w_hi/ppermute | solution.py:237
  64.9 0.0 copy-start
  64.9 0.0 copy-start.1
  64.9 4.5 %visit.1 = (f32[224,1152]{1,0:T(8,128)S(1)}, f32[224,1152]{1,0:T(8,128)S(1)}) custom-call(f32[2,128]{1,0:T(2,128)S(1)} %get-tuple-element.18.sc, bf16[896,1152]{1,0:T(8,128)(2,1)S(1)} %join.1.near, bf16[896,1152]{1,0:T(8,128)(2,1)} %collective-permute-done.3.near_c, bf16[224,1152]{1,0:T(8,128)(2,1)S(1)} %pair.1.y1, ...), custom_call_target="tpu_custom_call" | custom-call | flops 1 | bytes 1 | tf_op jit(solution)/shard_map/visit/pallas_call | solution.py:281
  69.5 0.0 collective-permute-done.9.w2_lo_c
  69.5 0.0 collective-permute-done.10.w2_hi_c
  69.5 0.0 copy-done
  69.5 0.0 copy-done.1
  69.5 2.1 %rest.1 = (f32[224,1152]{1,0:T(8,128)}, f32[224,1152]{1,0:T(8,128)}) custom-call(f32[2,128]{1,0:T(2,128)S(1)} %get-tuple-element.18.sc, s32[1]{0:T(128)S(6)} %select_n.5.odd, bf16[224,1152]{1,0:T(8,128)(2,1)S(1)} %copy-done, bf16[224,1152]{1,0:T(8,128)(2,1)S(1)} %copy-done.1, bf16[224,1152]{1,0:T(8,128)(2,1)S(1)} %unit_p.1.p, ...), custom_call_target="tpu_custom_call" | custom-call | flops 1000000000 | bytes 1 | tf_op jit(solution)/shard_map/rest/pallas_call | solution.py:285
  71.6 2.3 %collective-permute-done.8.back = bf16[224,1152]{1,0:T(8,128)(2,1)S(1)} collective-permute-done((bf16[224,1152]{1,0:T(8,128)(2,1)S(1)}, bf16[224,1152]{1,0:T(8,128)(2,1)S(1)}, u32[]{:S(2)}, u32[]{:S(2)}) %collective-permute-start.8) | collective-permute-done | bytes 516128 | tf_op jit(solution)/shard_map/chip_send/ppermute | solution.py:237
  73.9 1.3 %last.1 = (f32[224,1152]{1,0:T(8,128)}, f32[224,1152]{1,0:T(8,128)}) custom-call(s32[1]{0:T(128)S(6)} %select_n.5.odd, bf16[224,1152]{1,0:T(8,128)(2,1)S(1)} %copy-done, bf16[224,1152]{1,0:T(8,128)(2,1)S(1)} %copy-done.1, f32[224,1152]{1,0:T(8,128)S(1)} %get-tuple-element.28.sum_q, ...), custom_call_target="tpu_custom_call", output_to_operand_aliasing={{0}: (5, {}), {1}: (6, {})} | custom-call | flops 16000000000 | bytes 1 | tf_op jit(solution)/shard_map/last/pallas_call | solution.py:292
  (1 shorter events, 0.0 us)
Async XLA Ops:
  2.1 37.4 %collective-permute-start.2 = (bf16[224,1152]{1,0:T(8,128)(2,1)S(1)}, bf16[224,1152]{1,0:T(8,128)(2,1)S(1)}, u32[]{:S(2)}, u32[]{:S(2)}) collective-permute-start(bf16[224,1152]{1,0:T(8,128)(2,1)S(1)} %unit_p.1.p), channel_id=1, source_target_pairs={{0,510},{1,511},{2,4},{3,5},{4,2},{5,3},{6,8},{7,9},{8,6},{9,7},{1... | collective-permute-start | bytes 1548296 | tf_op jit(solution)/shard_map/group_p/ppermute | solution.py:237
  20.1 8.7 %collective-permute-start = (bf16[112,1152]{1,0:T(8,128)(2,1)S(1)}, bf16[112,1152]{1,0:T(8,128)(2,1)S(1)}, u32[]{:S(2)}, u32[]{:S(2)}) collective-permute-start(bf16[112,1152]{1,0:T(8,128)(2,1)S(1)} %get-tuple-element.19.q_lo), channel_id=1, source_target_pairs={{0,2},{1,3},{2,0},{3,1},{4,6},{5,7},{6,4},{7,5},{8,10},{9,11},{10,... | collective-permute-start | bytes 774152 | tf_op jit(solution)/shard_map/chip_lo/ppermute | solution.py:237
  22.0 25.7 %copy-start.2 = (s32[1,896]{1,0:T(1,128)S(1)}, s32[1,896]{1,0:T(1,128)}, u32[]{:S(2)}) copy-start(s32[1,896]{1,0:T(1,128)} %param.7) | copy-start | bytes 10756
  22.0 12.4 %collective-permute-start.1 = (bf16[112,1152]{1,0:T(8,128)(2,1)S(1)}, bf16[112,1152]{1,0:T(8,128)(2,1)}, u32[]{:S(2)}, u32[]{:S(2)}) collective-permute-start(bf16[112,1152]{1,0:T(8,128)(2,1)S(1)} %get-tuple-element.20.q_hi), channel_id=1, source_target_pairs={{0,2},{1,3},{2,0},{3,1},{4,6},{5,7},{6,4},{7,5},{8,10},{9,11},{10,... | collective-permute-start | bytes 774152 | tf_op jit(solution)/shard_map/chip_hi/ppermute | solution.py:237
  25.4 24.4 %collective-permute-start.6 = (bf16[224,1152]{1,0:T(8,128)(2,1)S(1)}, bf16[224,1152]{1,0:T(8,128)(2,1)S(1)}, u32[]{:S(2)}, u32[]{:S(2)}) collective-permute-start(bf16[224,1152]{1,0:T(8,128)(2,1)S(1)} %unit_p.1.p), channel_id=1, source_target_pairs={{0,2},{1,3},{2,0},{3,1},{4,6},{5,7},{6,4},{7,5},{8,10},{9,11},{10,... | collective-permute-start | bytes 1548296 | tf_op jit(solution)/shard_map/chip_p/ppermute | solution.py:237
  28.7 21.0 %collective-permute-start.4 = (bf16[112,1152]{1,0:T(8,128)(2,1)S(1)}, bf16[112,1152]{1,0:T(8,128)(2,1)}, u32[]{:S(2)}, u32[]{:S(2)}) collective-permute-start(bf16[112,1152]{1,0:T(8,128)(2,1)S(1)} %collective-permute-done.x2_lo), channel_id=1, source_target_pairs={{0,510},{1,511},{2,4},{3,5},{4,2},{5,3},{6,8},{7,9},{8,6},{9,7},{1... | collective-permute-start | bytes 774152 | tf_op jit(solution)/shard_map/group_lo/ppermute | solution.py:237
  34.4 15.4 %collective-permute-start.5 = (bf16[112,1152]{1,0:T(8,128)(2,1)}, bf16[112,1152]{1,0:T(8,128)(2,1)}, u32[]{:S(2)}, u32[]{:S(2)}) collective-permute-start(bf16[112,1152]{1,0:T(8,128)(2,1)} %collective-permute-done.1.x2_hi), channel_id=1, source_target_pairs={{0,510},{1,511},{2,4},{3,5},{4,2},{5,3},{6,8},{7,9},{8,6},{9,7},{1... | collective-permute-start | bytes 774152 | tf_op jit(solution)/shard_map/group_hi/ppermute | solution.py:237
  40.6 14.1 %collective-permute-start.3 = (bf16[896,1152]{1,0:T(8,128)(2,1)S(1)}, bf16[896,1152]{1,0:T(8,128)(2,1)}, u32[]{:S(2)}, u32[]{:S(2)}) collective-permute-start(bf16[896,1152]{1,0:T(8,128)(2,1)S(1)} %join.1.near), channel_id=1, source_target_pairs={{0,1},{1,0},{2,3},{3,2},{4,5},{5,4},{6,7},{7,6},{8,9},{9,8},{10,11... | collective-permute-start | bytes 6193160 | tf_op jit(solution)/shard_map/core_xy/ppermute | solution.py:237
  50.9 6.9 %collective-permute-start.7 = (bf16[224,1152]{1,0:T(8,128)(2,1)S(1)}, bf16[224,1152]{1,0:T(8,128)(2,1)S(1)}, u32[]{:S(2)}, u32[]{:S(2)}) collective-permute-start(bf16[224,1152]{1,0:T(8,128)(2,1)S(1)} %pair.1.y1), channel_id=1, source_target_pairs={{0,1},{1,0},{2,3},{3,2},{4,5},{5,4},{6,7},{7,6},{8,9},{9,8},{10,11... | collective-permute-start | bytes 1548296 | tf_op jit(solution)/shard_map/core_y/ppermute | solution.py:237
  58.6 15.3 %collective-permute-start.8 = (bf16[224,1152]{1,0:T(8,128)(2,1)S(1)}, bf16[224,1152]{1,0:T(8,128)(2,1)S(1)}, u32[]{:S(2)}, u32[]{:S(2)}) collective-permute-start(bf16[224,1152]{1,0:T(8,128)(2,1)S(1)} %get-tuple-element.26._send), channel_id=1, source_target_pairs={{0,2},{1,3},{2,0},{3,1},{4,6},{5,7},{6,4},{7,5},{8,10},{9,11},{10,... | collective-permute-start | bytes 1548296 | tf_op jit(solution)/shard_map/chip_send/ppermute | solution.py:237
  60.6 8.9 %collective-permute-start.9 = (bf16[112,1152]{1,0:T(8,128)(2,1)S(1)}, bf16[112,1152]{1,0:T(8,128)(2,1)S(1)}, u32[]{:S(2)}, u32[]{:S(2)}) collective-permute-start(bf16[112,1152]{1,0:T(8,128)(2,1)S(1)} %get-tuple-element.29), channel_id=1, source_target_pairs={{0,1},{1,0},{2,3},{3,2},{4,5},{5,4},{6,7},{7,6},{8,9},{9,8},{10,11... | collective-permute-start | bytes 774152 | tf_op jit(solution)/shard_map/core_w_lo/ppermute | solution.py:237
  62.5 7.0 %collective-permute-start.10 = (bf16[112,1152]{1,0:T(8,128)(2,1)S(1)}, bf16[112,1152]{1,0:T(8,128)(2,1)S(1)}, u32[]{:S(2)}, u32[]{:S(2)}) collective-permute-start(bf16[112,1152]{1,0:T(8,128)(2,1)S(1)} %get-tuple-element.30), channel_id=1, source_target_pairs={{0,1},{1,0},{2,3},{3,2},{4,5},{5,4},{6,7},{7,6},{8,9},{9,8},{10,11... | collective-permute-start | bytes 774152 | tf_op jit(solution)/shard_map/core_w_hi/ppermute | solution.py:237
  64.9 4.6 %copy-start = (bf16[224,1152]{1,0:T(8,128)(2,1)S(1)}, bf16[224,1152]{1,0:T(8,128)(2,1)}, u32[]{:S(2)}) copy-start(bf16[224,1152]{1,0:T(8,128)(2,1)} %img.7) | copy-start | bytes 1548292
  64.9 4.6 %copy-start.1 = (bf16[224,1152]{1,0:T(8,128)(2,1)S(1)}, bf16[224,1152]{1,0:T(8,128)(2,1)}, u32[]{:S(2)}) copy-start(bf16[224,1152]{1,0:T(8,128)(2,1)} %txt.7) | copy-start | bytes 1548292

commit v5 on v4

--- a/solution.py
+++ b/solution.py
@@ -11,7 +11,7 @@
 HBM = pl.BlockSpec(memory_space=pltpu.HBM)
 NT = (((1,), (1,)), ((), ()))
 NN = (((1,), (0,)), ((), ()))
-COST = {"pair": 16 * 10**9, "late": 8 * 10**9, "rest": 1 * 10**9, "last": 16 * 10**9}
+COST = {"unit": 16 * 10**9, "take": 64 * 10**9, "last": 64 * 10**9}
 
 
 def pieces_of(rows):
@@ -45,41 +45,40 @@
     )
 
 
-def unit_rows(take_txt, img, txt, outs, raw, sems):
-    pieces = pieces_of(img.shape[0])
-
-    def go(ref):
-        copies = []
-        for j, (start, size) in enumerate(pieces):
-            part = pl.ds(start, size)
-            copies.append(pltpu.make_async_copy(ref.at[part], raw.at[part], sems.at[j]))
-            copies[-1].start()
-        for copy, (start, size) in zip(copies, pieces):
-            copy.wait()
-            values = raw[pl.ds(start, size)].astype(jnp.float32)
-            out = outs[start // outs[0].shape[0]]
-            into = pl.ds(start % out.shape[0], size)
-            out[into] = (values * inv_norm(values)).astype(jnp.bfloat16)
-
-    @pl.when(jnp.logical_not(take_txt))
-    def _():
-        go(img)
-
-    @pl.when(take_txt)
-    def _():
-        go(txt)
-
-
-def unit_p_body(odd, img, txt, p, raw, sems):
-    unit_rows(odd[0] == 1, img, txt, [p], raw, sems)
-
-
-def unit_q_body(odd, img, txt, q_lo, q_hi, raw, sems):
-    unit_rows(odd[0] == 0, img, txt, [q_lo, q_hi], raw, sems)
-
-
-def match_body(here, scale, shift, pos, sc, u_p, v_p, u_q, v_q):
+def unit_body(here, img, txt, p, q, raw, sems):
+    half = img.shape[0] // 2
+    copies = []
+    for j in range(2):
+        part = pl.ds(j * half, half)
+        for i, ref in enumerate((img, txt)):
+            copies.append(
+                pltpu.make_async_copy(ref.at[part], raw.at[i, part], sems.at[2 * j + i])
+            )
+    for copy in copies:
+        copy.start()
+    for j in range(2):
+        part = pl.ds(j * half, half)
+        unit = []
+        for i in range(2):
+            copies[2 * j + i].wait()
+            values = raw[i, part].astype(jnp.float32)
+            unit.append((values * inv_norm(values)).astype(jnp.bfloat16))
+
+        @pl.when(here[0] < 2)
+        def _():
+            p[part] = unit[0]
+            q[part] = unit[1]
+
+        @pl.when(here[0] >= 2)
+        def _():
+            p[part] = unit[1]
+            q[part] = unit[0]
+
+
+def match_body(here, scale, shift, pos_far, sc, u_p, v_p, u_q, v_q, pos, sem):
     rows = u_p.shape[0]
+    copy = pltpu.make_async_copy(pos_far, pos, sem)
+    copy.start()
     sc[0:1] = jnp.full((1, sc.shape[1]), scale[0], jnp.float32)
     sc[1:2] = jnp.full((1, sc.shape[1]), shift[0], jnp.float32)
     me = here[0]
@@ -93,11 +92,16 @@
         spread = jnp.where(diagonal, jnp.broadcast_to(row, square).astype(jnp.float32), 0.0)
         return jnp.sum(spread, axis=1, keepdims=True).astype(jnp.int32)
 
+    copy.wait()
+    blocks = [pos[:, k * rows : (k + 1) * rows] for k in range(4)]
     matches, places = [], []
     for j in range(4):
-        block = me ^ j
-        matches.append(pos[pl.ds(block, 1)])
-        places.append(block * rows + lane)
+        them = me ^ j
+        match = blocks[0]
+        for k in range(1, 4):
+            match = jnp.where(them == k, blocks[k], match)
+        matches.append(match)
+        places.append(them * rows + lane)
 
     def put(u_img, v_img, u_txt, v_txt):
         u_img[...] = column(matches[0])
@@ -128,11 +132,10 @@
     return total
 
 
-def join_body(p, q_lo, q_hi, x2_lo, x2_hi, y0, out):
-    row = 0
-    for part in (p, q_lo, q_hi, x2_lo, x2_hi, y0):
-        out[pl.ds(row, part.shape[0])] = part[...]
-        row += part.shape[0]
+def join_body(p, q, x2, y0, out):
+    rows = p.shape[0]
+    for j, part in enumerate((p, q, x2, y0)):
+        out[j * rows : (j + 1) * rows] = part[...]
 
 
 def own_body(sc, near, u_p, v_p, u_q, v_q, sum_p, sum_q):
@@ -141,10 +144,8 @@
     sum_q[...] = terms(y, [x, x2], sc, (u_q[...], [v_q[0:1], v_q[2:3]]))
 
 
-def pair_body(y_lo, y_hi, _w2, _sum, y1):
-    half = y_lo.shape[0]
-    y1[:half] = y_lo[...]
-    y1[half:] = y_hi[...]
+def take_body(y, _sum, out):
+    out[...] = y[...]
 
 
 def block(ref, j):
@@ -205,19 +206,19 @@
 
 
 def rest_body(
-    sc, odd, img, txt, p, w2_lo_c, w2_hi_c, u_p, v_p, sum_p, img_grad, txt_grad, total, held, sems
+    sc, here, img, txt, p, w2_lo_c, w2_hi_c, u_p, v_p, sum_p, img_grad, txt_grad, total, held, sems
 ):
     half = p.shape[0] // 2
     own = (u_p[...], [v_p[3:4, :half], v_p[3:4, half:]])
     total[...] = sum_p[...] + terms(p[...], [w2_lo_c[...], w2_hi_c[...]], sc, own)
-    write_out(odd[0] == 1, img, txt, lambda part: total[part], img_grad, txt_grad, held, sems)
-
-
-def last_body(odd, img, txt, sum_q, back, _img, _txt, img_grad, txt_grad, held, sems):
+    write_out(here[0] >= 2, img, txt, lambda part: total[part], img_grad, txt_grad, held, sems)
+
+
+def last_body(here, img, txt, sum_q, back, _img, _txt, img_grad, txt_grad, held, sems):
     def dunit(part):
         return sum_q[part] + back[part].astype(jnp.float32)
 
-    write_out(odd[0] == 0, img, txt, dunit, img_grad, txt_grad, held, sems)
+    write_out(here[0] < 2, img, txt, dunit, img_grad, txt_grad, held, sems)
 
 
 def local(picture_vectors, caption_vectors, caption_position, sharpness_factor, affine_offset):
@@ -246,32 +247,34 @@
         return jax.ShapeDtypeStruct(shape, dtype)
 
     here = lax.axis_index("narrow").astype(jnp.int32).reshape(1)
-    odd = here // 2
     bf16 = jnp.bfloat16
     one, wide = of((rows, depth), bf16), of((rows, depth))
     part, four = of((half, depth), bf16), of((4 * rows, depth), bf16)
     dma = pltpu.SemaphoreType.DMA
     far = lambda x: pltpu.with_memory_space_constraint(x, pltpu.HBM)
 
-    img_far, txt_far = far(img), far(txt)
-    scratch = [pltpu.VMEM((rows, depth), bf16), dma((4,))]
-    p = call(unit_p_body, one, [SMEM, HBM, HBM], scratch_shapes=scratch)(odd, img_far, txt_far)
-    q_lo, q_hi = call(unit_q_body, (part, part), [SMEM, HBM, HBM], scratch_shapes=scratch)(
-        odd, img_far, txt_far
-    )
+    p, q = call(
+        unit_body,
+        (one, one),
+        [SMEM, HBM, HBM],
+        scratch_shapes=[pltpu.VMEM((2, rows, depth), bf16), dma((4,))],
+    )(here, far(img), far(txt))
+    x2 = chip(q, "chip_q")
     y0 = group(p, "group_p")
-    x2_lo, x2_hi = chip(q_lo, "chip_lo"), chip(q_hi, "chip_hi")
+    y1 = group(x2, "group_x2")
     w2 = chip(p, "chip_p")
-    y_lo, y_hi = group(x2_lo, "group_lo"), group(x2_hi, "group_hi")
 
     place = (of((rows, 1), jnp.int32), of((4, rows), jnp.int32))
-    sc, *match = call(match_body, (of((2, 128)),) + place + place, [SMEM] * 3 + [VMEM])(
-        here, scale, shift, caption_position.reshape(4, rows)
-    )
-    near = call(join_body, four, [VMEM] * 6)(p, q_lo, q_hi, x2_lo, x2_hi, y0)
+    sc, *match = call(
+        match_body,
+        (of((2, 128)),) + place + place,
+        [SMEM] * 3 + [HBM],
+        scratch_shapes=[pltpu.VMEM((1, 4 * rows), jnp.int32), dma],
+    )(here, scale, shift, far(caption_position))
+    near = call(join_body, four, [VMEM] * 4)(p, q, x2, y0)
     near_c = core(near, "core_xy")
     own_p, own_q = call(own_body, (wide, wide), [VMEM] * 6)(sc, near, *match)
-    y1 = call(pair_body, one, [VMEM] * 4)(y_lo, y_hi, w2, own_q)
+    y1 = call(take_body, one, [VMEM] * 2)(y1, own_q)
     y1_c = core(y1, "core_y")
     part_x = call(mid_body, wide, [VMEM] * 4)(sc, near, near_c, y1)
     send, w2_lo, w2_hi = call(late_body, (one, part, part), [VMEM] * 5)(
@@ -288,7 +291,7 @@
         [VMEM, SMEM] + [VMEM] * 8,
         (HBM, HBM),
         scratch_shapes=[pltpu.VMEM((rows, depth), jnp.float32)] + out,
-    )(sc, odd, img, txt, p, core(w2_lo, "core_w_lo"), core(w2_hi, "core_w_hi"), *match[:2], sum_p)
+    )(sc, here, img, txt, p, core(w2_lo, "core_w_lo"), core(w2_hi, "core_w_hi"), *match[:2], sum_p)
     return call(
         last_body,
         (wide, wide),
@@ -296,7 +299,7 @@
         (HBM, HBM),
         scratch_shapes=out,
         input_output_aliases={5: 0, 6: 1},
-    )(odd, img, txt, sum_q, back, *grads)
+    )(here, img, txt, sum_q, back, *grads)
 
 
 def solution(mesh):

time: 75.8 us -> 67 us (0.88)
  Pallas kernels: 18.8 us -> 13.2 us
  waiting for transfers between devices: 7.17 us -> 4.16 us
    ppermute x11 -> x9, waiting for transfers between devices: 7.17 us -> 4.16 us  [go(): return lax.ppermute(x, AXES, pairs)]
    pallas_call x5 -> x4, Pallas kernels: 5.22 us -> 2.93 us  [the longest x1 1.65 us: local(): call(unit_body, (one, one), [SMEM, HBM, HBM], scratch_shapes=[pltpu.VMEM(...]
    pallas_call x1, Pallas kernels: 4.5 us -> 2.85 us  [local(): call(visit_body, (wide, wide), [VMEM] * 13)]
    pallas_call x1, Pallas kernels: 3.03 us -> 1.43 us  [local(): part_x = call(mid_body, wide, [VMEM] * 4)(sc, near, near_c, y1)]
    ppermute x11 -> x9, starting transfers between devices: 47 us -> 47.1 us  [go(): return lax.ppermute(x, AXES, pairs)]
  transfers between devices with their start and end apart: 11 -> 9, of which waited for: 3 -> 2; matrix products, arithmetic and copies ran while one was open for 0% -> 0% of each run, Pallas kernels for 20% -> 14%
where the time goes in v5:
time: 67 us; the launch traced here: 66.6 us
  starting transfers between devices  47.1 us (70%)
  Pallas kernels  13.2 us (20%)
  waiting for transfers between devices  4.16 us (6%)
  between operations  2.14 us (3%)
    ppermute x9, starting transfers between devices, go(): return lax.ppermute(x, AXES, pairs)  47.1 us
    ppermute x9, waiting for transfers between devices, go(): return lax.ppermute(x, AXES, pairs)  4.16 us
    pallas_call x1, Pallas kernels, local(): call(visit_body, (wide, wide), [VMEM] * 13)  2.85 us
    pallas_call x1, Pallas kernels, local(): call(rest_body, (wide, wide), [VMEM, SMEM] + [VMEM] * 8, (HBM, HBM), scra...  2.09 us
    pallas_call x1, Pallas kernels, local(): own_p, own_q = call(own_body, (wide, wide), [VMEM] * 6)(sc, near, *match)  1.73 us
    pallas_call x1, Pallas kernels, local(): call(unit_body, (one, one), [SMEM, HBM, HBM], scratch_shapes=[pltpu.VMEM(...  1.65 us
    pallas_call x1, Pallas kernels, local(): part_x = call(mid_body, wide, [VMEM] * 4)(sc, near, near_c, y1)  1.43 us
  transfers between devices with their start and end apart: 9, of which 2 were waited for; matrix products, arithmetic and copies ran while one was open for 0% of the time, Pallas kernels for 14%

profile of v5, /device:TPU:1, one launch (start us, length us, event | category | flops | bytes accessed | tf_op | source)
XLA Modules:
  0.0 66.6 jit_solution(10067517190167732909)
XLA Ops:
  0.6 1.6 %unit.1 = (bf16[224,1152]{1,0:T(8,128)(2,1)S(1)}, bf16[224,1152]{1,0:T(8,128)(2,1)S(1)}) custom-call(s32[1]{0:T(128)} %bitcast.here, bf16[224,1152]{1,0:T(8,128)(2,1)} %img.5, bf16[224,1152]{1,0:T(8,128)(2,1)} %txt.5), custom_call_target="tpu_custom_call" | custom-call | flops 16000000000 | bytes 1 | tf_op jit(solution)/shard_map/unit/pallas_call | solution.py:256
  2.3 4.8 %collective-permute-start = (bf16[224,1152]{1,0:T(8,128)(2,1)S(1)}, bf16[224,1152]{1,0:T(8,128)(2,1)S(1)}, u32[]{:S(2)}, u32[]{:S(2)}) collective-permute-start(bf16[224,1152]{1,0:T(8,128)(2,1)S(1)} %get-tuple-element.20.q), channel_id=1, source_target_pairs={{0,2},{1,3},{2,0},{3,1},{4,6},{5,7},{6,4},{7,5},{8,10},{9,11},{10,... | collective-permute-start | bytes 1548296 | tf_op jit(solution)/shard_map/chip_q/ppermute | solution.py:238
  7.1 14.0 %collective-permute-start.1 = (bf16[224,1152]{1,0:T(8,128)(2,1)S(1)}, bf16[224,1152]{1,0:T(8,128)(2,1)S(1)}, u32[]{:S(2)}, u32[]{:S(2)}) collective-permute-start(bf16[224,1152]{1,0:T(8,128)(2,1)S(1)} %get-tuple-element.19.p), channel_id=1, source_target_pairs={{0,510},{1,511},{2,4},{3,5},{4,2},{5,3},{6,8},{7,9},{8,6},{9,7},{1... | collective-permute-start | bytes 1548296 | tf_op jit(solution)/shard_map/group_p/ppermute | solution.py:238
  21.1 0.0 collective-permute-done.x2
  21.1 12.3 %collective-permute-start.3 = (bf16[224,1152]{1,0:T(8,128)(2,1)S(1)}, bf16[224,1152]{1,0:T(8,128)(2,1)S(1)}, u32[]{:S(2)}, u32[]{:S(2)}) collective-permute-start(bf16[224,1152]{1,0:T(8,128)(2,1)S(1)} %collective-permute-done.x2), channel_id=1, source_target_pairs={{0,510},{1,511},{2,4},{3,5},{4,2},{5,3},{6,8},{7,9},{8,6},{9,7},{1... | collective-permute-start | bytes 1548296 | tf_op jit(solution)/shard_map/group_x2/ppermute | solution.py:238
  33.4 1.9 %collective-permute-start.5 = (bf16[224,1152]{1,0:T(8,128)(2,1)S(1)}, bf16[224,1152]{1,0:T(8,128)(2,1)S(1)}, u32[]{:S(2)}, u32[]{:S(2)}) collective-permute-start(bf16[224,1152]{1,0:T(8,128)(2,1)S(1)} %get-tuple-element.19.p), channel_id=1, source_target_pairs={{0,2},{1,3},{2,0},{3,1},{4,6},{5,7},{6,4},{7,5},{8,10},{9,11},{10,... | collective-permute-start | bytes 1548296 | tf_op jit(solution)/shard_map/chip_p/ppermute | solution.py:238
  36.6 1.1 %match.1 = (f32[2,128]{1,0:T(2,128)S(1)}, s32[224,1]{1,0:T(8,128)S(1)}, s32[4,224]{1,0:T(4,128)S(1)}, s32[224,1]{1,0:T(8,128)S(1)}, s32[4,224]{1,0:T(4,128)S(1)}) custom-call(s32[1]{0:T(128)} %bitcast.here, f32[1]{0:T(128)S(6)} %copy.11.scale, f32[1]{0:T(128)S(6)} %copy.12.shift, s32[1,896]{1,0:T(1,128)} %pos_far.1), custom_call_target="tpu_custom_call" | custom-call | flops 1 | bytes 1 | tf_op jit(solution)/shard_map/match/pallas_call | solution.py:268
  37.7 0.0 collective-permute-done.1.y0
  37.7 0.2 join.1.near
  37.9 3.7 %collective-permute-start.2 = (bf16[896,1152]{1,0:T(8,128)(2,1)S(1)}, bf16[896,1152]{1,0:T(8,128)(2,1)S(1)}, u32[]{:S(2)}, u32[]{:S(2)}) collective-permute-start(bf16[896,1152]{1,0:T(8,128)(2,1)S(1)} %join.1.near), channel_id=1, source_target_pairs={{0,1},{1,0},{2,3},{3,2},{4,5},{5,4},{6,7},{7,6},{8,9},{9,8},{10,11... | collective-permute-start | bytes 6193160 | tf_op jit(solution)/shard_map/core_xy/ppermute | solution.py:238
  41.6 1.7 %own.1 = (f32[224,1152]{1,0:T(8,128)S(1)}, f32[224,1152]{1,0:T(8,128)S(1)}) custom-call(f32[2,128]{1,0:T(2,128)S(1)} %get-tuple-element.18.sc, bf16[896,1152]{1,0:T(8,128)(2,1)S(1)} %join.1.near, s32[224,1]{1,0:T(8,128)S(1)} %get-tuple-element.21.u_p, s32[4,224]{1,0:T(4,128)S(1)} %get-tuple-element.22.v_p, s32[224,1]{1,0:T(8,128)S(1)} %get-tuple-element.23.u_q, ...), custom_call_target="tpu_custom_call" | custom-call | flops 1 | bytes 1 | tf_op jit(solution)/shard_map/own/pallas_call | solution.py:276
  43.4 0.5 collective-permute-done.3.y
  43.9 4.1 %collective-permute-start.4 = (bf16[224,1152]{1,0:T(8,128)(2,1)S(1)}, bf16[224,1152]{1,0:T(8,128)(2,1)S(1)}, u32[]{:S(2)}, u32[]{:S(2)}) collective-permute-start(bf16[224,1152]{1,0:T(8,128)(2,1)S(1)} %take.1.y1), channel_id=1, source_target_pairs={{0,1},{1,0},{2,3},{3,2},{4,5},{5,4},{6,7},{7,6},{8,9},{9,8},{10,11... | collective-permute-start | bytes 1548296 | tf_op jit(solution)/shard_map/core_y/ppermute | solution.py:238
  48.0 0.0 collective-permute-done.2.near_c
  48.0 1.4 %mid.1.part = f32[224,1152]{1,0:T(8,128)S(1)} custom-call(f32[2,128]{1,0:T(2,128)S(1)} %get-tuple-element.18.sc, bf16[896,1152]{1,0:T(8,128)(2,1)S(1)} %join.1.near, bf16[896,1152]{1,0:T(8,128)(2,1)S(1)} %collective-permute-done.2.near_c, bf16[224,1152]{1,0:T(8,128)(2,1)S(1)} %take.1.y1), custom_call_target="tpu_custom_call" | custom-call | flops 1 | bytes 1 | tf_op jit(solution)/shard_map/mid/pallas_call | solution.py:279
  49.5 0.0 collective-permute-done.5.w2
  49.5 0.0 collective-permute-done.4.y1_c
  49.5 0.9 %late.1 = (bf16[224,1152]{1,0:T(8,128)(2,1)S(1)}, bf16[112,1152]{1,0:T(8,128)(2,1)S(1)}, bf16[112,1152]{1,0:T(8,128)(2,1)S(1)}) custom-call(f32[2,128]{1,0:T(2,128)S(1)} %get-tuple-element.18.sc, bf16[896,1152]{1,0:T(8,128)(2,1)S(1)} %join.1.near, bf16[224,1152]{1,0:T(8,128)(2,1)S(1)} %collective-permute-done.4.y1_c, f32[224,1152]{1,0:T(8,128)S(1)} %mid.1.part, ...), custom_call_target="tpu_custom_call" | custom-call | flops 1 | bytes 1 | tf_op jit(solution)/shard_map/late/pallas_call | solution.py:280
  50.4 1.9 %collective-permute-start.6 = (bf16[224,1152]{1,0:T(8,128)(2,1)S(1)}, bf16[224,1152]{1,0:T(8,128)(2,1)S(1)}, u32[]{:S(2)}, u32[]{:S(2)}) collective-permute-start(bf16[224,1152]{1,0:T(8,128)(2,1)S(1)} %get-tuple-element.26._send), channel_id=1, source_target_pairs={{0,2},{1,3},{2,0},{3,1},{4,6},{5,7},{6,4},{7,5},{8,10},{9,11},{10,... | collective-permute-start | bytes 1548296 | tf_op jit(solution)/shard_map/chip_send/ppermute | solution.py:238
  52.4 2.3 %collective-permute-start.7 = (bf16[112,1152]{1,0:T(8,128)(2,1)S(1)}, bf16[112,1152]{1,0:T(8,128)(2,1)S(1)}, u32[]{:S(2)}, u32[]{:S(2)}) collective-permute-start(bf16[112,1152]{1,0:T(8,128)(2,1)S(1)} %get-tuple-element.29), channel_id=1, source_target_pairs={{0,1},{1,0},{2,3},{3,2},{4,5},{5,4},{6,7},{7,6},{8,9},{9,8},{10,11... | collective-permute-start | bytes 774152 | tf_op jit(solution)/shard_map/core_w_lo/ppermute | solution.py:238
  54.6 2.0 %collective-permute-start.8 = (bf16[112,1152]{1,0:T(8,128)(2,1)S(1)}, bf16[112,1152]{1,0:T(8,128)(2,1)S(1)}, u32[]{:S(2)}, u32[]{:S(2)}) collective-permute-start(bf16[112,1152]{1,0:T(8,128)(2,1)S(1)} %get-tuple-element.30), channel_id=1, source_target_pairs={{0,1},{1,0},{2,3},{3,2},{4,5},{5,4},{6,7},{7,6},{8,9},{9,8},{10,11... | collective-permute-start | bytes 774152 | tf_op jit(solution)/shard_map/core_w_hi/ppermute | solution.py:238
  56.7 0.0 copy-start
  56.7 0.0 copy-start.1
  56.7 2.8 %visit.1 = (f32[224,1152]{1,0:T(8,128)S(1)}, f32[224,1152]{1,0:T(8,128)S(1)}) custom-call(f32[2,128]{1,0:T(2,128)S(1)} %get-tuple-element.18.sc, bf16[896,1152]{1,0:T(8,128)(2,1)S(1)} %join.1.near, bf16[896,1152]{1,0:T(8,128)(2,1)S(1)} %collective-permute-done.2.near_c, bf16[224,1152]{1,0:T(8,128)(2,1)S(1)} %take.1.y1, ...), custom_call_target="tpu_custom_call" | custom-call | flops 1 | bytes 1 | tf_op jit(solution)/shard_map/visit/pallas_call | solution.py:284
  59.6 0.0 collective-permute-done.7.w2_lo_c
  59.6 0.0 collective-permute-done.8.w2_hi_c
  59.6 0.0 copy-done
  59.6 0.0 copy-done.1
  59.6 2.1 %rest.1 = (f32[224,1152]{1,0:T(8,128)}, f32[224,1152]{1,0:T(8,128)}) custom-call(f32[2,128]{1,0:T(2,128)S(1)} %get-tuple-element.18.sc, s32[1]{0:T(128)} %bitcast.here, bf16[224,1152]{1,0:T(8,128)(2,1)S(1)} %copy-done, bf16[224,1152]{1,0:T(8,128)(2,1)S(1)} %copy-done.1, bf16[224,1152]{1,0:T(8,128)(2,1)S(1)} %get-tuple-element.19.p, ...), custom_call_target="tpu_custom_call" | custom-call | flops 1 | bytes 1 | tf_op jit(solution)/shard_map/rest/pallas_call | solution.py:288
  61.7 3.6 %collective-permute-done.6.back = bf16[224,1152]{1,0:T(8,128)(2,1)S(1)} collective-permute-done((bf16[224,1152]{1,0:T(8,128)(2,1)S(1)}, bf16[224,1152]{1,0:T(8,128)(2,1)S(1)}, u32[]{:S(2)}, u32[]{:S(2)}) %collective-permute-start.6) | collective-permute-done | bytes 516128 | tf_op jit(solution)/shard_map/chip_send/ppermute | solution.py:238
  65.3 1.3 %last.1 = (f32[224,1152]{1,0:T(8,128)}, f32[224,1152]{1,0:T(8,128)}) custom-call(s32[1]{0:T(128)} %bitcast.here, bf16[224,1152]{1,0:T(8,128)(2,1)S(1)} %copy-done, bf16[224,1152]{1,0:T(8,128)(2,1)S(1)} %copy-done.1, f32[224,1152]{1,0:T(8,128)S(1)} %get-tuple-element.28.sum_q, ...), custom_call_target="tpu_custom_call", output_to_operand_aliasing={{0}: (5, {}), {1}: (6, {})} | custom-call | flops 64000000000 | bytes 1 | tf_op jit(solution)/shard_map/last/pallas_call | solution.py:295
  (1 shorter events, 0.0 us)
Async XLA Ops:
  2.3 18.8 %collective-permute-start = (bf16[224,1152]{1,0:T(8,128)(2,1)S(1)}, bf16[224,1152]{1,0:T(8,128)(2,1)S(1)}, u32[]{:S(2)}, u32[]{:S(2)}) collective-permute-start(bf16[224,1152]{1,0:T(8,128)(2,1)S(1)} %get-tuple-element.20.q), channel_id=1, source_target_pairs={{0,2},{1,3},{2,0},{3,1},{4,6},{5,7},{6,4},{7,5},{8,10},{9,11},{10,... | collective-permute-start | bytes 1548296 | tf_op jit(solution)/shard_map/chip_q/ppermute | solution.py:238
  7.1 30.6 %collective-permute-start.1 = (bf16[224,1152]{1,0:T(8,128)(2,1)S(1)}, bf16[224,1152]{1,0:T(8,128)(2,1)S(1)}, u32[]{:S(2)}, u32[]{:S(2)}) collective-permute-start(bf16[224,1152]{1,0:T(8,128)(2,1)S(1)} %get-tuple-element.19.p), channel_id=1, source_target_pairs={{0,510},{1,511},{2,4},{3,5},{4,2},{5,3},{6,8},{7,9},{8,6},{9,7},{1... | collective-permute-start | bytes 1548296 | tf_op jit(solution)/shard_map/group_p/ppermute | solution.py:238
  21.1 22.8 %collective-permute-start.3 = (bf16[224,1152]{1,0:T(8,128)(2,1)S(1)}, bf16[224,1152]{1,0:T(8,128)(2,1)S(1)}, u32[]{:S(2)}, u32[]{:S(2)}) collective-permute-start(bf16[224,1152]{1,0:T(8,128)(2,1)S(1)} %collective-permute-done.x2), channel_id=1, source_target_pairs={{0,510},{1,511},{2,4},{3,5},{4,2},{5,3},{6,8},{7,9},{8,6},{9,7},{1... | collective-permute-start | bytes 1548296 | tf_op jit(solution)/shard_map/group_x2/ppermute | solution.py:238
  33.4 16.1 %collective-permute-start.5 = (bf16[224,1152]{1,0:T(8,128)(2,1)S(1)}, bf16[224,1152]{1,0:T(8,128)(2,1)S(1)}, u32[]{:S(2)}, u32[]{:S(2)}) collective-permute-start(bf16[224,1152]{1,0:T(8,128)(2,1)S(1)} %get-tuple-element.19.p), channel_id=1, source_target_pairs={{0,2},{1,3},{2,0},{3,1},{4,6},{5,7},{6,4},{7,5},{8,10},{9,11},{10,... | collective-permute-start | bytes 1548296 | tf_op jit(solution)/shard_map/chip_p/ppermute | solution.py:238
  37.9 10.2 %collective-permute-start.2 = (bf16[896,1152]{1,0:T(8,128)(2,1)S(1)}, bf16[896,1152]{1,0:T(8,128)(2,1)S(1)}, u32[]{:S(2)}, u32[]{:S(2)}) collective-permute-start(bf16[896,1152]{1,0:T(8,128)(2,1)S(1)} %join.1.near), channel_id=1, source_target_pairs={{0,1},{1,0},{2,3},{3,2},{4,5},{5,4},{6,7},{7,6},{8,9},{9,8},{10,11... | collective-permute-start | bytes 6193160 | tf_op jit(solution)/shard_map/core_xy/ppermute | solution.py:238
  43.9 5.6 %collective-permute-start.4 = (bf16[224,1152]{1,0:T(8,128)(2,1)S(1)}, bf16[224,1152]{1,0:T(8,128)(2,1)S(1)}, u32[]{:S(2)}, u32[]{:S(2)}) collective-permute-start(bf16[224,1152]{1,0:T(8,128)(2,1)S(1)} %take.1.y1), channel_id=1, source_target_pairs={{0,1},{1,0},{2,3},{3,2},{4,5},{5,4},{6,7},{7,6},{8,9},{9,8},{10,11... | collective-permute-start | bytes 1548296 | tf_op jit(solution)/shard_map/core_y/ppermute | solution.py:238
  50.4 14.9 %collective-permute-start.6 = (bf16[224,1152]{1,0:T(8,128)(2,1)S(1)}, bf16[224,1152]{1,0:T(8,128)(2,1)S(1)}, u32[]{:S(2)}, u32[]{:S(2)}) collective-permute-start(bf16[224,1152]{1,0:T(8,128)(2,1)S(1)} %get-tuple-element.26._send), channel_id=1, source_target_pairs={{0,2},{1,3},{2,0},{3,1},{4,6},{5,7},{6,4},{7,5},{8,10},{9,11},{10,... | collective-permute-start | bytes 1548296 | tf_op jit(solution)/shard_map/chip_send/ppermute | solution.py:238
  52.4 7.2 %collective-permute-start.7 = (bf16[112,1152]{1,0:T(8,128)(2,1)S(1)}, bf16[112,1152]{1,0:T(8,128)(2,1)S(1)}, u32[]{:S(2)}, u32[]{:S(2)}) collective-permute-start(bf16[112,1152]{1,0:T(8,128)(2,1)S(1)} %get-tuple-element.29), channel_id=1, source_target_pairs={{0,1},{1,0},{2,3},{3,2},{4,5},{5,4},{6,7},{7,6},{8,9},{9,8},{10,11... | collective-permute-start | bytes 774152 | tf_op jit(solution)/shard_map/core_w_lo/ppermute | solution.py:238
  54.6 4.9 %collective-permute-start.8 = (bf16[112,1152]{1,0:T(8,128)(2,1)S(1)}, bf16[112,1152]{1,0:T(8,128)(2,1)S(1)}, u32[]{:S(2)}, u32[]{:S(2)}) collective-permute-start(bf16[112,1152]{1,0:T(8,128)(2,1)S(1)} %get-tuple-element.30), channel_id=1, source_target_pairs={{0,1},{1,0},{2,3},{3,2},{4,5},{5,4},{6,7},{7,6},{8,9},{9,8},{10,11... | collective-permute-start | bytes 774152 | tf_op jit(solution)/shard_map/core_w_hi/ppermute | solution.py:238
  56.7 2.9 %copy-start = (bf16[224,1152]{1,0:T(8,128)(2,1)S(1)}, bf16[224,1152]{1,0:T(8,128)(2,1)}, u32[]{:S(2)}) copy-start(bf16[224,1152]{1,0:T(8,128)(2,1)} %img.5) | copy-start | bytes 1548292
  56.7 2.9 %copy-start.1 = (bf16[224,1152]{1,0:T(8,128)(2,1)S(1)}, bf16[224,1152]{1,0:T(8,128)(2,1)}, u32[]{:S(2)}) copy-start(bf16[224,1152]{1,0:T(8,128)(2,1)} %txt.5) | copy-start | bytes 1548292

commit v6 on v5

--- a/solution.py
+++ b/solution.py
@@ -11,7 +11,11 @@
 HBM = pl.BlockSpec(memory_space=pltpu.HBM)
 NT = (((1,), (1,)), ((), ()))
 NN = (((1,), (0,)), ((), ()))
-COST = {"unit": 16 * 10**9, "take": 64 * 10**9, "last": 64 * 10**9}
+COST = {
+    "unit": 16 * 10**9,
+    "take": 64 * 10**9,
+    "last": 64 * 10**9,
+}
 
 
 def pieces_of(rows):
@@ -157,10 +161,25 @@
     part[...] = terms(block(near, 2), [block(near, 3), block(near_c, 3), y1[...]], sc)
 
 
-def late_body(sc, near, y1_c, part, w2, out, w2_lo, w2_hi):
-    half = w2_lo.shape[0]
-    w2_lo[...] = w2[:half]
-    w2_hi[...] = w2[half:]
+def far_sums(sc, near, near_c, y1, y1_c, w2, u_p, v_p, u_q, v_q, own_p, own_q, sum_p, sum_q):
+    x, y = block(near, 0), block(near, 1)
+    x_c, y_c, x2_c, y0_c = (block(near_c, j) for j in range(4))
+    sum_p[...] = (
+        own_p[...]
+        + terms(x, [y_c, w2[...]], sc, (u_p[...], [v_p[1:2], v_p[2:3]]))
+        + terms(x, [y0_c, y1[...], y1_c[...]], sc)
+    )
+    own = (u_q[...], [v_q[1:2], v_q[3:4]])
+    sum_q[...] = own_q[...] + terms(y, [x_c, x2_c], sc, own)
+
+
+def late_body(here, part, sc, near, near_c, y1, y1_c, *rest):
+    out, sum_p, sum_q = rest[-3:]
+
+    @pl.when(here[0] % 2 == 0)
+    def _():
+        far_sums(sc, near, near_c, y1, y1_c, *rest[:-3], sum_p, sum_q)
+
     out[...] = (part[...] + terms(block(near, 2), [y1_c[...]], sc)).astype(out.dtype)
 
 
@@ -191,18 +210,15 @@
         go(txt, txt_grad)
 
 
-def visit_body(
-    sc, near, near_c, y1, y1_c, w2, _send, u_p, v_p, u_q, v_q, own_p, own_q, sum_p, sum_q
-):
-    x, y = block(near, 0), block(near, 1)
-    x_c, y_c, x2_c, y0_c = (block(near_c, j) for j in range(4))
-    sum_p[...] = (
-        own_p[...]
-        + terms(x, [y_c, w2[...]], sc, (u_p[...], [v_p[1:2], v_p[2:3]]))
-        + terms(x, [y0_c, y1[...], y1_c[...]], sc)
-    )
-    own = (u_q[...], [v_q[1:2], v_q[3:4]])
-    sum_q[...] = own_q[...] + terms(y, [x_c, x2_c], sc, own)
+def visit_body(here, _send, _sum_p, _sum_q, sc, near, near_c, y1, y1_c, w2, *rest):
+    sum_p, sum_q, w2_lo, w2_hi = rest[-4:]
+    half = w2_lo.shape[0]
+    w2_lo[...] = w2[:half]
+    w2_hi[...] = w2[half:]
+
+    @pl.when(here[0] % 2 == 1)
+    def _():
+        far_sums(sc, near, near_c, y1, y1_c, w2, *rest[:-4], sum_p, sum_q)
 
 
 def rest_body(
@@ -277,13 +293,17 @@
     y1 = call(take_body, one, [VMEM] * 2)(y1, own_q)
     y1_c = core(y1, "core_y")
     part_x = call(mid_body, wide, [VMEM] * 4)(sc, near, near_c, y1)
-    send, w2_lo, w2_hi = call(late_body, (one, part, part), [VMEM] * 5)(
-        sc, near, y1_c, part_x, w2
+    blocks = (sc, near, near_c, y1, y1_c, w2, *match, own_p, own_q)
+    send, sum_p, sum_q = call(late_body, (one, wide, wide), [SMEM] + [VMEM] * 13)(
+        here, part_x, *blocks
     )
     back = chip(send, "chip_send")
-    sum_p, sum_q = call(visit_body, (wide, wide), [VMEM] * 13)(
-        sc, near, near_c, y1, y1_c, w2, send, *match, own_p, own_q
-    )
+    sum_p, sum_q, w2_lo, w2_hi = call(
+        visit_body,
+        (wide, wide, part, part),
+        [SMEM] + [VMEM] * 15,
+        input_output_aliases={2: 0, 3: 1},
+    )(here, send, sum_p, sum_q, *blocks)
     out = [pltpu.VMEM((rows, depth), jnp.float32), dma((4,))]
     grads = call(
         rest_body,

time: 67 us -> 64.9 us (0.969)
  waiting for transfers between devices: 4.16 us -> 2.06 us
    ppermute x9, waiting for transfers between devices: 4.16 us -> 2.06 us  [go(): return lax.ppermute(x, AXES, pairs)]
  transfers between devices with their start and end apart: 9 -> 9, of which waited for: 2 -> 2; matrix products, arithmetic and copies ran while one was open for 0% -> 0% of each run, Pallas kernels for 14% -> 15%
where the time goes in v6:
time: 64.9 us; the launch traced here: 64.5 us
  starting transfers between devices  47.1 us (73%)
  Pallas kernels  13.2 us (20%)
  between operations  2.12 us (3%)
  waiting for transfers between devices  2.06 us (3%)
    ppermute x9, starting transfers between devices, go(): return lax.ppermute(x, AXES, pairs)  47.1 us
    pallas_call x1, Pallas kernels, local(): call(visit_body, (wide, wide, part, part), [SMEM] + [VMEM] * 15, input_ou...  2.84 us
    pallas_call x1, Pallas kernels, local(): call(rest_body, (wide, wide), [VMEM, SMEM] + [VMEM] * 8, (HBM, HBM), scra...  2.1 us
    ppermute x9, waiting for transfers between devices, go(): return lax.ppermute(x, AXES, pairs)  2.06 us
    pallas_call x1, Pallas kernels, local(): own_p, own_q = call(own_body, (wide, wide), [VMEM] * 6)(sc, near, *match)  1.73 us
    pallas_call x1, Pallas kernels, local(): call(unit_body, (one, one), [SMEM, HBM, HBM], scratch_shapes=[pltpu.VMEM(...  1.65 us
    pallas_call x1, Pallas kernels, local(): part_x = call(mid_body, wide, [VMEM] * 4)(sc, near, near_c, y1)  1.44 us
    pallas_call x1, Pallas kernels, local(): call(last_body, (wide, wide), [SMEM] + [VMEM] * 4 + [HBM] * 2, (HBM, HBM)...  1.32 us
  transfers between devices with their start and end apart: 9, of which 2 were waited for; matrix products, arithmetic and copies ran while one was open for 0% of the time, Pallas kernels for 15%

profile of v6, /device:TPU:1, one launch (start us, length us, event | category | flops | bytes accessed | tf_op | source)
XLA Modules:
  0.0 64.5 jit_solution(13690401075306280968)
XLA Ops:
  0.6 1.6 %unit.1 = (bf16[224,1152]{1,0:T(8,128)(2,1)S(1)}, bf16[224,1152]{1,0:T(8,128)(2,1)S(1)}) custom-call(s32[1]{0:T(128)} %bitcast.here, bf16[224,1152]{1,0:T(8,128)(2,1)} %img.5, bf16[224,1152]{1,0:T(8,128)(2,1)} %txt.5), custom_call_target="tpu_custom_call" | custom-call | flops 16000000000 | bytes 1 | tf_op jit(solution)/shard_map/unit/pallas_call | solution.py:272
  2.3 4.8 %collective-permute-start = (bf16[224,1152]{1,0:T(8,128)(2,1)S(1)}, bf16[224,1152]{1,0:T(8,128)(2,1)S(1)}, u32[]{:S(2)}, u32[]{:S(2)}) collective-permute-start(bf16[224,1152]{1,0:T(8,128)(2,1)S(1)} %get-tuple-element.22.q), channel_id=1, source_target_pairs={{0,2},{1,3},{2,0},{3,1},{4,6},{5,7},{6,4},{7,5},{8,10},{9,11},{10,... | collective-permute-start | bytes 1548296 | tf_op jit(solution)/shard_map/chip_q/ppermute | solution.py:254
  7.1 14.0 %collective-permute-start.1 = (bf16[224,1152]{1,0:T(8,128)(2,1)S(1)}, bf16[224,1152]{1,0:T(8,128)(2,1)S(1)}, u32[]{:S(2)}, u32[]{:S(2)}) collective-permute-start(bf16[224,1152]{1,0:T(8,128)(2,1)S(1)} %get-tuple-element.21.p), channel_id=1, source_target_pairs={{0,510},{1,511},{2,4},{3,5},{4,2},{5,3},{6,8},{7,9},{8,6},{9,7},{1... | collective-permute-start | bytes 1548296 | tf_op jit(solution)/shard_map/group_p/ppermute | solution.py:254
  21.1 0.0 collective-permute-done.x2
  21.1 12.3 %collective-permute-start.3 = (bf16[224,1152]{1,0:T(8,128)(2,1)S(1)}, bf16[224,1152]{1,0:T(8,128)(2,1)S(1)}, u32[]{:S(2)}, u32[]{:S(2)}) collective-permute-start(bf16[224,1152]{1,0:T(8,128)(2,1)S(1)} %collective-permute-done.x2), channel_id=1, source_target_pairs={{0,510},{1,511},{2,4},{3,5},{4,2},{5,3},{6,8},{7,9},{8,6},{9,7},{1... | collective-permute-start | bytes 1548296 | tf_op jit(solution)/shard_map/group_x2/ppermute | solution.py:254
  33.4 1.9 %collective-permute-start.5 = (bf16[224,1152]{1,0:T(8,128)(2,1)S(1)}, bf16[224,1152]{1,0:T(8,128)(2,1)S(1)}, u32[]{:S(2)}, u32[]{:S(2)}) collective-permute-start(bf16[224,1152]{1,0:T(8,128)(2,1)S(1)} %get-tuple-element.21.p), channel_id=1, source_target_pairs={{0,2},{1,3},{2,0},{3,1},{4,6},{5,7},{6,4},{7,5},{8,10},{9,11},{10,... | collective-permute-start | bytes 1548296 | tf_op jit(solution)/shard_map/chip_p/ppermute | solution.py:254
  36.6 1.1 %match.1 = (f32[2,128]{1,0:T(2,128)S(1)}, s32[224,1]{1,0:T(8,128)S(1)}, s32[4,224]{1,0:T(4,128)S(1)}, s32[224,1]{1,0:T(8,128)S(1)}, s32[4,224]{1,0:T(4,128)S(1)}) custom-call(s32[1]{0:T(128)} %bitcast.here, f32[1]{0:T(128)S(6)} %copy.15.scale, f32[1]{0:T(128)S(6)} %copy.16.shift, s32[1,896]{1,0:T(1,128)} %pos_far.1), custom_call_target="tpu_custom_call" | custom-call | flops 1 | bytes 1 | tf_op jit(solution)/shard_map/match/pallas_call | solution.py:284
  37.7 0.0 collective-permute-done.1.y0
  37.7 0.2 join.1.near
  37.9 3.7 %collective-permute-start.2 = (bf16[896,1152]{1,0:T(8,128)(2,1)S(1)}, bf16[896,1152]{1,0:T(8,128)(2,1)S(1)}, u32[]{:S(2)}, u32[]{:S(2)}) collective-permute-start(bf16[896,1152]{1,0:T(8,128)(2,1)S(1)} %join.1.near), channel_id=1, source_target_pairs={{0,1},{1,0},{2,3},{3,2},{4,5},{5,4},{6,7},{7,6},{8,9},{9,8},{10,11... | collective-permute-start | bytes 6193160 | tf_op jit(solution)/shard_map/core_xy/ppermute | solution.py:254
  41.6 1.7 %own.1 = (f32[224,1152]{1,0:T(8,128)S(1)}, f32[224,1152]{1,0:T(8,128)S(1)}) custom-call(f32[2,128]{1,0:T(2,128)S(1)} %get-tuple-element.20.sc, bf16[896,1152]{1,0:T(8,128)(2,1)S(1)} %join.1.near, s32[224,1]{1,0:T(8,128)S(1)} %get-tuple-element.23.u_p.rest_1_.rest_0_, s32[4,224]{1,0:T(4,128)S(1)} %get-tuple-element.24.v_p.rest_2_.rest_1_, ...), custom_call_target="tpu_custom_call" | custom-call | flops 1 | bytes 1 | tf_op jit(solution)/shard_map/own/pallas_call | solution.py:292
  43.4 0.5 collective-permute-done.3.y
  43.9 4.1 %collective-permute-start.4 = (bf16[224,1152]{1,0:T(8,128)(2,1)S(1)}, bf16[224,1152]{1,0:T(8,128)(2,1)S(1)}, u32[]{:S(2)}, u32[]{:S(2)}) collective-permute-start(bf16[224,1152]{1,0:T(8,128)(2,1)S(1)} %take.1.y1), channel_id=1, source_target_pairs={{0,1},{1,0},{2,3},{3,2},{4,5},{5,4},{6,7},{7,6},{8,9},{9,8},{10,11... | collective-permute-start | bytes 1548296 | tf_op jit(solution)/shard_map/core_y/ppermute | solution.py:254
  48.0 0.0 collective-permute-done.2.near_c
  48.0 1.4 %mid.1.part = f32[224,1152]{1,0:T(8,128)S(1)} custom-call(f32[2,128]{1,0:T(2,128)S(1)} %get-tuple-element.20.sc, bf16[896,1152]{1,0:T(8,128)(2,1)S(1)} %join.1.near, bf16[896,1152]{1,0:T(8,128)(2,1)S(1)} %collective-permute-done.2.near_c, bf16[224,1152]{1,0:T(8,128)(2,1)S(1)} %take.1.y1), custom_call_target="tpu_custom_call" | custom-call | flops 1 | bytes 1 | tf_op jit(solution)/shard_map/mid/pallas_call | solution.py:295
  49.5 0.0 collective-permute-done.5.rest_0_.w2
  49.5 0.0 collective-permute-done.4.y1_c
  49.5 0.8 %late.1 = (bf16[224,1152]{1,0:T(8,128)(2,1)S(1)}, f32[224,1152]{1,0:T(8,128)S(1)}, f32[224,1152]{1,0:T(8,128)S(1)}) custom-call(s32[1]{0:T(128)} %bitcast.here, f32[224,1152]{1,0:T(8,128)S(1)} %mid.1.part, f32[2,128]{1,0:T(2,128)S(1)} %get-tuple-element.20.sc, bf16[896,1152]{1,0:T(8,128)(2,1)S(1)} %join.1.near, ...), custom_call_target="tpu_custom_call" | custom-call | flops 1 | bytes 1 | tf_op jit(solution)/shard_map/late/pallas_call | solution.py:297
  50.4 1.9 %collective-permute-start.6 = (bf16[224,1152]{1,0:T(8,128)(2,1)S(1)}, bf16[224,1152]{1,0:T(8,128)(2,1)S(1)}, u32[]{:S(2)}, u32[]{:S(2)}) collective-permute-start(bf16[224,1152]{1,0:T(8,128)(2,1)S(1)} %get-tuple-element.29._send), channel_id=1, source_target_pairs={{0,2},{1,3},{2,0},{3,1},{4,6},{5,7},{6,4},{7,5},{8,10},{9,11},{10,... | collective-permute-start | bytes 1548296 | tf_op jit(solution)/shard_map/chip_send/ppermute | solution.py:254
  52.3 0.0 copy-start
  52.3 0.0 copy-start.1
  52.3 2.8 %visit.1 = (f32[224,1152]{1,0:T(8,128)S(1)}, f32[224,1152]{1,0:T(8,128)S(1)}, bf16[112,1152]{1,0:T(8,128)(2,1)S(1)}, bf16[112,1152]{1,0:T(8,128)(2,1)S(1)}) custom-call(s32[1]{0:T(128)} %bitcast.here, bf16[224,1152]{1,0:T(8,128)(2,1)S(1)} %get-tuple-element.29._send, ...), custom_call_target="tpu_custom_call", output_to_operand_aliasing={{0}: (2, {}), {1}: (3, {})} | custom-call | flops 1 | bytes 1 | tf_op jit(solution)/shard_map/visit/pallas_call | solution.py:301
  55.2 2.4 %collective-permute-start.7 = (bf16[112,1152]{1,0:T(8,128)(2,1)S(1)}, bf16[112,1152]{1,0:T(8,128)(2,1)S(1)}, u32[]{:S(2)}, u32[]{:S(2)}) collective-permute-start(bf16[112,1152]{1,0:T(8,128)(2,1)S(1)} %get-tuple-element.33), channel_id=1, source_target_pairs={{0,1},{1,0},{2,3},{3,2},{4,5},{5,4},{6,7},{7,6},{8,9},{9,8},{10,11... | collective-permute-start | bytes 774152 | tf_op jit(solution)/shard_map/core_w_lo/ppermute | solution.py:254
  57.6 1.9 %collective-permute-start.8 = (bf16[112,1152]{1,0:T(8,128)(2,1)S(1)}, bf16[112,1152]{1,0:T(8,128)(2,1)S(1)}, u32[]{:S(2)}, u32[]{:S(2)}) collective-permute-start(bf16[112,1152]{1,0:T(8,128)(2,1)S(1)} %get-tuple-element.34), channel_id=1, source_target_pairs={{0,1},{1,0},{2,3},{3,2},{4,5},{5,4},{6,7},{7,6},{8,9},{9,8},{10,11... | collective-permute-start | bytes 774152 | tf_op jit(solution)/shard_map/core_w_hi/ppermute | solution.py:254
  59.5 0.0 collective-permute-done.7.w2_lo_c
  59.5 1.5 %collective-permute-done.8.w2_hi_c = bf16[112,1152]{1,0:T(8,128)(2,1)S(1)} collective-permute-done((bf16[112,1152]{1,0:T(8,128)(2,1)S(1)}, bf16[112,1152]{1,0:T(8,128)(2,1)S(1)}, u32[]{:S(2)}, u32[]{:S(2)}) %collective-permute-start.8) | collective-permute-done | bytes 258080 | tf_op jit(solution)/shard_map/core_w_hi/ppermute | solution.py:254
  61.0 0.0 copy-done
  61.0 0.0 copy-done.1
  61.0 2.1 %rest.1 = (f32[224,1152]{1,0:T(8,128)}, f32[224,1152]{1,0:T(8,128)}) custom-call(f32[2,128]{1,0:T(2,128)S(1)} %get-tuple-element.20.sc, s32[1]{0:T(128)} %bitcast.here, bf16[224,1152]{1,0:T(8,128)(2,1)S(1)} %copy-done, bf16[224,1152]{1,0:T(8,128)(2,1)S(1)} %copy-done.1, bf16[224,1152]{1,0:T(8,128)(2,1)S(1)} %get-tuple-element.21.p, ...), custom_call_target="tpu_custom_call" | custom-call | flops 1 | bytes 1 | tf_op jit(solution)/shard_map/rest/pallas_call | solution.py:308
  63.1 0.0 collective-permute-done.6.back
  63.2 1.3 %last.1 = (f32[224,1152]{1,0:T(8,128)}, f32[224,1152]{1,0:T(8,128)}) custom-call(s32[1]{0:T(128)} %bitcast.here, bf16[224,1152]{1,0:T(8,128)(2,1)S(1)} %copy-done, bf16[224,1152]{1,0:T(8,128)(2,1)S(1)} %copy-done.1, f32[224,1152]{1,0:T(8,128)S(1)} %get-tuple-element.32.sum_q, ...), custom_call_target="tpu_custom_call", output_to_operand_aliasing={{0}: (5, {}), {1}: (6, {})} | custom-call | flops 64000000000 | bytes 1 | tf_op jit(solution)/shard_map/last/pallas_call | solution.py:315
  (1 shorter events, 0.0 us)
Async XLA Ops:
  2.3 18.8 %collective-permute-start = (bf16[224,1152]{1,0:T(8,128)(2,1)S(1)}, bf16[224,1152]{1,0:T(8,128)(2,1)S(1)}, u32[]{:S(2)}, u32[]{:S(2)}) collective-permute-start(bf16[224,1152]{1,0:T(8,128)(2,1)S(1)} %get-tuple-element.22.q), channel_id=1, source_target_pairs={{0,2},{1,3},{2,0},{3,1},{4,6},{5,7},{6,4},{7,5},{8,10},{9,11},{10,... | collective-permute-start | bytes 1548296 | tf_op jit(solution)/shard_map/chip_q/ppermute | solution.py:254
  7.1 30.6 %collective-permute-start.1 = (bf16[224,1152]{1,0:T(8,128)(2,1)S(1)}, bf16[224,1152]{1,0:T(8,128)(2,1)S(1)}, u32[]{:S(2)}, u32[]{:S(2)}) collective-permute-start(bf16[224,1152]{1,0:T(8,128)(2,1)S(1)} %get-tuple-element.21.p), channel_id=1, source_target_pairs={{0,510},{1,511},{2,4},{3,5},{4,2},{5,3},{6,8},{7,9},{8,6},{9,7},{1... | collective-permute-start | bytes 1548296 | tf_op jit(solution)/shard_map/group_p/ppermute | solution.py:254
  21.1 22.8 %collective-permute-start.3 = (bf16[224,1152]{1,0:T(8,128)(2,1)S(1)}, bf16[224,1152]{1,0:T(8,128)(2,1)S(1)}, u32[]{:S(2)}, u32[]{:S(2)}) collective-permute-start(bf16[224,1152]{1,0:T(8,128)(2,1)S(1)} %collective-permute-done.x2), channel_id=1, source_target_pairs={{0,510},{1,511},{2,4},{3,5},{4,2},{5,3},{6,8},{7,9},{8,6},{9,7},{1... | collective-permute-start | bytes 1548296 | tf_op jit(solution)/shard_map/group_x2/ppermute | solution.py:254
  33.4 16.1 %collective-permute-start.5 = (bf16[224,1152]{1,0:T(8,128)(2,1)S(1)}, bf16[224,1152]{1,0:T(8,128)(2,1)S(1)}, u32[]{:S(2)}, u32[]{:S(2)}) collective-permute-start(bf16[224,1152]{1,0:T(8,128)(2,1)S(1)} %get-tuple-element.21.p), channel_id=1, source_target_pairs={{0,2},{1,3},{2,0},{3,1},{4,6},{5,7},{6,4},{7,5},{8,10},{9,11},{10,... | collective-permute-start | bytes 1548296 | tf_op jit(solution)/shard_map/chip_p/ppermute | solution.py:254
  37.9 10.2 %collective-permute-start.2 = (bf16[896,1152]{1,0:T(8,128)(2,1)S(1)}, bf16[896,1152]{1,0:T(8,128)(2,1)S(1)}, u32[]{:S(2)}, u32[]{:S(2)}) collective-permute-start(bf16[896,1152]{1,0:T(8,128)(2,1)S(1)} %join.1.near), channel_id=1, source_target_pairs={{0,1},{1,0},{2,3},{3,2},{4,5},{5,4},{6,7},{7,6},{8,9},{9,8},{10,11... | collective-permute-start | bytes 6193160 | tf_op jit(solution)/shard_map/core_xy/ppermute | solution.py:254
  43.9 5.6 %collective-permute-start.4 = (bf16[224,1152]{1,0:T(8,128)(2,1)S(1)}, bf16[224,1152]{1,0:T(8,128)(2,1)S(1)}, u32[]{:S(2)}, u32[]{:S(2)}) collective-permute-start(bf16[224,1152]{1,0:T(8,128)(2,1)S(1)} %take.1.y1), channel_id=1, source_target_pairs={{0,1},{1,0},{2,3},{3,2},{4,5},{5,4},{6,7},{7,6},{8,9},{9,8},{10,11... | collective-permute-start | bytes 1548296 | tf_op jit(solution)/shard_map/core_y/ppermute | solution.py:254
  50.4 12.8 %collective-permute-start.6 = (bf16[224,1152]{1,0:T(8,128)(2,1)S(1)}, bf16[224,1152]{1,0:T(8,128)(2,1)S(1)}, u32[]{:S(2)}, u32[]{:S(2)}) collective-permute-start(bf16[224,1152]{1,0:T(8,128)(2,1)S(1)} %get-tuple-element.29._send), channel_id=1, source_target_pairs={{0,2},{1,3},{2,0},{3,1},{4,6},{5,7},{6,4},{7,5},{8,10},{9,11},{10,... | collective-permute-start | bytes 1548296 | tf_op jit(solution)/shard_map/chip_send/ppermute | solution.py:254
  52.3 8.7 %copy-start = (bf16[224,1152]{1,0:T(8,128)(2,1)S(1)}, bf16[224,1152]{1,0:T(8,128)(2,1)}, u32[]{:S(2)}) copy-start(bf16[224,1152]{1,0:T(8,128)(2,1)} %img.5) | copy-start | bytes 1548292
  52.3 8.7 %copy-start.1 = (bf16[224,1152]{1,0:T(8,128)(2,1)S(1)}, bf16[224,1152]{1,0:T(8,128)(2,1)}, u32[]{:S(2)}) copy-start(bf16[224,1152]{1,0:T(8,128)(2,1)} %txt.5) | copy-start | bytes 1548292
  55.2 4.4 %collective-permute-start.7 = (bf16[112,1152]{1,0:T(8,128)(2,1)S(1)}, bf16[112,1152]{1,0:T(8,128)(2,1)S(1)}, u32[]{:S(2)}, u32[]{:S(2)}) collective-permute-start(bf16[112,1152]{1,0:T(8,128)(2,1)S(1)} %get-tuple-element.33), channel_id=1, source_target_pairs={{0,1},{1,0},{2,3},{3,2},{4,5},{5,4},{6,7},{7,6},{8,9},{9,8},{10,11... | collective-permute-start | bytes 774152 | tf_op jit(solution)/shard_map/core_w_lo/ppermute | solution.py:254
  57.6 3.4 %collective-permute-start.8 = (bf16[112,1152]{1,0:T(8,128)(2,1)S(1)}, bf16[112,1152]{1,0:T(8,128)(2,1)S(1)}, u32[]{:S(2)}, u32[]{:S(2)}) collective-permute-start(bf16[112,1152]{1,0:T(8,128)(2,1)S(1)} %get-tuple-element.34), channel_id=1, source_target_pairs={{0,1},{1,0},{2,3},{3,2},{4,5},{5,4},{6,7},{7,6},{8,9},{9,8},{10,11... | collective-permute-start | bytes 774152 | tf_op jit(solution)/shard_map/core_w_hi/ppermute | solution.py:254

commit v7 on v6

--- a/solution.py
+++ b/solution.py
@@ -11,11 +11,7 @@
 HBM = pl.BlockSpec(memory_space=pltpu.HBM)
 NT = (((1,), (1,)), ((), ()))
 NN = (((1,), (0,)), ((), ()))
-COST = {
-    "unit": 16 * 10**9,
-    "take": 64 * 10**9,
-    "last": 64 * 10**9,
-}
+COST = {"unit": 16 * 10**9, "take": 64 * 10**9, "last": 64 * 10**9, "nums": 10**9}
 
 
 def pieces_of(rows):
@@ -49,7 +45,8 @@
     )
 
 
-def unit_body(here, img, txt, p, q, raw, sems):
+def unit_body(here, img, txt, pos_far, p, q, *rest):
+    raw, sems = rest[-2:]
     half = img.shape[0] // 2
     copies = []
     for j in range(2):
@@ -78,13 +75,27 @@
             p[part] = unit[1]
             q[part] = unit[0]
 
-
-def match_body(here, scale, shift, pos_far, sc, u_p, v_p, u_q, v_q, pos, sem):
+    @pl.when(here[0] % 2 == 0)
+    def _():
+        spots(here, pos_far, *rest[:-2])
+
+
+def nums_body(scale, shift, sc):
+    sc[0:1] = jnp.full((1, sc.shape[1]), scale[0], jnp.float32)
+    sc[1:2] = jnp.full((1, sc.shape[1]), shift[0], jnp.float32)
+
+
+def match_body(here, pos_far, *rest):
+    @pl.when(here[0] % 2 == 1)
+    def _():
+        spots(here, pos_far, *rest[4:])
+
+
+def spots(here, pos_far, u_p, v_p, u_q, v_q, pos, sem):
     rows = u_p.shape[0]
     copy = pltpu.make_async_copy(pos_far, pos, sem)
     copy.start()
-    sc[0:1] = jnp.full((1, sc.shape[1]), scale[0], jnp.float32)
-    sc[1:2] = jnp.full((1, sc.shape[1]), shift[0], jnp.float32)
+    copy.wait()
     me = here[0]
     lane = lax.broadcasted_iota(jnp.int32, (1, rows), 1)
     square = (rows, rows)
@@ -96,7 +107,6 @@
         spread = jnp.where(diagonal, jnp.broadcast_to(row, square).astype(jnp.float32), 0.0)
         return jnp.sum(spread, axis=1, keepdims=True).astype(jnp.int32)
 
-    copy.wait()
     blocks = [pos[:, k * rows : (k + 1) * rows] for k in range(4)]
     matches, places = [], []
     for j in range(4):
@@ -269,24 +279,28 @@
     dma = pltpu.SemaphoreType.DMA
     far = lambda x: pltpu.with_memory_space_constraint(x, pltpu.HBM)
 
-    p, q = call(
+    place = (of((rows, 1), jnp.int32), of((4, rows), jnp.int32)) * 2
+    pos = far(caption_position)
+    reading = [pltpu.VMEM((1, 4 * rows), jnp.int32), dma]
+    p, q, *spot = call(
         unit_body,
-        (one, one),
-        [SMEM, HBM, HBM],
-        scratch_shapes=[pltpu.VMEM((2, rows, depth), bf16), dma((4,))],
-    )(here, far(img), far(txt))
+        (one, one) + place,
+        [SMEM] + [HBM] * 3,
+        scratch_shapes=reading + [pltpu.VMEM((2, rows, depth), bf16), dma((4,))],
+    )(here, far(img), far(txt), pos)
     x2 = chip(q, "chip_q")
     y0 = group(p, "group_p")
     y1 = group(x2, "group_x2")
     w2 = chip(p, "chip_p")
 
-    place = (of((rows, 1), jnp.int32), of((4, rows), jnp.int32))
-    sc, *match = call(
+    sc = call(nums_body, of((2, 128)), [SMEM] * 2)(scale, shift)
+    match = call(
         match_body,
-        (of((2, 128)),) + place + place,
-        [SMEM] * 3 + [HBM],
-        scratch_shapes=[pltpu.VMEM((1, 4 * rows), jnp.int32), dma],
-    )(here, scale, shift, far(caption_position))
+        place,
+        [SMEM, HBM] + [VMEM] * 4,
+        scratch_shapes=reading,
+        input_output_aliases={2 + j: j for j in range(4)},
+    )(here, pos, *spot)
     near = call(join_body, four, [VMEM] * 4)(p, q, x2, y0)
     near_c = core(near, "core_xy")
     own_p, own_q = call(own_body, (wide, wide), [VMEM] * 6)(sc, near, *match)

time: 64.9 us -> 63.8 us (0.983)
  starting transfers between devices: 47.1 us -> 46.4 us
    pallas_call x2 -> x3, Pallas kernels: 2.74 us -> 2.78 us  [the longest x1 1.67 us: local(): call(unit_body, (one, one) + place, [SMEM] + [HBM] * 3, scratch_shapes=re...]
  transfers between devices with their start and end apart: 9 -> 9, of which waited for: 2 -> 1; matrix products, arithmetic and copies ran while one was open for 0% -> 0% of each run, Pallas kernels for 15% -> 15%
where the time goes in v7:
time: 63.8 us; the launch traced here: 63.3 us
  starting transfers between devices  46.4 us (73%)
  Pallas kernels  13.2 us (21%)
  between operations  2.14 us (3%)
  waiting for transfers between devices  1.54 us (2%)
    ppermute x9, starting transfers between devices, go(): return lax.ppermute(x, AXES, pairs)  46.4 us
    pallas_call x1, Pallas kernels, local(): call(visit_body, (wide, wide, part, part), [SMEM] + [VMEM] * 15, input_ou...  2.83 us
    pallas_call x1, Pallas kernels, local(): call(rest_body, (wide, wide), [VMEM, SMEM] + [VMEM] * 8, (HBM, HBM), scra...  2.08 us
    pallas_call x1, Pallas kernels, local(): own_p, own_q = call(own_body, (wide, wide), [VMEM] * 6)(sc, near, *match)  1.74 us
    pallas_call x1, Pallas kernels, local(): call(unit_body, (one, one) + place, [SMEM] + [HBM] * 3, scratch_shapes=re...  1.67 us
    ppermute x9, waiting for transfers between devices, go(): return lax.ppermute(x, AXES, pairs)  1.54 us
    pallas_call x1, Pallas kernels, local(): part_x = call(mid_body, wide, [VMEM] * 4)(sc, near, near_c, y1)  1.44 us
    pallas_call x1, Pallas kernels, local(): call(last_body, (wide, wide), [SMEM] + [VMEM] * 4 + [HBM] * 2, (HBM, HBM)...  1.32 us
  transfers between devices with their start and end apart: 9, of which 1 were waited for; matrix products, arithmetic and copies ran while one was open for 0% of the time, Pallas kernels for 15%

profile of v7, /device:TPU:1, one launch (start us, length us, event | category | flops | bytes accessed | tf_op | source)
XLA Modules:
  0.0 63.3 jit_solution(15819149481123051132)
XLA Ops:
  0.6 1.7 %unit.1 = (bf16[224,1152]{1,0:T(8,128)(2,1)S(1)}, bf16[224,1152]{1,0:T(8,128)(2,1)S(1)}, s32[224,1]{1,0:T(8,128)S(1)}, s32[4,224]{1,0:T(4,128)S(1)}, s32[224,1]{1,0:T(8,128)S(1)}, /*index=5*/s32[4,224]{1,0:T(4,128)S(1)}) custom-call(s32[1]{0:T(128)} %bitcast.here, bf16[224,1152]{1,0:T(8,128)(2,1)} %img.5, bf16[224,1152]{1,0:T(8,128)(2,1)} %txt.5, ...), custom_call_target="tpu_custom_call" | custom-call | flops 16000000000 | bytes 1 | tf_op jit(solution)/shard_map/unit/pallas_call | solution.py:285
  2.3 4.8 %collective-permute-start = (bf16[224,1152]{1,0:T(8,128)(2,1)S(1)}, bf16[224,1152]{1,0:T(8,128)(2,1)S(1)}, u32[]{:S(2)}, u32[]{:S(2)}) collective-permute-start(bf16[224,1152]{1,0:T(8,128)(2,1)S(1)} %get-tuple-element.24.q), channel_id=1, source_target_pairs={{0,2},{1,3},{2,0},{3,1},{4,6},{5,7},{6,4},{7,5},{8,10},{9,11},{10,... | collective-permute-start | bytes 1548296 | tf_op jit(solution)/shard_map/chip_q/ppermute | solution.py:264
  7.1 14.0 %collective-permute-start.1 = (bf16[224,1152]{1,0:T(8,128)(2,1)S(1)}, bf16[224,1152]{1,0:T(8,128)(2,1)S(1)}, u32[]{:S(2)}, u32[]{:S(2)}) collective-permute-start(bf16[224,1152]{1,0:T(8,128)(2,1)S(1)} %get-tuple-element.23.p), channel_id=1, source_target_pairs={{0,510},{1,511},{2,4},{3,5},{4,2},{5,3},{6,8},{7,9},{8,6},{9,7},{1... | collective-permute-start | bytes 1548296 | tf_op jit(solution)/shard_map/group_p/ppermute | solution.py:264
  21.1 0.0 collective-permute-done.x2
  21.1 11.2 %collective-permute-start.3 = (bf16[224,1152]{1,0:T(8,128)(2,1)S(1)}, bf16[224,1152]{1,0:T(8,128)(2,1)S(1)}, u32[]{:S(2)}, u32[]{:S(2)}) collective-permute-start(bf16[224,1152]{1,0:T(8,128)(2,1)S(1)} %collective-permute-done.x2), channel_id=1, source_target_pairs={{0,510},{1,511},{2,4},{3,5},{4,2},{5,3},{6,8},{7,9},{8,6},{9,7},{1... | collective-permute-start | bytes 1548296 | tf_op jit(solution)/shard_map/group_x2/ppermute | solution.py:264
  32.3 1.9 %collective-permute-start.5 = (bf16[224,1152]{1,0:T(8,128)(2,1)S(1)}, bf16[224,1152]{1,0:T(8,128)(2,1)S(1)}, u32[]{:S(2)}, u32[]{:S(2)}) collective-permute-start(bf16[224,1152]{1,0:T(8,128)(2,1)S(1)} %get-tuple-element.23.p), channel_id=1, source_target_pairs={{0,2},{1,3},{2,0},{3,1},{4,6},{5,7},{6,4},{7,5},{8,10},{9,11},{10,... | collective-permute-start | bytes 1548296 | tf_op jit(solution)/shard_map/chip_p/ppermute | solution.py:264
  34.2 1.1 %match.1 = (s32[224,1]{1,0:T(8,128)S(1)}, s32[4,224]{1,0:T(4,128)S(1)}, s32[224,1]{1,0:T(8,128)S(1)}, s32[4,224]{1,0:T(4,128)S(1)}) custom-call(s32[1]{0:T(128)} %bitcast.here, s32[1,896]{1,0:T(1,128)} %pos_far.3, s32[224,1]{1,0:T(8,128)S(1)} %get-tuple-element.25.rest_0_, ...), custom_call_target="tpu_custom_call", output_to_operand_aliasing={{0}: (2, {}), {1}: (3, {}), {2}: (4, {}), {3}: (5, {})} | custom-call | flops 1 | bytes 1 | tf_op jit(solution)/shard_map/match/pallas_call | solution.py:297
  36.6 0.0 collective-permute-done.1.y0
  36.6 0.2 join.1.near
  36.8 3.8 %collective-permute-start.2 = (bf16[896,1152]{1,0:T(8,128)(2,1)S(1)}, bf16[896,1152]{1,0:T(8,128)(2,1)S(1)}, u32[]{:S(2)}, u32[]{:S(2)}) collective-permute-start(bf16[896,1152]{1,0:T(8,128)(2,1)S(1)} %join.1.near), channel_id=1, source_target_pairs={{0,1},{1,0},{2,3},{3,2},{4,5},{5,4},{6,7},{7,6},{8,9},{9,8},{10,11... | collective-permute-start | bytes 6193160 | tf_op jit(solution)/shard_map/core_xy/ppermute | solution.py:264
  40.6 1.7 %own.1 = (f32[224,1152]{1,0:T(8,128)S(1)}, f32[224,1152]{1,0:T(8,128)S(1)}) custom-call(f32[2,128]{1,0:T(2,128)S(1)} %nums.1.sc, bf16[896,1152]{1,0:T(8,128)(2,1)S(1)} %join.1.near, s32[224,1]{1,0:T(8,128)S(1)} %get-tuple-element.29.u_p.rest_1_.rest_0_, s32[4,224]{1,0:T(4,128)S(1)} %get-tuple-element.30.v_p.rest_2_.rest_1_, ...), custom_call_target="tpu_custom_call" | custom-call | flops 1 | bytes 1 | tf_op jit(solution)/shard_map/own/pallas_call | solution.py:306
  42.3 0.0 collective-permute-done.3.y
  42.4 4.5 %collective-permute-start.4 = (bf16[224,1152]{1,0:T(8,128)(2,1)S(1)}, bf16[224,1152]{1,0:T(8,128)(2,1)S(1)}, u32[]{:S(2)}, u32[]{:S(2)}) collective-permute-start(bf16[224,1152]{1,0:T(8,128)(2,1)S(1)} %take.1.y1), channel_id=1, source_target_pairs={{0,1},{1,0},{2,3},{3,2},{4,5},{5,4},{6,7},{7,6},{8,9},{9,8},{10,11... | collective-permute-start | bytes 1548296 | tf_op jit(solution)/shard_map/core_y/ppermute | solution.py:264
  46.9 0.0 collective-permute-done.2.near_c
  46.9 1.4 %mid.1.part = f32[224,1152]{1,0:T(8,128)S(1)} custom-call(f32[2,128]{1,0:T(2,128)S(1)} %nums.1.sc, bf16[896,1152]{1,0:T(8,128)(2,1)S(1)} %join.1.near, bf16[896,1152]{1,0:T(8,128)(2,1)S(1)} %collective-permute-done.2.near_c, bf16[224,1152]{1,0:T(8,128)(2,1)S(1)} %take.1.y1), custom_call_target="tpu_custom_call" | custom-call | flops 1 | bytes 1 | tf_op jit(solution)/shard_map/mid/pallas_call | solution.py:309
  48.4 0.0 collective-permute-done.5.rest_0_.w2
  48.4 0.0 collective-permute-done.4.y1_c
  48.4 0.8 %late.1 = (bf16[224,1152]{1,0:T(8,128)(2,1)S(1)}, f32[224,1152]{1,0:T(8,128)S(1)}, f32[224,1152]{1,0:T(8,128)S(1)}) custom-call(s32[1]{0:T(128)} %bitcast.here, f32[224,1152]{1,0:T(8,128)S(1)} %mid.1.part, f32[2,128]{1,0:T(2,128)S(1)} %nums.1.sc, bf16[896,1152]{1,0:T(8,128)(2,1)S(1)} %join.1.near, bf16[896,1152]{1,0:T(8,128)(2,1)S(1)} %collective-permute-done.2.near_c, ...), custom_call_target="tpu_custom_call" | custom-call | flops 1 | bytes 1 | tf_op jit(solution)/shard_map/late/pallas_call | solution.py:311
  49.3 1.9 %collective-permute-start.6 = (bf16[224,1152]{1,0:T(8,128)(2,1)S(1)}, bf16[224,1152]{1,0:T(8,128)(2,1)S(1)}, u32[]{:S(2)}, u32[]{:S(2)}) collective-permute-start(bf16[224,1152]{1,0:T(8,128)(2,1)S(1)} %get-tuple-element.35._send), channel_id=1, source_target_pairs={{0,2},{1,3},{2,0},{3,1},{4,6},{5,7},{6,4},{7,5},{8,10},{9,11},{10,... | collective-permute-start | bytes 1548296 | tf_op jit(solution)/shard_map/chip_send/ppermute | solution.py:264
  51.2 0.0 copy-start
  51.2 0.0 copy-start.1
  51.2 2.8 %visit.1 = (f32[224,1152]{1,0:T(8,128)S(1)}, f32[224,1152]{1,0:T(8,128)S(1)}, bf16[112,1152]{1,0:T(8,128)(2,1)S(1)}, bf16[112,1152]{1,0:T(8,128)(2,1)S(1)}) custom-call(s32[1]{0:T(128)} %bitcast.here, bf16[224,1152]{1,0:T(8,128)(2,1)S(1)} %get-tuple-element.35._send, ...), custom_call_target="tpu_custom_call", output_to_operand_aliasing={{0}: (2, {}), {1}: (3, {})} | custom-call | flops 1 | bytes 1 | tf_op jit(solution)/shard_map/visit/pallas_call | solution.py:315
  54.1 2.4 %collective-permute-start.7 = (bf16[112,1152]{1,0:T(8,128)(2,1)S(1)}, bf16[112,1152]{1,0:T(8,128)(2,1)S(1)}, u32[]{:S(2)}, u32[]{:S(2)}) collective-permute-start(bf16[112,1152]{1,0:T(8,128)(2,1)S(1)} %get-tuple-element.39), channel_id=1, source_target_pairs={{0,1},{1,0},{2,3},{3,2},{4,5},{5,4},{6,7},{7,6},{8,9},{9,8},{10,11... | collective-permute-start | bytes 774152 | tf_op jit(solution)/shard_map/core_w_lo/ppermute | solution.py:264
  56.5 1.9 %collective-permute-start.8 = (bf16[112,1152]{1,0:T(8,128)(2,1)S(1)}, bf16[112,1152]{1,0:T(8,128)(2,1)S(1)}, u32[]{:S(2)}, u32[]{:S(2)}) collective-permute-start(bf16[112,1152]{1,0:T(8,128)(2,1)S(1)} %get-tuple-element.40), channel_id=1, source_target_pairs={{0,1},{1,0},{2,3},{3,2},{4,5},{5,4},{6,7},{7,6},{8,9},{9,8},{10,11... | collective-permute-start | bytes 774152 | tf_op jit(solution)/shard_map/core_w_hi/ppermute | solution.py:264
  58.4 0.0 collective-permute-done.7.w2_lo_c
  58.4 1.5 %collective-permute-done.8.w2_hi_c = bf16[112,1152]{1,0:T(8,128)(2,1)S(1)} collective-permute-done((bf16[112,1152]{1,0:T(8,128)(2,1)S(1)}, bf16[112,1152]{1,0:T(8,128)(2,1)S(1)}, u32[]{:S(2)}, u32[]{:S(2)}) %collective-permute-start.8) | collective-permute-done | bytes 258080 | tf_op jit(solution)/shard_map/core_w_hi/ppermute | solution.py:264
  59.9 0.0 copy-done
  59.9 0.0 copy-done.1
  59.9 2.1 %rest.1 = (f32[224,1152]{1,0:T(8,128)}, f32[224,1152]{1,0:T(8,128)}) custom-call(f32[2,128]{1,0:T(2,128)S(1)} %nums.1.sc, s32[1]{0:T(128)} %bitcast.here, bf16[224,1152]{1,0:T(8,128)(2,1)S(1)} %copy-done, bf16[224,1152]{1,0:T(8,128)(2,1)S(1)} %copy-done.1, bf16[224,1152]{1,0:T(8,128)(2,1)S(1)} %get-tuple-element.23.p, ...), custom_call_target="tpu_custom_call" | custom-call | flops 1 | bytes 1 | tf_op jit(solution)/shard_map/rest/pallas_call | solution.py:322
  62.0 0.0 collective-permute-done.6.back
  62.0 1.3 %last.1 = (f32[224,1152]{1,0:T(8,128)}, f32[224,1152]{1,0:T(8,128)}) custom-call(s32[1]{0:T(128)} %bitcast.here, bf16[224,1152]{1,0:T(8,128)(2,1)S(1)} %copy-done, bf16[224,1152]{1,0:T(8,128)(2,1)S(1)} %copy-done.1, f32[224,1152]{1,0:T(8,128)S(1)} %get-tuple-element.38.sum_q, ...), custom_call_target="tpu_custom_call", output_to_operand_aliasing={{0}: (5, {}), {1}: (6, {})} | custom-call | flops 64000000000 | bytes 1 | tf_op jit(solution)/shard_map/last/pallas_call | solution.py:329
  (2 shorter events, 0.0 us)
Async XLA Ops:
  2.3 18.8 %collective-permute-start = (bf16[224,1152]{1,0:T(8,128)(2,1)S(1)}, bf16[224,1152]{1,0:T(8,128)(2,1)S(1)}, u32[]{:S(2)}, u32[]{:S(2)}) collective-permute-start(bf16[224,1152]{1,0:T(8,128)(2,1)S(1)} %get-tuple-element.24.q), channel_id=1, source_target_pairs={{0,2},{1,3},{2,0},{3,1},{4,6},{5,7},{6,4},{7,5},{8,10},{9,11},{10,... | collective-permute-start | bytes 1548296 | tf_op jit(solution)/shard_map/chip_q/ppermute | solution.py:264
  7.1 29.5 %collective-permute-start.1 = (bf16[224,1152]{1,0:T(8,128)(2,1)S(1)}, bf16[224,1152]{1,0:T(8,128)(2,1)S(1)}, u32[]{:S(2)}, u32[]{:S(2)}) collective-permute-start(bf16[224,1152]{1,0:T(8,128)(2,1)S(1)} %get-tuple-element.23.p), channel_id=1, source_target_pairs={{0,510},{1,511},{2,4},{3,5},{4,2},{5,3},{6,8},{7,9},{8,6},{9,7},{1... | collective-permute-start | bytes 1548296 | tf_op jit(solution)/shard_map/group_p/ppermute | solution.py:264
  21.1 21.2 %collective-permute-start.3 = (bf16[224,1152]{1,0:T(8,128)(2,1)S(1)}, bf16[224,1152]{1,0:T(8,128)(2,1)S(1)}, u32[]{:S(2)}, u32[]{:S(2)}) collective-permute-start(bf16[224,1152]{1,0:T(8,128)(2,1)S(1)} %collective-permute-done.x2), channel_id=1, source_target_pairs={{0,510},{1,511},{2,4},{3,5},{4,2},{5,3},{6,8},{7,9},{8,6},{9,7},{1... | collective-permute-start | bytes 1548296 | tf_op jit(solution)/shard_map/group_x2/ppermute | solution.py:264
  32.3 16.1 %collective-permute-start.5 = (bf16[224,1152]{1,0:T(8,128)(2,1)S(1)}, bf16[224,1152]{1,0:T(8,128)(2,1)S(1)}, u32[]{:S(2)}, u32[]{:S(2)}) collective-permute-start(bf16[224,1152]{1,0:T(8,128)(2,1)S(1)} %get-tuple-element.23.p), channel_id=1, source_target_pairs={{0,2},{1,3},{2,0},{3,1},{4,6},{5,7},{6,4},{7,5},{8,10},{9,11},{10,... | collective-permute-start | bytes 1548296 | tf_op jit(solution)/shard_map/chip_p/ppermute | solution.py:264
  36.8 10.1 %collective-permute-start.2 = (bf16[896,1152]{1,0:T(8,128)(2,1)S(1)}, bf16[896,1152]{1,0:T(8,128)(2,1)S(1)}, u32[]{:S(2)}, u32[]{:S(2)}) collective-permute-start(bf16[896,1152]{1,0:T(8,128)(2,1)S(1)} %join.1.near), channel_id=1, source_target_pairs={{0,1},{1,0},{2,3},{3,2},{4,5},{5,4},{6,7},{7,6},{8,9},{9,8},{10,11... | collective-permute-start | bytes 6193160 | tf_op jit(solution)/shard_map/core_xy/ppermute | solution.py:264
  42.4 6.0 %collective-permute-start.4 = (bf16[224,1152]{1,0:T(8,128)(2,1)S(1)}, bf16[224,1152]{1,0:T(8,128)(2,1)S(1)}, u32[]{:S(2)}, u32[]{:S(2)}) collective-permute-start(bf16[224,1152]{1,0:T(8,128)(2,1)S(1)} %take.1.y1), channel_id=1, source_target_pairs={{0,1},{1,0},{2,3},{3,2},{4,5},{5,4},{6,7},{7,6},{8,9},{9,8},{10,11... | collective-permute-start | bytes 1548296 | tf_op jit(solution)/shard_map/core_y/ppermute | solution.py:264
  49.3 12.7 %collective-permute-start.6 = (bf16[224,1152]{1,0:T(8,128)(2,1)S(1)}, bf16[224,1152]{1,0:T(8,128)(2,1)S(1)}, u32[]{:S(2)}, u32[]{:S(2)}) collective-permute-start(bf16[224,1152]{1,0:T(8,128)(2,1)S(1)} %get-tuple-element.35._send), channel_id=1, source_target_pairs={{0,2},{1,3},{2,0},{3,1},{4,6},{5,7},{6,4},{7,5},{8,10},{9,11},{10,... | collective-permute-start | bytes 1548296 | tf_op jit(solution)/shard_map/chip_send/ppermute | solution.py:264
  51.2 8.7 %copy-start = (bf16[224,1152]{1,0:T(8,128)(2,1)S(1)}, bf16[224,1152]{1,0:T(8,128)(2,1)}, u32[]{:S(2)}) copy-start(bf16[224,1152]{1,0:T(8,128)(2,1)} %img.5) | copy-start | bytes 1548292
  51.2 8.7 %copy-start.1 = (bf16[224,1152]{1,0:T(8,128)(2,1)S(1)}, bf16[224,1152]{1,0:T(8,128)(2,1)}, u32[]{:S(2)}) copy-start(bf16[224,1152]{1,0:T(8,128)(2,1)} %txt.5) | copy-start | bytes 1548292
  54.1 4.4 %collective-permute-start.7 = (bf16[112,1152]{1,0:T(8,128)(2,1)S(1)}, bf16[112,1152]{1,0:T(8,128)(2,1)S(1)}, u32[]{:S(2)}, u32[]{:S(2)}) collective-permute-start(bf16[112,1152]{1,0:T(8,128)(2,1)S(1)} %get-tuple-element.39), channel_id=1, source_target_pairs={{0,1},{1,0},{2,3},{3,2},{4,5},{5,4},{6,7},{7,6},{8,9},{9,8},{10,11... | collective-permute-start | bytes 774152 | tf_op jit(solution)/shard_map/core_w_lo/ppermute | solution.py:264
  56.5 3.4 %collective-permute-start.8 = (bf16[112,1152]{1,0:T(8,128)(2,1)S(1)}, bf16[112,1152]{1,0:T(8,128)(2,1)S(1)}, u32[]{:S(2)}, u32[]{:S(2)}) collective-permute-start(bf16[112,1152]{1,0:T(8,128)(2,1)S(1)} %get-tuple-element.40), channel_id=1, source_target_pairs={{0,1},{1,0},{2,3},{3,2},{4,5},{5,4},{6,7},{7,6},{8,9},{9,8},{10,11... | collective-permute-start | bytes 774152 | tf_op jit(solution)/shard_map/core_w_hi/ppermute | solution.py:264

commit v8 on v7

--- a/solution.py
+++ b/solution.py
@@ -47,33 +47,25 @@
 
 def unit_body(here, img, txt, pos_far, p, q, *rest):
     raw, sems = rest[-2:]
-    half = img.shape[0] // 2
     copies = []
-    for j in range(2):
-        part = pl.ds(j * half, half)
-        for i, ref in enumerate((img, txt)):
-            copies.append(
-                pltpu.make_async_copy(ref.at[part], raw.at[i, part], sems.at[2 * j + i])
-            )
-    for copy in copies:
-        copy.start()
-    for j in range(2):
-        part = pl.ds(j * half, half)
-        unit = []
-        for i in range(2):
-            copies[2 * j + i].wait()
-            values = raw[i, part].astype(jnp.float32)
-            unit.append((values * inv_norm(values)).astype(jnp.bfloat16))
-
-        @pl.when(here[0] < 2)
-        def _():
-            p[part] = unit[0]
-            q[part] = unit[1]
-
-        @pl.when(here[0] >= 2)
-        def _():
-            p[part] = unit[1]
-            q[part] = unit[0]
+    for i, ref in enumerate((img, txt)):
+        copies.append(pltpu.make_async_copy(ref, raw.at[i], sems.at[i]))
+        copies[-1].start()
+
+    def unit(i):
+        copies[i].wait()
+        values = raw[i].astype(jnp.float32)
+        return (values * inv_norm(values)).astype(jnp.bfloat16)
+
+    @pl.when(here[0] < 2)
+    def _():
+        p[...] = unit(0)
+        q[...] = unit(1)
+
+    @pl.when(here[0] >= 2)
+    def _():
+        p[...] = unit(1)
+        q[...] = unit(0)
 
     @pl.when(here[0] % 2 == 0)
     def _():
@@ -152,8 +144,9 @@
         out[j * rows : (j + 1) * rows] = part[...]
 
 
-def own_body(sc, near, u_p, v_p, u_q, v_q, sum_p, sum_q):
+def own_body(sc, near, u_p, v_p, u_q, v_q, sum_p, sum_q, part):
     x, y, x2, y0 = (block(near, j) for j in range(4))
+    part[...] = terms(x2, [y0], sc)
     sum_p[...] = terms(x, [y], sc, (u_p[...], [v_p[0:1]])) + terms(x, [y0], sc)
     sum_q[...] = terms(y, [x, x2], sc, (u_q[...], [v_q[0:1], v_q[2:3]]))
 
@@ -167,8 +160,8 @@
     return ref[j * rows : (j + 1) * rows]
 
 
-def mid_body(sc, near, near_c, y1, part):
-    part[...] = terms(block(near, 2), [block(near, 3), block(near_c, 3), y1[...]], sc)
+def mid_body(sc, near, near_c, y1, part, out):
+    out[...] = part[...] + terms(block(near, 2), [block(near_c, 3), y1[...]], sc)
 
 
 def far_sums(sc, near, near_c, y1, y1_c, w2, u_p, v_p, u_q, v_q, own_p, own_q, sum_p, sum_q):
@@ -286,7 +279,7 @@
         unit_body,
         (one, one) + place,
         [SMEM] + [HBM] * 3,
-        scratch_shapes=reading + [pltpu.VMEM((2, rows, depth), bf16), dma((4,))],
+        scratch_shapes=reading + [pltpu.VMEM((2, rows, depth), bf16), dma((2,))],
     )(here, far(img), far(txt), pos)
     x2 = chip(q, "chip_q")
     y0 = group(p, "group_p")
@@ -303,10 +296,10 @@
     )(here, pos, *spot)
     near = call(join_body, four, [VMEM] * 4)(p, q, x2, y0)
     near_c = core(near, "core_xy")
-    own_p, own_q = call(own_body, (wide, wide), [VMEM] * 6)(sc, near, *match)
+    own_p, own_q, part_x = call(own_body, (wide,) * 3, [VMEM] * 6)(sc, near, *match)
     y1 = call(take_body, one, [VMEM] * 2)(y1, own_q)
     y1_c = core(y1, "core_y")
-    part_x = call(mid_body, wide, [VMEM] * 4)(sc, near, near_c, y1)
+    part_x = call(mid_body, wide, [VMEM] * 5)(sc, near, near_c, y1, part_x)
     blocks = (sc, near, near_c, y1, y1_c, w2, *match, own_p, own_q)
     send, sum_p, sum_q = call(late_body, (one, wide, wide), [SMEM] + [VMEM] * 13)(
         here, part_x, *blocks

time: 63.8 us -> 63.8 us (level)
  transfers between devices with their start and end apart: 9 -> 9, of which waited for: 1 -> 2; matrix products, arithmetic and copies ran while one was open for 0% -> 0% of each run, Pallas kernels for 15% -> 15%
where the time goes in v8:
time: 63.8 us; the launch traced here: 63.3 us
  starting transfers between devices  46.1 us (72%)
  Pallas kernels  13.1 us (21%)
  between operations  2.14 us (3%)
  waiting for transfers between devices  2.04 us (3%)
    ppermute x9, starting transfers between devices, go(): return lax.ppermute(x, AXES, pairs)  46.1 us
    pallas_call x1, Pallas kernels, local(): call(visit_body, (wide, wide, part, part), [SMEM] + [VMEM] * 15, input_ou...  2.84 us
    pallas_call x1, Pallas kernels, local(): call(own_body, (wide,) * 3, [VMEM] * 6)(sc, near, *match)  2.27 us
    pallas_call x1, Pallas kernels, local(): call(rest_body, (wide, wide), [VMEM, SMEM] + [VMEM] * 8, (HBM, HBM), scra...  2.09 us
    ppermute x9, waiting for transfers between devices, go(): return lax.ppermute(x, AXES, pairs)  2.04 us
    pallas_call x1, Pallas kernels, local(): call(unit_body, (one, one) + place, [SMEM] + [HBM] * 3, scratch_shapes=re...  1.46 us
    pallas_call x1, Pallas kernels, local(): call(last_body, (wide, wide), [SMEM] + [VMEM] * 4 + [HBM] * 2, (HBM, HBM)...  1.32 us
  transfers between devices with their start and end apart: 9, of which 2 were waited for; matrix products, arithmetic and copies ran while one was open for 0% of the time, Pallas kernels for 15%

profile of v8, /device:TPU:1, one launch (start us, length us, event | category | flops | bytes accessed | tf_op | source)
XLA Modules:
  0.0 63.3 jit_solution(4397039317107434505)
XLA Ops:
  0.6 1.5 %unit.1 = (bf16[224,1152]{1,0:T(8,128)(2,1)S(1)}, bf16[224,1152]{1,0:T(8,128)(2,1)S(1)}, s32[224,1]{1,0:T(8,128)S(1)}, s32[4,224]{1,0:T(4,128)S(1)}, s32[224,1]{1,0:T(8,128)S(1)}, /*index=5*/s32[4,224]{1,0:T(4,128)S(1)}) custom-call(s32[1]{0:T(128)} %bitcast.here, bf16[224,1152]{1,0:T(8,128)(2,1)} %img.5, bf16[224,1152]{1,0:T(8,128)(2,1)} %txt.5, ...), custom_call_target="tpu_custom_call" | custom-call | flops 16000000000 | bytes 1 | tf_op jit(solution)/shard_map/unit/pallas_call | solution.py:278
  2.1 5.0 %collective-permute-start = (bf16[224,1152]{1,0:T(8,128)(2,1)S(1)}, bf16[224,1152]{1,0:T(8,128)(2,1)S(1)}, u32[]{:S(2)}, u32[]{:S(2)}) collective-permute-start(bf16[224,1152]{1,0:T(8,128)(2,1)S(1)} %get-tuple-element.25.q), channel_id=1, source_target_pairs={{0,2},{1,3},{2,0},{3,1},{4,6},{5,7},{6,4},{7,5},{8,10},{9,11},{10,... | collective-permute-start | bytes 1548296 | tf_op jit(solution)/shard_map/chip_q/ppermute | solution.py:257
  7.1 13.8 %collective-permute-start.1 = (bf16[224,1152]{1,0:T(8,128)(2,1)S(1)}, bf16[224,1152]{1,0:T(8,128)(2,1)S(1)}, u32[]{:S(2)}, u32[]{:S(2)}) collective-permute-start(bf16[224,1152]{1,0:T(8,128)(2,1)S(1)} %get-tuple-element.24.p), channel_id=1, source_target_pairs={{0,510},{1,511},{2,4},{3,5},{4,2},{5,3},{6,8},{7,9},{8,6},{9,7},{1... | collective-permute-start | bytes 1548296 | tf_op jit(solution)/shard_map/group_p/ppermute | solution.py:257
  20.9 0.0 collective-permute-done.x2
  20.9 11.3 %collective-permute-start.3 = (bf16[224,1152]{1,0:T(8,128)(2,1)S(1)}, bf16[224,1152]{1,0:T(8,128)(2,1)S(1)}, u32[]{:S(2)}, u32[]{:S(2)}) collective-permute-start(bf16[224,1152]{1,0:T(8,128)(2,1)S(1)} %collective-permute-done.x2), channel_id=1, source_target_pairs={{0,510},{1,511},{2,4},{3,5},{4,2},{5,3},{6,8},{7,9},{8,6},{9,7},{1... | collective-permute-start | bytes 1548296 | tf_op jit(solution)/shard_map/group_x2/ppermute | solution.py:257
  32.2 1.9 %collective-permute-start.5 = (bf16[224,1152]{1,0:T(8,128)(2,1)S(1)}, bf16[224,1152]{1,0:T(8,128)(2,1)S(1)}, u32[]{:S(2)}, u32[]{:S(2)}) collective-permute-start(bf16[224,1152]{1,0:T(8,128)(2,1)S(1)} %get-tuple-element.24.p), channel_id=1, source_target_pairs={{0,2},{1,3},{2,0},{3,1},{4,6},{5,7},{6,4},{7,5},{8,10},{9,11},{10,... | collective-permute-start | bytes 1548296 | tf_op jit(solution)/shard_map/chip_p/ppermute | solution.py:257
  34.1 1.1 %match.1 = (s32[224,1]{1,0:T(8,128)S(1)}, s32[4,224]{1,0:T(4,128)S(1)}, s32[224,1]{1,0:T(8,128)S(1)}, s32[4,224]{1,0:T(4,128)S(1)}) custom-call(s32[1]{0:T(128)} %bitcast.here, s32[1,896]{1,0:T(1,128)} %pos_far.3, s32[224,1]{1,0:T(8,128)S(1)} %get-tuple-element.26.rest_0_, ...), custom_call_target="tpu_custom_call", output_to_operand_aliasing={{0}: (2, {}), {1}: (3, {}), {2}: (4, {}), {3}: (5, {})} | custom-call | flops 1 | bytes 1 | tf_op jit(solution)/shard_map/match/pallas_call | solution.py:290
  36.6 0.0 collective-permute-done.1.y0
  36.6 0.2 join.1.near
  36.7 3.8 %collective-permute-start.2 = (bf16[896,1152]{1,0:T(8,128)(2,1)S(1)}, bf16[896,1152]{1,0:T(8,128)(2,1)S(1)}, u32[]{:S(2)}, u32[]{:S(2)}) collective-permute-start(bf16[896,1152]{1,0:T(8,128)(2,1)S(1)} %join.1.near), channel_id=1, source_target_pairs={{0,1},{1,0},{2,3},{3,2},{4,5},{5,4},{6,7},{7,6},{8,9},{9,8},{10,11... | collective-permute-start | bytes 6193160 | tf_op jit(solution)/shard_map/core_xy/ppermute | solution.py:257
  40.5 2.3 %own.1 = (f32[224,1152]{1,0:T(8,128)S(1)}, f32[224,1152]{1,0:T(8,128)S(1)}, f32[224,1152]{1,0:T(8,128)S(1)}) custom-call(f32[2,128]{1,0:T(2,128)S(1)} %nums.1.sc, bf16[896,1152]{1,0:T(8,128)(2,1)S(1)} %join.1.near, s32[224,1]{1,0:T(8,128)S(1)} %get-tuple-element.30.u_p.rest_1_.rest_0_, s32[4,224]{1,0:T(4,128)S(1)} %get-tuple-element.31.v_p.rest_2_.rest_1_, ...), custom_call_target="tpu_custom_call" | custom-call | flops 1 | bytes 1 | tf_op jit(solution)/shard_map/own/pallas_call | solution.py:299
  42.8 0.0 collective-permute-done.3.y
  42.9 4.0 %collective-permute-start.4 = (bf16[224,1152]{1,0:T(8,128)(2,1)S(1)}, bf16[224,1152]{1,0:T(8,128)(2,1)S(1)}, u32[]{:S(2)}, u32[]{:S(2)}) collective-permute-start(bf16[224,1152]{1,0:T(8,128)(2,1)S(1)} %take.1.y1), channel_id=1, source_target_pairs={{0,1},{1,0},{2,3},{3,2},{4,5},{5,4},{6,7},{7,6},{8,9},{9,8},{10,11... | collective-permute-start | bytes 1548296 | tf_op jit(solution)/shard_map/core_y/ppermute | solution.py:257
  46.9 0.0 collective-permute-done.2.near_c
  46.9 0.9 %mid.1.part = f32[224,1152]{1,0:T(8,128)S(1)} custom-call(f32[2,128]{1,0:T(2,128)S(1)} %nums.1.sc, bf16[896,1152]{1,0:T(8,128)(2,1)S(1)} %join.1.near, bf16[896,1152]{1,0:T(8,128)(2,1)S(1)} %collective-permute-done.2.near_c, bf16[224,1152]{1,0:T(8,128)(2,1)S(1)} %take.1.y1, f32[224,1152]{1,0:T(8,128)S(1)} %get-tuple-element.35.part), custom_call_target="tpu_custom_call" | custom-call | flops 1 | bytes 1 | tf_op jit(solution)/shard_map/mid/pallas_call | solution.py:302
  47.8 0.0 collective-permute-done.5.rest_0_.w2
  47.8 0.5 collective-permute-done.4.y1_c
  48.4 0.8 %late.1 = (bf16[224,1152]{1,0:T(8,128)(2,1)S(1)}, f32[224,1152]{1,0:T(8,128)S(1)}, f32[224,1152]{1,0:T(8,128)S(1)}) custom-call(s32[1]{0:T(128)} %bitcast.here, f32[224,1152]{1,0:T(8,128)S(1)} %mid.1.part, f32[2,128]{1,0:T(2,128)S(1)} %nums.1.sc, bf16[896,1152]{1,0:T(8,128)(2,1)S(1)} %join.1.near, bf16[896,1152]{1,0:T(8,128)(2,1)S(1)} %collective-permute-done.2.near_c, ...), custom_call_target="tpu_custom_call" | custom-call | flops 1 | bytes 1 | tf_op jit(solution)/shard_map/late/pallas_call | solution.py:304
  49.2 1.9 %collective-permute-start.6 = (bf16[224,1152]{1,0:T(8,128)(2,1)S(1)}, bf16[224,1152]{1,0:T(8,128)(2,1)S(1)}, u32[]{:S(2)}, u32[]{:S(2)}) collective-permute-start(bf16[224,1152]{1,0:T(8,128)(2,1)S(1)} %get-tuple-element.37._send), channel_id=1, source_target_pairs={{0,2},{1,3},{2,0},{3,1},{4,6},{5,7},{6,4},{7,5},{8,10},{9,11},{10,... | collective-permute-start | bytes 1548296 | tf_op jit(solution)/shard_map/chip_send/ppermute | solution.py:257
  51.2 0.0 copy-start
  51.2 0.0 copy-start.1
  51.2 2.8 %visit.1 = (f32[224,1152]{1,0:T(8,128)S(1)}, f32[224,1152]{1,0:T(8,128)S(1)}, bf16[112,1152]{1,0:T(8,128)(2,1)S(1)}, bf16[112,1152]{1,0:T(8,128)(2,1)S(1)}) custom-call(s32[1]{0:T(128)} %bitcast.here, bf16[224,1152]{1,0:T(8,128)(2,1)S(1)} %get-tuple-element.37._send, ...), custom_call_target="tpu_custom_call", output_to_operand_aliasing={{0}: (2, {}), {1}: (3, {})} | custom-call | flops 1 | bytes 1 | tf_op jit(solution)/shard_map/visit/pallas_call | solution.py:308
  54.0 2.5 %collective-permute-start.7 = (bf16[112,1152]{1,0:T(8,128)(2,1)S(1)}, bf16[112,1152]{1,0:T(8,128)(2,1)S(1)}, u32[]{:S(2)}, u32[]{:S(2)}) collective-permute-start(bf16[112,1152]{1,0:T(8,128)(2,1)S(1)} %get-tuple-element.41), channel_id=1, source_target_pairs={{0,1},{1,0},{2,3},{3,2},{4,5},{5,4},{6,7},{7,6},{8,9},{9,8},{10,11... | collective-permute-start | bytes 774152 | tf_op jit(solution)/shard_map/core_w_lo/ppermute | solution.py:257
  56.5 1.9 %collective-permute-start.8 = (bf16[112,1152]{1,0:T(8,128)(2,1)S(1)}, bf16[112,1152]{1,0:T(8,128)(2,1)S(1)}, u32[]{:S(2)}, u32[]{:S(2)}) collective-permute-start(bf16[112,1152]{1,0:T(8,128)(2,1)S(1)} %get-tuple-element.42), channel_id=1, source_target_pairs={{0,1},{1,0},{2,3},{3,2},{4,5},{5,4},{6,7},{7,6},{8,9},{9,8},{10,11... | collective-permute-start | bytes 774152 | tf_op jit(solution)/shard_map/core_w_hi/ppermute | solution.py:257
  58.4 0.0 collective-permute-done.7.w2_lo_c
  58.4 1.5 %collective-permute-done.8.w2_hi_c = bf16[112,1152]{1,0:T(8,128)(2,1)S(1)} collective-permute-done((bf16[112,1152]{1,0:T(8,128)(2,1)S(1)}, bf16[112,1152]{1,0:T(8,128)(2,1)S(1)}, u32[]{:S(2)}, u32[]{:S(2)}) %collective-permute-start.8) | collective-permute-done | bytes 258080 | tf_op jit(solution)/shard_map/core_w_hi/ppermute | solution.py:257
  59.9 0.0 copy-done
  59.9 0.0 copy-done.1
  59.9 2.1 %rest.1 = (f32[224,1152]{1,0:T(8,128)}, f32[224,1152]{1,0:T(8,128)}) custom-call(f32[2,128]{1,0:T(2,128)S(1)} %nums.1.sc, s32[1]{0:T(128)} %bitcast.here, bf16[224,1152]{1,0:T(8,128)(2,1)S(1)} %copy-done, bf16[224,1152]{1,0:T(8,128)(2,1)S(1)} %copy-done.1, bf16[224,1152]{1,0:T(8,128)(2,1)S(1)} %get-tuple-element.24.p, ...), custom_call_target="tpu_custom_call" | custom-call | flops 1 | bytes 1 | tf_op jit(solution)/shard_map/rest/pallas_call | solution.py:315
  62.0 0.0 collective-permute-done.6.back
  62.0 1.3 %last.1 = (f32[224,1152]{1,0:T(8,128)}, f32[224,1152]{1,0:T(8,128)}) custom-call(s32[1]{0:T(128)} %bitcast.here, bf16[224,1152]{1,0:T(8,128)(2,1)S(1)} %copy-done, bf16[224,1152]{1,0:T(8,128)(2,1)S(1)} %copy-done.1, f32[224,1152]{1,0:T(8,128)S(1)} %get-tuple-element.40.sum_q, ...), custom_call_target="tpu_custom_call", output_to_operand_aliasing={{0}: (5, {}), {1}: (6, {})} | custom-call | flops 64000000000 | bytes 1 | tf_op jit(solution)/shard_map/last/pallas_call | solution.py:322
  (2 shorter events, 0.0 us)
Async XLA Ops:
  2.1 18.8 %collective-permute-start = (bf16[224,1152]{1,0:T(8,128)(2,1)S(1)}, bf16[224,1152]{1,0:T(8,128)(2,1)S(1)}, u32[]{:S(2)}, u32[]{:S(2)}) collective-permute-start(bf16[224,1152]{1,0:T(8,128)(2,1)S(1)} %get-tuple-element.25.q), channel_id=1, source_target_pairs={{0,2},{1,3},{2,0},{3,1},{4,6},{5,7},{6,4},{7,5},{8,10},{9,11},{10,... | collective-permute-start | bytes 1548296 | tf_op jit(solution)/shard_map/chip_q/ppermute | solution.py:257
  7.1 29.5 %collective-permute-start.1 = (bf16[224,1152]{1,0:T(8,128)(2,1)S(1)}, bf16[224,1152]{1,0:T(8,128)(2,1)S(1)}, u32[]{:S(2)}, u32[]{:S(2)}) collective-permute-start(bf16[224,1152]{1,0:T(8,128)(2,1)S(1)} %get-tuple-element.24.p), channel_id=1, source_target_pairs={{0,510},{1,511},{2,4},{3,5},{4,2},{5,3},{6,8},{7,9},{8,6},{9,7},{1... | collective-permute-start | bytes 1548296 | tf_op jit(solution)/shard_map/group_p/ppermute | solution.py:257
  20.9 21.9 %collective-permute-start.3 = (bf16[224,1152]{1,0:T(8,128)(2,1)S(1)}, bf16[224,1152]{1,0:T(8,128)(2,1)S(1)}, u32[]{:S(2)}, u32[]{:S(2)}) collective-permute-start(bf16[224,1152]{1,0:T(8,128)(2,1)S(1)} %collective-permute-done.x2), channel_id=1, source_target_pairs={{0,510},{1,511},{2,4},{3,5},{4,2},{5,3},{6,8},{7,9},{8,6},{9,7},{1... | collective-permute-start | bytes 1548296 | tf_op jit(solution)/shard_map/group_x2/ppermute | solution.py:257
  32.2 15.6 %collective-permute-start.5 = (bf16[224,1152]{1,0:T(8,128)(2,1)S(1)}, bf16[224,1152]{1,0:T(8,128)(2,1)S(1)}, u32[]{:S(2)}, u32[]{:S(2)}) collective-permute-start(bf16[224,1152]{1,0:T(8,128)(2,1)S(1)} %get-tuple-element.24.p), channel_id=1, source_target_pairs={{0,2},{1,3},{2,0},{3,1},{4,6},{5,7},{6,4},{7,5},{8,10},{9,11},{10,... | collective-permute-start | bytes 1548296 | tf_op jit(solution)/shard_map/chip_p/ppermute | solution.py:257
  36.7 10.1 %collective-permute-start.2 = (bf16[896,1152]{1,0:T(8,128)(2,1)S(1)}, bf16[896,1152]{1,0:T(8,128)(2,1)S(1)}, u32[]{:S(2)}, u32[]{:S(2)}) collective-permute-start(bf16[896,1152]{1,0:T(8,128)(2,1)S(1)} %join.1.near), channel_id=1, source_target_pairs={{0,1},{1,0},{2,3},{3,2},{4,5},{5,4},{6,7},{7,6},{8,9},{9,8},{10,11... | collective-permute-start | bytes 6193160 | tf_op jit(solution)/shard_map/core_xy/ppermute | solution.py:257
  42.9 5.5 %collective-permute-start.4 = (bf16[224,1152]{1,0:T(8,128)(2,1)S(1)}, bf16[224,1152]{1,0:T(8,128)(2,1)S(1)}, u32[]{:S(2)}, u32[]{:S(2)}) collective-permute-start(bf16[224,1152]{1,0:T(8,128)(2,1)S(1)} %take.1.y1), channel_id=1, source_target_pairs={{0,1},{1,0},{2,3},{3,2},{4,5},{5,4},{6,7},{7,6},{8,9},{9,8},{10,11... | collective-permute-start | bytes 1548296 | tf_op jit(solution)/shard_map/core_y/ppermute | solution.py:257
  49.2 12.8 %collective-permute-start.6 = (bf16[224,1152]{1,0:T(8,128)(2,1)S(1)}, bf16[224,1152]{1,0:T(8,128)(2,1)S(1)}, u32[]{:S(2)}, u32[]{:S(2)}) collective-permute-start(bf16[224,1152]{1,0:T(8,128)(2,1)S(1)} %get-tuple-element.37._send), channel_id=1, source_target_pairs={{0,2},{1,3},{2,0},{3,1},{4,6},{5,7},{6,4},{7,5},{8,10},{9,11},{10,... | collective-permute-start | bytes 1548296 | tf_op jit(solution)/shard_map/chip_send/ppermute | solution.py:257
  51.2 8.8 %copy-start = (bf16[224,1152]{1,0:T(8,128)(2,1)S(1)}, bf16[224,1152]{1,0:T(8,128)(2,1)}, u32[]{:S(2)}) copy-start(bf16[224,1152]{1,0:T(8,128)(2,1)} %img.5) | copy-start | bytes 1548292
  51.2 8.8 %copy-start.1 = (bf16[224,1152]{1,0:T(8,128)(2,1)S(1)}, bf16[224,1152]{1,0:T(8,128)(2,1)}, u32[]{:S(2)}) copy-start(bf16[224,1152]{1,0:T(8,128)(2,1)} %txt.5) | copy-start | bytes 1548292
  54.0 4.4 %collective-permute-start.7 = (bf16[112,1152]{1,0:T(8,128)(2,1)S(1)}, bf16[112,1152]{1,0:T(8,128)(2,1)S(1)}, u32[]{:S(2)}, u32[]{:S(2)}) collective-permute-start(bf16[112,1152]{1,0:T(8,128)(2,1)S(1)} %get-tuple-element.41), channel_id=1, source_target_pairs={{0,1},{1,0},{2,3},{3,2},{4,5},{5,4},{6,7},{7,6},{8,9},{9,8},{10,11... | collective-permute-start | bytes 774152 | tf_op jit(solution)/shard_map/core_w_lo/ppermute | solution.py:257
  56.5 3.4 %collective-permute-start.8 = (bf16[112,1152]{1,0:T(8,128)(2,1)S(1)}, bf16[112,1152]{1,0:T(8,128)(2,1)S(1)}, u32[]{:S(2)}, u32[]{:S(2)}) collective-permute-start(bf16[112,1152]{1,0:T(8,128)(2,1)S(1)} %get-tuple-element.42), channel_id=1, source_target_pairs={{0,1},{1,0},{2,3},{3,2},{4,5},{5,4},{6,7},{7,6},{8,9},{9,8},{10,11... | collective-permute-start | bytes 774152 | tf_op jit(solution)/shard_map/core_w_hi/ppermute | solution.py:257

commit v9 on v8

--- a/solution.py
+++ b/solution.py
@@ -127,13 +127,17 @@
 
 def terms(x, ys, sc, positive=None):
     scale, shift = sc[0:1, 0:1], sc[1:2, 0:1]
-    total = None
-    for j, y in enumerate(ys):
-        g = lax.logistic(scale * dot(x, y, NT) + shift)
+    logits = [scale * dot(x, y, NT) + shift for y in ys]
+    weights = []
+    for j, logit in enumerate(logits):
+        g = lax.logistic(logit)
         if positive is not None:
             u, v = positive
             g = g - (u == v[j]).astype(jnp.float32)
-        term = dot((scale * g).astype(jnp.bfloat16), y, NN)
+        weights.append((scale * g).astype(jnp.bfloat16))
+    total = None
+    for g, y in zip(weights, ys):
+        term = dot(g, y, NN)
         total = term if total is None else total + term
     return total
 

time: 63.8 us -> 63.5 us (level)
  transfers between devices with their start and end apart: 9 -> 9, of which waited for: 2 -> 2; matrix products, arithmetic and copies ran while one was open for 0% -> 0% of each run, Pallas kernels for 15% -> 14%
where the time goes in v9:
time: 63.5 us; the launch traced here: 63 us
  starting transfers between devices  46.1 us (73%)
  Pallas kernels  12.7 us (20%)
  between operations  2.14 us (3%)
  waiting for transfers between devices  2.04 us (3%)
    ppermute x9, starting transfers between devices, go(): return lax.ppermute(x, AXES, pairs)  46.1 us
    pallas_call x1, Pallas kernels, local(): call(visit_body, (wide, wide, part, part), [SMEM] + [VMEM] * 15, input_ou...  2.53 us
    pallas_call x1, Pallas kernels, local(): call(own_body, (wide,) * 3, [VMEM] * 6)(sc, near, *match)  2.27 us
    pallas_call x1, Pallas kernels, local(): call(rest_body, (wide, wide), [VMEM, SMEM] + [VMEM] * 8, (HBM, HBM), scra...  2.09 us
    ppermute x9, waiting for transfers between devices, go(): return lax.ppermute(x, AXES, pairs)  2.04 us
    pallas_call x1, Pallas kernels, local(): call(unit_body, (one, one) + place, [SMEM] + [HBM] * 3, scratch_shapes=re...  1.46 us
    pallas_call x1, Pallas kernels, local(): call(last_body, (wide, wide), [SMEM] + [VMEM] * 4 + [HBM] * 2, (HBM, HBM)...  1.32 us
  transfers between devices with their start and end apart: 9, of which 2 were waited for; matrix products, arithmetic and copies ran while one was open for 0% of the time, Pallas kernels for 14%

profile of v9, /device:TPU:1, one launch (start us, length us, event | category | flops | bytes accessed | tf_op | source)
XLA Modules:
  0.0 63.0 jit_solution(2507039850214554736)
XLA Ops:
  0.6 1.5 %unit.1 = (bf16[224,1152]{1,0:T(8,128)(2,1)S(1)}, bf16[224,1152]{1,0:T(8,128)(2,1)S(1)}, s32[224,1]{1,0:T(8,128)S(1)}, s32[4,224]{1,0:T(4,128)S(1)}, s32[224,1]{1,0:T(8,128)S(1)}, /*index=5*/s32[4,224]{1,0:T(4,128)S(1)}) custom-call(s32[1]{0:T(128)} %bitcast.here, bf16[224,1152]{1,0:T(8,128)(2,1)} %img.5, bf16[224,1152]{1,0:T(8,128)(2,1)} %txt.5, ...), custom_call_target="tpu_custom_call" | custom-call | flops 16000000000 | bytes 1 | tf_op jit(solution)/shard_map/unit/pallas_call | solution.py:282
  2.1 5.0 %collective-permute-start = (bf16[224,1152]{1,0:T(8,128)(2,1)S(1)}, bf16[224,1152]{1,0:T(8,128)(2,1)S(1)}, u32[]{:S(2)}, u32[]{:S(2)}) collective-permute-start(bf16[224,1152]{1,0:T(8,128)(2,1)S(1)} %get-tuple-element.25.q), channel_id=1, source_target_pairs={{0,2},{1,3},{2,0},{3,1},{4,6},{5,7},{6,4},{7,5},{8,10},{9,11},{10,... | collective-permute-start | bytes 1548296 | tf_op jit(solution)/shard_map/chip_q/ppermute | solution.py:261
  7.1 13.8 %collective-permute-start.1 = (bf16[224,1152]{1,0:T(8,128)(2,1)S(1)}, bf16[224,1152]{1,0:T(8,128)(2,1)S(1)}, u32[]{:S(2)}, u32[]{:S(2)}) collective-permute-start(bf16[224,1152]{1,0:T(8,128)(2,1)S(1)} %get-tuple-element.24.p), channel_id=1, source_target_pairs={{0,510},{1,511},{2,4},{3,5},{4,2},{5,3},{6,8},{7,9},{8,6},{9,7},{1... | collective-permute-start | bytes 1548296 | tf_op jit(solution)/shard_map/group_p/ppermute | solution.py:261
  20.9 0.0 collective-permute-done.x2
  20.9 11.3 %collective-permute-start.3 = (bf16[224,1152]{1,0:T(8,128)(2,1)S(1)}, bf16[224,1152]{1,0:T(8,128)(2,1)S(1)}, u32[]{:S(2)}, u32[]{:S(2)}) collective-permute-start(bf16[224,1152]{1,0:T(8,128)(2,1)S(1)} %collective-permute-done.x2), channel_id=1, source_target_pairs={{0,510},{1,511},{2,4},{3,5},{4,2},{5,3},{6,8},{7,9},{8,6},{9,7},{1... | collective-permute-start | bytes 1548296 | tf_op jit(solution)/shard_map/group_x2/ppermute | solution.py:261
  32.2 1.9 %collective-permute-start.5 = (bf16[224,1152]{1,0:T(8,128)(2,1)S(1)}, bf16[224,1152]{1,0:T(8,128)(2,1)S(1)}, u32[]{:S(2)}, u32[]{:S(2)}) collective-permute-start(bf16[224,1152]{1,0:T(8,128)(2,1)S(1)} %get-tuple-element.24.p), channel_id=1, source_target_pairs={{0,2},{1,3},{2,0},{3,1},{4,6},{5,7},{6,4},{7,5},{8,10},{9,11},{10,... | collective-permute-start | bytes 1548296 | tf_op jit(solution)/shard_map/chip_p/ppermute | solution.py:261
  34.1 1.1 %match.1 = (s32[224,1]{1,0:T(8,128)S(1)}, s32[4,224]{1,0:T(4,128)S(1)}, s32[224,1]{1,0:T(8,128)S(1)}, s32[4,224]{1,0:T(4,128)S(1)}) custom-call(s32[1]{0:T(128)} %bitcast.here, s32[1,896]{1,0:T(1,128)} %pos_far.3, s32[224,1]{1,0:T(8,128)S(1)} %get-tuple-element.26.rest_0_, ...), custom_call_target="tpu_custom_call", output_to_operand_aliasing={{0}: (2, {}), {1}: (3, {}), {2}: (4, {}), {3}: (5, {})} | custom-call | flops 1 | bytes 1 | tf_op jit(solution)/shard_map/match/pallas_call | solution.py:294
  36.6 0.0 collective-permute-done.1.y0
  36.6 0.2 join.1.near
  36.7 3.8 %collective-permute-start.2 = (bf16[896,1152]{1,0:T(8,128)(2,1)S(1)}, bf16[896,1152]{1,0:T(8,128)(2,1)S(1)}, u32[]{:S(2)}, u32[]{:S(2)}) collective-permute-start(bf16[896,1152]{1,0:T(8,128)(2,1)S(1)} %join.1.near), channel_id=1, source_target_pairs={{0,1},{1,0},{2,3},{3,2},{4,5},{5,4},{6,7},{7,6},{8,9},{9,8},{10,11... | collective-permute-start | bytes 6193160 | tf_op jit(solution)/shard_map/core_xy/ppermute | solution.py:261
  40.5 2.3 %own.1 = (f32[224,1152]{1,0:T(8,128)S(1)}, f32[224,1152]{1,0:T(8,128)S(1)}, f32[224,1152]{1,0:T(8,128)S(1)}) custom-call(f32[2,128]{1,0:T(2,128)S(1)} %nums.1.sc, bf16[896,1152]{1,0:T(8,128)(2,1)S(1)} %join.1.near, s32[224,1]{1,0:T(8,128)S(1)} %get-tuple-element.30.u_p.rest_1_.rest_0_, s32[4,224]{1,0:T(4,128)S(1)} %get-tuple-element.31.v_p.rest_2_.rest_1_, ...), custom_call_target="tpu_custom_call" | custom-call | flops 1 | bytes 1 | tf_op jit(solution)/shard_map/own/pallas_call | solution.py:303
  42.8 0.0 collective-permute-done.3.y
  42.9 4.0 %collective-permute-start.4 = (bf16[224,1152]{1,0:T(8,128)(2,1)S(1)}, bf16[224,1152]{1,0:T(8,128)(2,1)S(1)}, u32[]{:S(2)}, u32[]{:S(2)}) collective-permute-start(bf16[224,1152]{1,0:T(8,128)(2,1)S(1)} %take.1.y1), channel_id=1, source_target_pairs={{0,1},{1,0},{2,3},{3,2},{4,5},{5,4},{6,7},{7,6},{8,9},{9,8},{10,11... | collective-permute-start | bytes 1548296 | tf_op jit(solution)/shard_map/core_y/ppermute | solution.py:261
  46.9 0.0 collective-permute-done.2.near_c
  46.9 0.9 %mid.1.part = f32[224,1152]{1,0:T(8,128)S(1)} custom-call(f32[2,128]{1,0:T(2,128)S(1)} %nums.1.sc, bf16[896,1152]{1,0:T(8,128)(2,1)S(1)} %join.1.near, bf16[896,1152]{1,0:T(8,128)(2,1)S(1)} %collective-permute-done.2.near_c, bf16[224,1152]{1,0:T(8,128)(2,1)S(1)} %take.1.y1, f32[224,1152]{1,0:T(8,128)S(1)} %get-tuple-element.35.part), custom_call_target="tpu_custom_call" | custom-call | flops 1 | bytes 1 | tf_op jit(solution)/shard_map/mid/pallas_call | solution.py:306
  47.8 0.0 collective-permute-done.5.rest_0_.w2
  47.8 0.5 collective-permute-done.4.y1_c
  48.4 0.8 %late.1 = (bf16[224,1152]{1,0:T(8,128)(2,1)S(1)}, f32[224,1152]{1,0:T(8,128)S(1)}, f32[224,1152]{1,0:T(8,128)S(1)}) custom-call(s32[1]{0:T(128)} %bitcast.here, f32[224,1152]{1,0:T(8,128)S(1)} %mid.1.part, f32[2,128]{1,0:T(2,128)S(1)} %nums.1.sc, bf16[896,1152]{1,0:T(8,128)(2,1)S(1)} %join.1.near, bf16[896,1152]{1,0:T(8,128)(2,1)S(1)} %collective-permute-done.2.near_c, ...), custom_call_target="tpu_custom_call" | custom-call | flops 1 | bytes 1 | tf_op jit(solution)/shard_map/late/pallas_call | solution.py:308
  49.2 1.9 %collective-permute-start.6 = (bf16[224,1152]{1,0:T(8,128)(2,1)S(1)}, bf16[224,1152]{1,0:T(8,128)(2,1)S(1)}, u32[]{:S(2)}, u32[]{:S(2)}) collective-permute-start(bf16[224,1152]{1,0:T(8,128)(2,1)S(1)} %get-tuple-element.37._send), channel_id=1, source_target_pairs={{0,2},{1,3},{2,0},{3,1},{4,6},{5,7},{6,4},{7,5},{8,10},{9,11},{10,... | collective-permute-start | bytes 1548296 | tf_op jit(solution)/shard_map/chip_send/ppermute | solution.py:261
  51.2 0.0 copy-start
  51.2 0.0 copy-start.1
  51.2 2.5 %visit.1 = (f32[224,1152]{1,0:T(8,128)S(1)}, f32[224,1152]{1,0:T(8,128)S(1)}, bf16[112,1152]{1,0:T(8,128)(2,1)S(1)}, bf16[112,1152]{1,0:T(8,128)(2,1)S(1)}) custom-call(s32[1]{0:T(128)} %bitcast.here, bf16[224,1152]{1,0:T(8,128)(2,1)S(1)} %get-tuple-element.37._send, ...), custom_call_target="tpu_custom_call", output_to_operand_aliasing={{0}: (2, {}), {1}: (3, {})} | custom-call | flops 1 | bytes 1 | tf_op jit(solution)/shard_map/visit/pallas_call | solution.py:312
  53.7 2.5 %collective-permute-start.7 = (bf16[112,1152]{1,0:T(8,128)(2,1)S(1)}, bf16[112,1152]{1,0:T(8,128)(2,1)S(1)}, u32[]{:S(2)}, u32[]{:S(2)}) collective-permute-start(bf16[112,1152]{1,0:T(8,128)(2,1)S(1)} %get-tuple-element.41), channel_id=1, source_target_pairs={{0,1},{1,0},{2,3},{3,2},{4,5},{5,4},{6,7},{7,6},{8,9},{9,8},{10,11... | collective-permute-start | bytes 774152 | tf_op jit(solution)/shard_map/core_w_lo/ppermute | solution.py:261
  56.2 1.9 %collective-permute-start.8 = (bf16[112,1152]{1,0:T(8,128)(2,1)S(1)}, bf16[112,1152]{1,0:T(8,128)(2,1)S(1)}, u32[]{:S(2)}, u32[]{:S(2)}) collective-permute-start(bf16[112,1152]{1,0:T(8,128)(2,1)S(1)} %get-tuple-element.42), channel_id=1, source_target_pairs={{0,1},{1,0},{2,3},{3,2},{4,5},{5,4},{6,7},{7,6},{8,9},{9,8},{10,11... | collective-permute-start | bytes 774152 | tf_op jit(solution)/shard_map/core_w_hi/ppermute | solution.py:261
  58.1 0.0 collective-permute-done.7.w2_lo_c
  58.1 1.5 %collective-permute-done.8.w2_hi_c = bf16[112,1152]{1,0:T(8,128)(2,1)S(1)} collective-permute-done((bf16[112,1152]{1,0:T(8,128)(2,1)S(1)}, bf16[112,1152]{1,0:T(8,128)(2,1)S(1)}, u32[]{:S(2)}, u32[]{:S(2)}) %collective-permute-start.8) | collective-permute-done | bytes 258080 | tf_op jit(solution)/shard_map/core_w_hi/ppermute | solution.py:261
  59.6 0.0 copy-done
  59.6 0.0 copy-done.1
  59.6 2.1 %rest.1 = (f32[224,1152]{1,0:T(8,128)}, f32[224,1152]{1,0:T(8,128)}) custom-call(f32[2,128]{1,0:T(2,128)S(1)} %nums.1.sc, s32[1]{0:T(128)} %bitcast.here, bf16[224,1152]{1,0:T(8,128)(2,1)S(1)} %copy-done, bf16[224,1152]{1,0:T(8,128)(2,1)S(1)} %copy-done.1, bf16[224,1152]{1,0:T(8,128)(2,1)S(1)} %get-tuple-element.24.p, ...), custom_call_target="tpu_custom_call" | custom-call | flops 1 | bytes 1 | tf_op jit(solution)/shard_map/rest/pallas_call | solution.py:319
  61.7 0.0 collective-permute-done.6.back
  61.7 1.3 %last.1 = (f32[224,1152]{1,0:T(8,128)}, f32[224,1152]{1,0:T(8,128)}) custom-call(s32[1]{0:T(128)} %bitcast.here, bf16[224,1152]{1,0:T(8,128)(2,1)S(1)} %copy-done, bf16[224,1152]{1,0:T(8,128)(2,1)S(1)} %copy-done.1, f32[224,1152]{1,0:T(8,128)S(1)} %get-tuple-element.40.sum_q, ...), custom_call_target="tpu_custom_call", output_to_operand_aliasing={{0}: (5, {}), {1}: (6, {})} | custom-call | flops 64000000000 | bytes 1 | tf_op jit(solution)/shard_map/last/pallas_call | solution.py:326
  (2 shorter events, 0.0 us)
Async XLA Ops:
  2.1 18.8 %collective-permute-start = (bf16[224,1152]{1,0:T(8,128)(2,1)S(1)}, bf16[224,1152]{1,0:T(8,128)(2,1)S(1)}, u32[]{:S(2)}, u32[]{:S(2)}) collective-permute-start(bf16[224,1152]{1,0:T(8,128)(2,1)S(1)} %get-tuple-element.25.q), channel_id=1, source_target_pairs={{0,2},{1,3},{2,0},{3,1},{4,6},{5,7},{6,4},{7,5},{8,10},{9,11},{10,... | collective-permute-start | bytes 1548296 | tf_op jit(solution)/shard_map/chip_q/ppermute | solution.py:261
  7.1 29.5 %collective-permute-start.1 = (bf16[224,1152]{1,0:T(8,128)(2,1)S(1)}, bf16[224,1152]{1,0:T(8,128)(2,1)S(1)}, u32[]{:S(2)}, u32[]{:S(2)}) collective-permute-start(bf16[224,1152]{1,0:T(8,128)(2,1)S(1)} %get-tuple-element.24.p), channel_id=1, source_target_pairs={{0,510},{1,511},{2,4},{3,5},{4,2},{5,3},{6,8},{7,9},{8,6},{9,7},{1... | collective-permute-start | bytes 1548296 | tf_op jit(solution)/shard_map/group_p/ppermute | solution.py:261
  20.9 21.9 %collective-permute-start.3 = (bf16[224,1152]{1,0:T(8,128)(2,1)S(1)}, bf16[224,1152]{1,0:T(8,128)(2,1)S(1)}, u32[]{:S(2)}, u32[]{:S(2)}) collective-permute-start(bf16[224,1152]{1,0:T(8,128)(2,1)S(1)} %collective-permute-done.x2), channel_id=1, source_target_pairs={{0,510},{1,511},{2,4},{3,5},{4,2},{5,3},{6,8},{7,9},{8,6},{9,7},{1... | collective-permute-start | bytes 1548296 | tf_op jit(solution)/shard_map/group_x2/ppermute | solution.py:261
  32.2 15.6 %collective-permute-start.5 = (bf16[224,1152]{1,0:T(8,128)(2,1)S(1)}, bf16[224,1152]{1,0:T(8,128)(2,1)S(1)}, u32[]{:S(2)}, u32[]{:S(2)}) collective-permute-start(bf16[224,1152]{1,0:T(8,128)(2,1)S(1)} %get-tuple-element.24.p), channel_id=1, source_target_pairs={{0,2},{1,3},{2,0},{3,1},{4,6},{5,7},{6,4},{7,5},{8,10},{9,11},{10,... | collective-permute-start | bytes 1548296 | tf_op jit(solution)/shard_map/chip_p/ppermute | solution.py:261
  36.7 10.1 %collective-permute-start.2 = (bf16[896,1152]{1,0:T(8,128)(2,1)S(1)}, bf16[896,1152]{1,0:T(8,128)(2,1)S(1)}, u32[]{:S(2)}, u32[]{:S(2)}) collective-permute-start(bf16[896,1152]{1,0:T(8,128)(2,1)S(1)} %join.1.near), channel_id=1, source_target_pairs={{0,1},{1,0},{2,3},{3,2},{4,5},{5,4},{6,7},{7,6},{8,9},{9,8},{10,11... | collective-permute-start | bytes 6193160 | tf_op jit(solution)/shard_map/core_xy/ppermute | solution.py:261
  42.9 5.5 %collective-permute-start.4 = (bf16[224,1152]{1,0:T(8,128)(2,1)S(1)}, bf16[224,1152]{1,0:T(8,128)(2,1)S(1)}, u32[]{:S(2)}, u32[]{:S(2)}) collective-permute-start(bf16[224,1152]{1,0:T(8,128)(2,1)S(1)} %take.1.y1), channel_id=1, source_target_pairs={{0,1},{1,0},{2,3},{3,2},{4,5},{5,4},{6,7},{7,6},{8,9},{9,8},{10,11... | collective-permute-start | bytes 1548296 | tf_op jit(solution)/shard_map/core_y/ppermute | solution.py:261
  49.2 12.5 %collective-permute-start.6 = (bf16[224,1152]{1,0:T(8,128)(2,1)S(1)}, bf16[224,1152]{1,0:T(8,128)(2,1)S(1)}, u32[]{:S(2)}, u32[]{:S(2)}) collective-permute-start(bf16[224,1152]{1,0:T(8,128)(2,1)S(1)} %get-tuple-element.37._send), channel_id=1, source_target_pairs={{0,2},{1,3},{2,0},{3,1},{4,6},{5,7},{6,4},{7,5},{8,10},{9,11},{10,... | collective-permute-start | bytes 1548296 | tf_op jit(solution)/shard_map/chip_send/ppermute | solution.py:261
  51.2 8.5 %copy-start = (bf16[224,1152]{1,0:T(8,128)(2,1)S(1)}, bf16[224,1152]{1,0:T(8,128)(2,1)}, u32[]{:S(2)}) copy-start(bf16[224,1152]{1,0:T(8,128)(2,1)} %img.5) | copy-start | bytes 1548292
  51.2 8.4 %copy-start.1 = (bf16[224,1152]{1,0:T(8,128)(2,1)S(1)}, bf16[224,1152]{1,0:T(8,128)(2,1)}, u32[]{:S(2)}) copy-start(bf16[224,1152]{1,0:T(8,128)(2,1)} %txt.5) | copy-start | bytes 1548292
  53.7 4.4 %collective-permute-start.7 = (bf16[112,1152]{1,0:T(8,128)(2,1)S(1)}, bf16[112,1152]{1,0:T(8,128)(2,1)S(1)}, u32[]{:S(2)}, u32[]{:S(2)}) collective-permute-start(bf16[112,1152]{1,0:T(8,128)(2,1)S(1)} %get-tuple-element.41), channel_id=1, source_target_pairs={{0,1},{1,0},{2,3},{3,2},{4,5},{5,4},{6,7},{7,6},{8,9},{9,8},{10,11... | collective-permute-start | bytes 774152 | tf_op jit(solution)/shard_map/core_w_lo/ppermute | solution.py:261
  56.2 3.4 %collective-permute-start.8 = (bf16[112,1152]{1,0:T(8,128)(2,1)S(1)}, bf16[112,1152]{1,0:T(8,128)(2,1)S(1)}, u32[]{:S(2)}, u32[]{:S(2)}) collective-permute-start(bf16[112,1152]{1,0:T(8,128)(2,1)S(1)} %get-tuple-element.42), channel_id=1, source_target_pairs={{0,1},{1,0},{2,3},{3,2},{4,5},{5,4},{6,7},{7,6},{8,9},{9,8},{10,11... | collective-permute-start | bytes 774152 | tf_op jit(solution)/shard_map/core_w_hi/ppermute | solution.py:261

commit v10 on v9

--- a/solution.py
+++ b/solution.py
@@ -171,11 +171,10 @@
 def far_sums(sc, near, near_c, y1, y1_c, w2, u_p, v_p, u_q, v_q, own_p, own_q, sum_p, sum_q):
     x, y = block(near, 0), block(near, 1)
     x_c, y_c, x2_c, y0_c = (block(near_c, j) for j in range(4))
-    sum_p[...] = (
-        own_p[...]
-        + terms(x, [y_c, w2[...]], sc, (u_p[...], [v_p[1:2], v_p[2:3]]))
-        + terms(x, [y0_c, y1[...], y1_c[...]], sc)
-    )
+    none = jnp.full((1, x.shape[0]), -1, jnp.int32)
+    columns = [v_p[1:2], v_p[2:3], none, none, none]
+    blocks = [y_c, w2[...], y0_c, y1[...], y1_c[...]]
+    sum_p[...] = own_p[...] + terms(x, blocks, sc, (u_p[...], columns))
     own = (u_q[...], [v_q[1:2], v_q[3:4]])
     sum_q[...] = own_q[...] + terms(y, [x_c, x2_c], sc, own)
 

time: 63.5 us -> 63.4 us (level)
  no operation moved by 1% of the time
where the time goes in v10:
time: 63.4 us; the launch traced here: 62.9 us
  starting transfers between devices  46.1 us (73%)
  Pallas kernels  12.7 us (20%)
  between operations  2.14 us (3%)
  waiting for transfers between devices  2.04 us (3%)
    ppermute x9, starting transfers between devices, go(): return lax.ppermute(x, AXES, pairs)  46.1 us
    pallas_call x1, Pallas kernels, local(): call(visit_body, (wide, wide, part, part), [SMEM] + [VMEM] * 15, input_ou...  2.44 us
    pallas_call x1, Pallas kernels, local(): call(own_body, (wide,) * 3, [VMEM] * 6)(sc, near, *match)  2.27 us
    pallas_call x1, Pallas kernels, local(): call(rest_body, (wide, wide), [VMEM, SMEM] + [VMEM] * 8, (HBM, HBM), scra...  2.09 us
    ppermute x9, waiting for transfers between devices, go(): return lax.ppermute(x, AXES, pairs)  2.04 us
    pallas_call x1, Pallas kernels, local(): call(unit_body, (one, one) + place, [SMEM] + [HBM] * 3, scratch_shapes=re...  1.46 us
    pallas_call x1, Pallas kernels, local(): call(last_body, (wide, wide), [SMEM] + [VMEM] * 4 + [HBM] * 2, (HBM, HBM)...  1.32 us
  transfers between devices with their start and end apart: 9, of which 2 were waited for; matrix products, arithmetic and copies ran while one was open for 0% of the time, Pallas kernels for 14%

profile of v10, /device:TPU:1, one launch (start us, length us, event | category | flops | bytes accessed | tf_op | source)
XLA Modules:
  0.0 62.9 jit_solution(3544114410007254694)
XLA Ops:
  0.6 1.5 %unit.1 = (bf16[224,1152]{1,0:T(8,128)(2,1)S(1)}, bf16[224,1152]{1,0:T(8,128)(2,1)S(1)}, s32[224,1]{1,0:T(8,128)S(1)}, s32[4,224]{1,0:T(4,128)S(1)}, s32[224,1]{1,0:T(8,128)S(1)}, /*index=5*/s32[4,224]{1,0:T(4,128)S(1)}) custom-call(s32[1]{0:T(128)} %bitcast.here, bf16[224,1152]{1,0:T(8,128)(2,1)} %img.5, bf16[224,1152]{1,0:T(8,128)(2,1)} %txt.5, ...), custom_call_target="tpu_custom_call" | custom-call | flops 16000000000 | bytes 1 | tf_op jit(solution)/shard_map/unit/pallas_call | solution.py:281
  2.1 5.0 %collective-permute-start = (bf16[224,1152]{1,0:T(8,128)(2,1)S(1)}, bf16[224,1152]{1,0:T(8,128)(2,1)S(1)}, u32[]{:S(2)}, u32[]{:S(2)}) collective-permute-start(bf16[224,1152]{1,0:T(8,128)(2,1)S(1)} %get-tuple-element.25.q), channel_id=1, source_target_pairs={{0,2},{1,3},{2,0},{3,1},{4,6},{5,7},{6,4},{7,5},{8,10},{9,11},{10,... | collective-permute-start | bytes 1548296 | tf_op jit(solution)/shard_map/chip_q/ppermute | solution.py:260
  7.1 13.8 %collective-permute-start.1 = (bf16[224,1152]{1,0:T(8,128)(2,1)S(1)}, bf16[224,1152]{1,0:T(8,128)(2,1)S(1)}, u32[]{:S(2)}, u32[]{:S(2)}) collective-permute-start(bf16[224,1152]{1,0:T(8,128)(2,1)S(1)} %get-tuple-element.24.p), channel_id=1, source_target_pairs={{0,510},{1,511},{2,4},{3,5},{4,2},{5,3},{6,8},{7,9},{8,6},{9,7},{1... | collective-permute-start | bytes 1548296 | tf_op jit(solution)/shard_map/group_p/ppermute | solution.py:260
  20.9 0.0 collective-permute-done.x2
  20.9 11.3 %collective-permute-start.3 = (bf16[224,1152]{1,0:T(8,128)(2,1)S(1)}, bf16[224,1152]{1,0:T(8,128)(2,1)S(1)}, u32[]{:S(2)}, u32[]{:S(2)}) collective-permute-start(bf16[224,1152]{1,0:T(8,128)(2,1)S(1)} %collective-permute-done.x2), channel_id=1, source_target_pairs={{0,510},{1,511},{2,4},{3,5},{4,2},{5,3},{6,8},{7,9},{8,6},{9,7},{1... | collective-permute-start | bytes 1548296 | tf_op jit(solution)/shard_map/group_x2/ppermute | solution.py:260
  32.2 1.9 %collective-permute-start.5 = (bf16[224,1152]{1,0:T(8,128)(2,1)S(1)}, bf16[224,1152]{1,0:T(8,128)(2,1)S(1)}, u32[]{:S(2)}, u32[]{:S(2)}) collective-permute-start(bf16[224,1152]{1,0:T(8,128)(2,1)S(1)} %get-tuple-element.24.p), channel_id=1, source_target_pairs={{0,2},{1,3},{2,0},{3,1},{4,6},{5,7},{6,4},{7,5},{8,10},{9,11},{10,... | collective-permute-start | bytes 1548296 | tf_op jit(solution)/shard_map/chip_p/ppermute | solution.py:260
  34.1 1.1 %match.1 = (s32[224,1]{1,0:T(8,128)S(1)}, s32[4,224]{1,0:T(4,128)S(1)}, s32[224,1]{1,0:T(8,128)S(1)}, s32[4,224]{1,0:T(4,128)S(1)}) custom-call(s32[1]{0:T(128)} %bitcast.here, s32[1,896]{1,0:T(1,128)} %pos_far.3, s32[224,1]{1,0:T(8,128)S(1)} %get-tuple-element.26.rest_0_, ...), custom_call_target="tpu_custom_call", output_to_operand_aliasing={{0}: (2, {}), {1}: (3, {}), {2}: (4, {}), {3}: (5, {})} | custom-call | flops 1 | bytes 1 | tf_op jit(solution)/shard_map/match/pallas_call | solution.py:293
  36.6 0.0 collective-permute-done.1.y0
  36.6 0.2 join.1.near
  36.7 3.8 %collective-permute-start.2 = (bf16[896,1152]{1,0:T(8,128)(2,1)S(1)}, bf16[896,1152]{1,0:T(8,128)(2,1)S(1)}, u32[]{:S(2)}, u32[]{:S(2)}) collective-permute-start(bf16[896,1152]{1,0:T(8,128)(2,1)S(1)} %join.1.near), channel_id=1, source_target_pairs={{0,1},{1,0},{2,3},{3,2},{4,5},{5,4},{6,7},{7,6},{8,9},{9,8},{10,11... | collective-permute-start | bytes 6193160 | tf_op jit(solution)/shard_map/core_xy/ppermute | solution.py:260
  40.5 2.3 %own.1 = (f32[224,1152]{1,0:T(8,128)S(1)}, f32[224,1152]{1,0:T(8,128)S(1)}, f32[224,1152]{1,0:T(8,128)S(1)}) custom-call(f32[2,128]{1,0:T(2,128)S(1)} %nums.1.sc, bf16[896,1152]{1,0:T(8,128)(2,1)S(1)} %join.1.near, s32[224,1]{1,0:T(8,128)S(1)} %get-tuple-element.30.u_p.rest_1_.rest_0_, s32[4,224]{1,0:T(4,128)S(1)} %get-tuple-element.31.v_p.rest_2_.rest_1_, ...), custom_call_target="tpu_custom_call" | custom-call | flops 1 | bytes 1 | tf_op jit(solution)/shard_map/own/pallas_call | solution.py:302
  42.8 0.0 collective-permute-done.3.y
  42.9 4.0 %collective-permute-start.4 = (bf16[224,1152]{1,0:T(8,128)(2,1)S(1)}, bf16[224,1152]{1,0:T(8,128)(2,1)S(1)}, u32[]{:S(2)}, u32[]{:S(2)}) collective-permute-start(bf16[224,1152]{1,0:T(8,128)(2,1)S(1)} %take.1.y1), channel_id=1, source_target_pairs={{0,1},{1,0},{2,3},{3,2},{4,5},{5,4},{6,7},{7,6},{8,9},{9,8},{10,11... | collective-permute-start | bytes 1548296 | tf_op jit(solution)/shard_map/core_y/ppermute | solution.py:260
  46.9 0.0 collective-permute-done.2.near_c
  46.9 0.9 %mid.1.part = f32[224,1152]{1,0:T(8,128)S(1)} custom-call(f32[2,128]{1,0:T(2,128)S(1)} %nums.1.sc, bf16[896,1152]{1,0:T(8,128)(2,1)S(1)} %join.1.near, bf16[896,1152]{1,0:T(8,128)(2,1)S(1)} %collective-permute-done.2.near_c, bf16[224,1152]{1,0:T(8,128)(2,1)S(1)} %take.1.y1, f32[224,1152]{1,0:T(8,128)S(1)} %get-tuple-element.35.part), custom_call_target="tpu_custom_call" | custom-call | flops 1 | bytes 1 | tf_op jit(solution)/shard_map/mid/pallas_call | solution.py:305
  47.8 0.0 collective-permute-done.5.rest_0_.w2
  47.8 0.5 collective-permute-done.4.y1_c
  48.4 0.8 %late.1 = (bf16[224,1152]{1,0:T(8,128)(2,1)S(1)}, f32[224,1152]{1,0:T(8,128)S(1)}, f32[224,1152]{1,0:T(8,128)S(1)}) custom-call(s32[1]{0:T(128)} %bitcast.here, f32[224,1152]{1,0:T(8,128)S(1)} %mid.1.part, f32[2,128]{1,0:T(2,128)S(1)} %nums.1.sc, bf16[896,1152]{1,0:T(8,128)(2,1)S(1)} %join.1.near, bf16[896,1152]{1,0:T(8,128)(2,1)S(1)} %collective-permute-done.2.near_c, ...), custom_call_target="tpu_custom_call" | custom-call | flops 1 | bytes 1 | tf_op jit(solution)/shard_map/late/pallas_call | solution.py:307
  49.2 1.9 %collective-permute-start.6 = (bf16[224,1152]{1,0:T(8,128)(2,1)S(1)}, bf16[224,1152]{1,0:T(8,128)(2,1)S(1)}, u32[]{:S(2)}, u32[]{:S(2)}) collective-permute-start(bf16[224,1152]{1,0:T(8,128)(2,1)S(1)} %get-tuple-element.37._send), channel_id=1, source_target_pairs={{0,2},{1,3},{2,0},{3,1},{4,6},{5,7},{6,4},{7,5},{8,10},{9,11},{10,... | collective-permute-start | bytes 1548296 | tf_op jit(solution)/shard_map/chip_send/ppermute | solution.py:260
  51.2 0.0 copy-start
  51.2 0.0 copy-start.1
  51.2 2.4 %visit.1 = (f32[224,1152]{1,0:T(8,128)S(1)}, f32[224,1152]{1,0:T(8,128)S(1)}, bf16[112,1152]{1,0:T(8,128)(2,1)S(1)}, bf16[112,1152]{1,0:T(8,128)(2,1)S(1)}) custom-call(s32[1]{0:T(128)} %bitcast.here, bf16[224,1152]{1,0:T(8,128)(2,1)S(1)} %get-tuple-element.37._send, ...), custom_call_target="tpu_custom_call", output_to_operand_aliasing={{0}: (2, {}), {1}: (3, {})} | custom-call | flops 1 | bytes 1 | tf_op jit(solution)/shard_map/visit/pallas_call | solution.py:311
  53.6 2.5 %collective-permute-start.7 = (bf16[112,1152]{1,0:T(8,128)(2,1)S(1)}, bf16[112,1152]{1,0:T(8,128)(2,1)S(1)}, u32[]{:S(2)}, u32[]{:S(2)}) collective-permute-start(bf16[112,1152]{1,0:T(8,128)(2,1)S(1)} %get-tuple-element.41), channel_id=1, source_target_pairs={{0,1},{1,0},{2,3},{3,2},{4,5},{5,4},{6,7},{7,6},{8,9},{9,8},{10,11... | collective-permute-start | bytes 774152 | tf_op jit(solution)/shard_map/core_w_lo/ppermute | solution.py:260
  56.1 1.9 %collective-permute-start.8 = (bf16[112,1152]{1,0:T(8,128)(2,1)S(1)}, bf16[112,1152]{1,0:T(8,128)(2,1)S(1)}, u32[]{:S(2)}, u32[]{:S(2)}) collective-permute-start(bf16[112,1152]{1,0:T(8,128)(2,1)S(1)} %get-tuple-element.42), channel_id=1, source_target_pairs={{0,1},{1,0},{2,3},{3,2},{4,5},{5,4},{6,7},{7,6},{8,9},{9,8},{10,11... | collective-permute-start | bytes 774152 | tf_op jit(solution)/shard_map/core_w_hi/ppermute | solution.py:260
  58.0 0.0 collective-permute-done.7.w2_lo_c
  58.0 1.5 %collective-permute-done.8.w2_hi_c = bf16[112,1152]{1,0:T(8,128)(2,1)S(1)} collective-permute-done((bf16[112,1152]{1,0:T(8,128)(2,1)S(1)}, bf16[112,1152]{1,0:T(8,128)(2,1)S(1)}, u32[]{:S(2)}, u32[]{:S(2)}) %collective-permute-start.8) | collective-permute-done | bytes 258080 | tf_op jit(solution)/shard_map/core_w_hi/ppermute | solution.py:260
  59.5 0.0 copy-done
  59.5 0.0 copy-done.1
  59.5 2.1 %rest.1 = (f32[224,1152]{1,0:T(8,128)}, f32[224,1152]{1,0:T(8,128)}) custom-call(f32[2,128]{1,0:T(2,128)S(1)} %nums.1.sc, s32[1]{0:T(128)} %bitcast.here, bf16[224,1152]{1,0:T(8,128)(2,1)S(1)} %copy-done, bf16[224,1152]{1,0:T(8,128)(2,1)S(1)} %copy-done.1, bf16[224,1152]{1,0:T(8,128)(2,1)S(1)} %get-tuple-element.24.p, ...), custom_call_target="tpu_custom_call" | custom-call | flops 1 | bytes 1 | tf_op jit(solution)/shard_map/rest/pallas_call | solution.py:318
  61.6 0.0 collective-permute-done.6.back
  61.6 1.3 %last.1 = (f32[224,1152]{1,0:T(8,128)}, f32[224,1152]{1,0:T(8,128)}) custom-call(s32[1]{0:T(128)} %bitcast.here, bf16[224,1152]{1,0:T(8,128)(2,1)S(1)} %copy-done, bf16[224,1152]{1,0:T(8,128)(2,1)S(1)} %copy-done.1, f32[224,1152]{1,0:T(8,128)S(1)} %get-tuple-element.40.sum_q, ...), custom_call_target="tpu_custom_call", output_to_operand_aliasing={{0}: (5, {}), {1}: (6, {})} | custom-call | flops 64000000000 | bytes 1 | tf_op jit(solution)/shard_map/last/pallas_call | solution.py:325
  (2 shorter events, 0.0 us)
Async XLA Ops:
  2.1 18.8 %collective-permute-start = (bf16[224,1152]{1,0:T(8,128)(2,1)S(1)}, bf16[224,1152]{1,0:T(8,128)(2,1)S(1)}, u32[]{:S(2)}, u32[]{:S(2)}) collective-permute-start(bf16[224,1152]{1,0:T(8,128)(2,1)S(1)} %get-tuple-element.25.q), channel_id=1, source_target_pairs={{0,2},{1,3},{2,0},{3,1},{4,6},{5,7},{6,4},{7,5},{8,10},{9,11},{10,... | collective-permute-start | bytes 1548296 | tf_op jit(solution)/shard_map/chip_q/ppermute | solution.py:260
  7.1 29.5 %collective-permute-start.1 = (bf16[224,1152]{1,0:T(8,128)(2,1)S(1)}, bf16[224,1152]{1,0:T(8,128)(2,1)S(1)}, u32[]{:S(2)}, u32[]{:S(2)}) collective-permute-start(bf16[224,1152]{1,0:T(8,128)(2,1)S(1)} %get-tuple-element.24.p), channel_id=1, source_target_pairs={{0,510},{1,511},{2,4},{3,5},{4,2},{5,3},{6,8},{7,9},{8,6},{9,7},{1... | collective-permute-start | bytes 1548296 | tf_op jit(solution)/shard_map/group_p/ppermute | solution.py:260
  20.9 21.9 %collective-permute-start.3 = (bf16[224,1152]{1,0:T(8,128)(2,1)S(1)}, bf16[224,1152]{1,0:T(8,128)(2,1)S(1)}, u32[]{:S(2)}, u32[]{:S(2)}) collective-permute-start(bf16[224,1152]{1,0:T(8,128)(2,1)S(1)} %collective-permute-done.x2), channel_id=1, source_target_pairs={{0,510},{1,511},{2,4},{3,5},{4,2},{5,3},{6,8},{7,9},{8,6},{9,7},{1... | collective-permute-start | bytes 1548296 | tf_op jit(solution)/shard_map/group_x2/ppermute | solution.py:260
  32.2 15.6 %collective-permute-start.5 = (bf16[224,1152]{1,0:T(8,128)(2,1)S(1)}, bf16[224,1152]{1,0:T(8,128)(2,1)S(1)}, u32[]{:S(2)}, u32[]{:S(2)}) collective-permute-start(bf16[224,1152]{1,0:T(8,128)(2,1)S(1)} %get-tuple-element.24.p), channel_id=1, source_target_pairs={{0,2},{1,3},{2,0},{3,1},{4,6},{5,7},{6,4},{7,5},{8,10},{9,11},{10,... | collective-permute-start | bytes 1548296 | tf_op jit(solution)/shard_map/chip_p/ppermute | solution.py:260
  36.7 10.1 %collective-permute-start.2 = (bf16[896,1152]{1,0:T(8,128)(2,1)S(1)}, bf16[896,1152]{1,0:T(8,128)(2,1)S(1)}, u32[]{:S(2)}, u32[]{:S(2)}) collective-permute-start(bf16[896,1152]{1,0:T(8,128)(2,1)S(1)} %join.1.near), channel_id=1, source_target_pairs={{0,1},{1,0},{2,3},{3,2},{4,5},{5,4},{6,7},{7,6},{8,9},{9,8},{10,11... | collective-permute-start | bytes 6193160 | tf_op jit(solution)/shard_map/core_xy/ppermute | solution.py:260
  42.9 5.5 %collective-permute-start.4 = (bf16[224,1152]{1,0:T(8,128)(2,1)S(1)}, bf16[224,1152]{1,0:T(8,128)(2,1)S(1)}, u32[]{:S(2)}, u32[]{:S(2)}) collective-permute-start(bf16[224,1152]{1,0:T(8,128)(2,1)S(1)} %take.1.y1), channel_id=1, source_target_pairs={{0,1},{1,0},{2,3},{3,2},{4,5},{5,4},{6,7},{7,6},{8,9},{9,8},{10,11... | collective-permute-start | bytes 1548296 | tf_op jit(solution)/shard_map/core_y/ppermute | solution.py:260
  49.2 12.4 %collective-permute-start.6 = (bf16[224,1152]{1,0:T(8,128)(2,1)S(1)}, bf16[224,1152]{1,0:T(8,128)(2,1)S(1)}, u32[]{:S(2)}, u32[]{:S(2)}) collective-permute-start(bf16[224,1152]{1,0:T(8,128)(2,1)S(1)} %get-tuple-element.37._send), channel_id=1, source_target_pairs={{0,2},{1,3},{2,0},{3,1},{4,6},{5,7},{6,4},{7,5},{8,10},{9,11},{10,... | collective-permute-start | bytes 1548296 | tf_op jit(solution)/shard_map/chip_send/ppermute | solution.py:260
  51.2 8.4 %copy-start = (bf16[224,1152]{1,0:T(8,128)(2,1)S(1)}, bf16[224,1152]{1,0:T(8,128)(2,1)}, u32[]{:S(2)}) copy-start(bf16[224,1152]{1,0:T(8,128)(2,1)} %img.5) | copy-start | bytes 1548292
  51.2 8.4 %copy-start.1 = (bf16[224,1152]{1,0:T(8,128)(2,1)S(1)}, bf16[224,1152]{1,0:T(8,128)(2,1)}, u32[]{:S(2)}) copy-start(bf16[224,1152]{1,0:T(8,128)(2,1)} %txt.5) | copy-start | bytes 1548292
  53.6 4.4 %collective-permute-start.7 = (bf16[112,1152]{1,0:T(8,128)(2,1)S(1)}, bf16[112,1152]{1,0:T(8,128)(2,1)S(1)}, u32[]{:S(2)}, u32[]{:S(2)}) collective-permute-start(bf16[112,1152]{1,0:T(8,128)(2,1)S(1)} %get-tuple-element.41), channel_id=1, source_target_pairs={{0,1},{1,0},{2,3},{3,2},{4,5},{5,4},{6,7},{7,6},{8,9},{9,8},{10,11... | collective-permute-start | bytes 774152 | tf_op jit(solution)/shard_map/core_w_lo/ppermute | solution.py:260
  56.1 3.4 %collective-permute-start.8 = (bf16[112,1152]{1,0:T(8,128)(2,1)S(1)}, bf16[112,1152]{1,0:T(8,128)(2,1)S(1)}, u32[]{:S(2)}, u32[]{:S(2)}) collective-permute-start(bf16[112,1152]{1,0:T(8,128)(2,1)S(1)} %get-tuple-element.42), channel_id=1, source_target_pairs={{0,1},{1,0},{2,3},{3,2},{4,5},{5,4},{6,7},{7,6},{8,9},{9,8},{10,11... | collective-permute-start | bytes 774152 | tf_op jit(solution)/shard_map/core_w_hi/ppermute | solution.py:260
